TPU v7x, 256 devices: a whole 4x4x8 slice. The times are simulated.
256 devices in a mesh: cuts: 8 (over x_hi, y), mode: 32 (over z, x_lo, core).
Axes of the slice: x: 4 (x_hi: 2, x_lo: 2; x = x_hi * 2 + x_lo), y: 4, z: 8, core: 2. Of those that a mesh axis runs over, the one named last changes fastest.
Arguments:
- stem_tensor: bfloat16 [2, 32, 32, 32, 32, 256], P(None, 'cuts', 'mode'), may hold values from -6 to 6
- branch_first: bfloat16 [2, 32, 256, 256], P(None, 'cuts'), may hold values from -0.25 to 0.25
- branch_second: bfloat16 [2, 32, 512, 512], P(None, 'cuts', 'mode'), may hold values from -0.25 to 0.25
Outputs:
- amplitudes: float32 [2, 512, 32, 512], P(None, 'cuts', 'mode')
All inputs are finite; a program needn't handle non-finite values.
Results may differ from a plain program's by a relative error of at most 0.0029.
Values may be sent and summed in bfloat16 or wider, within the bound.
No kernel may reach another device: no remote copies, remote signals or barrier semaphores. Data moves between devices by JAX's collectives and lax.ppermute only.
A program may use at most 64 MiB of HBM per device.

v0:
```python
import jax
import jax.numpy as jnp
from jax import lax
from jax.sharding import PartitionSpec as P


def first_step(block, branch):
    real_part = jnp.einsum(
        "sabc,sco->saob", block[0], branch[0], preferred_element_type=jnp.float32
    ) - jnp.einsum("sabc,sco->saob", block[1], branch[1], preferred_element_type=jnp.float32)
    imag_part = jnp.einsum(
        "sabc,sco->saob", block[0], branch[1], preferred_element_type=jnp.float32
    ) + jnp.einsum("sabc,sco->saob", block[1], branch[0], preferred_element_type=jnp.float32)
    shape_now = real_part.shape
    merged = (shape_now[0], shape_now[1], shape_now[2] * shape_now[3])
    return jnp.stack([real_part.reshape(merged), imag_part.reshape(merged)]).astype(jnp.bfloat16)


def second_step(regrouped, branch):
    real_part = jnp.einsum(
        "skj,skm->sjm", branch[0], regrouped[0], preferred_element_type=jnp.float32
    ) - jnp.einsum("skj,skm->sjm", branch[1], regrouped[1], preferred_element_type=jnp.float32)
    imag_part = jnp.einsum(
        "skj,skm->sjm", branch[1], regrouped[0], preferred_element_type=jnp.float32
    ) + jnp.einsum("skj,skm->sjm", branch[0], regrouped[1], preferred_element_type=jnp.float32)
    return jnp.stack([real_part, imag_part])


def shards(stem_tensor, branch_first, branch_second):
    slices = stem_tensor.shape[1]
    local_stem = stem_tensor[:, :, 0]
    split_count = local_stem.shape[2]
    kept_rows = local_stem.shape[3]
    joint_first = local_stem.shape[4]
    second_full = lax.all_gather(branch_second, "mode", axis=2, tiled=True)
    joint_second = second_full.shape[2]
    group_rows = joint_second // split_count
    open_cols = joint_first // group_rows * kept_rows
    arrived = lax.all_to_all(local_stem, "mode", split_axis=2, concat_axis=2, tiled=True)
    first = first_step(arrived, branch_first)
    second = second_step(first.reshape(2, slices, joint_second, open_cols), second_full)
    summed = jnp.sum(second, axis=1)
    owned = lax.psum_scatter(summed, "cuts", scatter_dimension=1, tiled=True)
    return owned.reshape(2, owned.shape[1], 1, open_cols)


def solution(mesh):
    in_specs = (
        P(None, "cuts", "mode", None, None, None),
        P(None, "cuts", None, None),
        P(None, "cuts", "mode", None),
    )
    out_specs = P(None, "cuts", "mode", None)
    return jax.shard_map(shards, mesh=mesh, in_specs=in_specs, out_specs=out_specs, check_vma=False)
```

profile of v0, /device:TPU:24, one launch (start us, length us, event | category | flops | bytes accessed | tf_op | source)
XLA Modules:
  0.0 300.3 jit_solution(1313793638724075309)
XLA Ops:
  6.5 4.8 %copy.50 = bf16[2,4,1,32,32,256]{5,4,1,0,3,2:T(8,128)(2,1)} copy(bf16[2,4,1,32,32,256]{5,4,3,2,1,0:T(8,128)(2,1)} %param.3) | data formatting | bytes 8388608 | tf_op args[0]
  11.3 9.9 %all-to-all-start = ((bf16[2,4,32,32,256]{4,3,1,0,2:T(8,128)(2,1)}), bf16[2,4,32,32,256]{4,3,1,0,2:T(8,128)(2,1)}, u32[]{:S(2)}, u32[]{:S(2)}) async-start(bf16[2,4,32,32,256]{4,3,1,0,2:T(8,128)(2,1)} %bitcast.62), calls=%async_computation | async-start | bytes 8388608 | tf_op jit(solution)/shard_map/all_to_all | solution.py:39
  21.3 0.0 all-gather.2.cloned.1.call-start
  21.3 0.7 all-gather.2.cloned.1.call-update
  22.0 0.0 copy-start.4
  22.0 0.0 all-reduce.3.cloned.1.call-start
  22.1 117.0 %all-to-all-done = bf16[2,4,32,32,256]{4,3,1,0,2:T(8,128)(2,1)} async-done(((bf16[2,4,32,32,256]{4,3,1,0,2:T(8,128)(2,1)}), bf16[2,4,32,32,256]{4,3,1,0,2:T(8,128)(2,1)}, u32[]{:S(2)}, u32[]{:S(2)}) %all-to-all-start) | async-done | bytes 4194336 | tf_op jit(solution)/shard_map/all_to_all | solution.py:39
  139.0 2.9 fusion.14
  141.9 0.0 copy-start.3
  141.9 0.0 copy-done.4
  141.9 0.7 fusion.1
  142.7 0.6 copy-done.3
  143.2 2.0 fusion.4
  145.3 7.7 %copy.23 = bf16[4,32,256,32]{3,2,1,0:T(8,128)(2,1)} copy(bf16[4,32,256,32]{2,3,1,0:T(8,128)(2,1)} %fusion.4) | data formatting | bytes 4194304 | tf_op jit(solution)/shard_map/sub | solution.py:8
  153.0 12.0 %squeeze.40 = bf16[4,512,512]{2,1,0:T(8,128)(2,1)} reshape(bf16[4,32,256,32]{3,2,1,0:T(8,128)(2,1)} %copy.23) | data formatting | bytes 4194304 | tf_op jit(solution)/shard_map/squeeze | solution.py:21
  165.0 2.3 fusion
  167.3 2.0 fusion.5
  169.3 7.7 %copy.25 = bf16[4,32,256,32]{3,2,1,0:T(8,128)(2,1)} copy(bf16[4,32,256,32]{2,3,1,0:T(8,128)(2,1)} %fusion.5) | data formatting | bytes 4194304 | tf_op jit(solution)/shard_map/add | solution.py:11
  177.1 0.0 copy-start
  177.1 12.1 %squeeze.42 = bf16[4,512,512]{2,1,0:T(8,128)(2,1)} reshape(bf16[4,32,256,32]{3,2,1,0:T(8,128)(2,1)} %copy.25) | data formatting | bytes 4194304 | tf_op jit(solution)/shard_map/squeeze | solution.py:22
  189.2 0.0 all-gather.2.cloned.1.call-done
  189.2 0.0 copy-done
  189.2 0.0 copy-start.2
  189.2 3.0 %fusion.2 = f32[4,512,512]{2,1,0:T(8,128)S(1)} fusion(bf16[4,512,512]{2,1,0:T(8,128)(2,1)S(1)} %copy-done, bf16[2,4,512,512]{3,2,1,0:T(8,128)(2,1)} %all-gather.2.cloned.1.call-done), kind=kOutput, calls=%fused_computation.12 | convolution fusion | flops 1073741824 | bytes 8388608 | tf_op jit(solution)/shard_map/skj,skm->sjm/dot_general | solution.py:20
  192.2 0.0 copy-done.2
  192.3 0.0 copy-start.1
  192.3 1.3 fusion.3
  193.6 0.3 copy-done.1
  193.8 1.4 subtract_bitcast_fusion
  195.2 1.3 add_bitcast_fusion
  196.6 1.1 maximum_reduce_fusion
  197.6 2.4 copy.29
  200.1 0.0 copy-start.5
  200.1 0.0 all-reduce.3.cloned.1.call-update
  200.1 0.6 copy-done.5
  200.8 0.6 dynamic-slice
  202.0 89.6 %all-reduce.3.cloned.1.call-done = f32[2,512,512]{2,0,1:T(2,128)} async-done(((f32[2,512,512]{2,0,1:T(2,128)}), f32[2,512,512]{2,0,1:T(2,128)}) %all-reduce.3.cloned.1.call-update) | async-done | bytes 2097168
  291.6 1.0 dynamic-slice_bitcast_fusion
  292.5 1.0 copy.30
Async XLA Ops:
  11.3 127.7 %all-to-all-start = ((bf16[2,4,32,32,256]{4,3,1,0,2:T(8,128)(2,1)}), bf16[2,4,32,32,256]{4,3,1,0,2:T(8,128)(2,1)}, u32[]{:S(2)}, u32[]{:S(2)}) async-start(bf16[2,4,32,32,256]{4,3,1,0,2:T(8,128)(2,1)} %bitcast.62), calls=%async_computation | async-start | bytes 8388608 | tf_op jit(solution)/shard_map/all_to_all | solution.py:39
  21.3 167.9 %all-gather.2.cloned.1.call-start = ((), (), s32[]{:S(2)}) async-start(), calls=%async_computation.1 | async-start | bytes 4325376 | tf_op jit(solution)/shard_map/all_gather | solution.py:35
  22.0 119.9 %copy-start.4 = (bf16[2,4,256,256]{3,2,1,0:T(8,128)(2,1)S(1)}, bf16[2,4,256,256]{3,2,1,0:T(8,128)(2,1)}, u32[]{:S(2)}) copy-start(bf16[2,4,256,256]{3,2,1,0:T(8,128)(2,1)} %param.4) | copy-start | bytes 3145732
  22.0 269.5 %all-reduce.3.cloned.1.call-start = ((), (), s32[]{:S(2)}) async-start(), calls=%async_computation.2 | async-start | bytes 4194304
  141.9 1.3 copy-start.3
  177.1 12.1 %copy-start = (bf16[4,512,512]{2,1,0:T(8,128)(2,1)S(1)}, bf16[4,512,512]{2,1,0:T(8,128)(2,1)}, u32[]{:S(2)}) copy-start(bf16[4,512,512]{2,1,0:T(8,128)(2,1)} %squeeze.40) | copy-start | bytes 6291460
  189.2 3.0 %copy-start.2 = (bf16[2,4,512,512]{3,2,1,0:T(8,128)(2,1)S(1)}, bf16[2,4,512,512]{3,2,1,0:T(8,128)(2,1)}, u32[]{:S(2)}) copy-start(bf16[2,4,512,512]{3,2,1,0:T(8,128)(2,1)} %all-gather.2.cloned.1.call-done) | copy-start | bytes 12582916
  192.3 1.6 copy-start.1
  200.1 0.7 copy-start.5
Sparse Core Ops, SparseCore 0:
  24.0 108.2 all-gather.1
  200.2 91.2 all-reduce.2
where the time goes:
time: 304 us; the launch traced here: 300 us
  waiting for transfers between devices  207 us (68%)
  local copies, waits for them, and re-layouts  53.8 us (18%)
  between operations  14.2 us (5%)
  matrix products  14.1 us (5%)
  starting transfers between devices  9.99 us (3%)
    all_to_all x1, waiting for transfers between devices, shards(): lax.all_to_all(local_stem, 'mode', split_axis=2, concat_axis=2, tiled=True)  117 us
    unnamed x3, waiting for transfers between devices  90.3 us
    squeeze x1, local copies, waits for them, and re-layouts, second_step(): regrouped[1]  12.1 us
    squeeze x1, local copies, waits for them, and re-layouts, second_step(): regrouped[0]  12 us
    all_to_all x1, starting transfers between devices, shards(): lax.all_to_all(local_stem, 'mode', split_axis=2, concat_axis=2, tiled=True)  9.91 us
    sub x1, local copies, waits for them, and re-layouts, first_step(): jnp.einsum('sabc,sco->saob', block[0], branch[0], preferred_element_type=...  7.74 us
    add x1, local copies, waits for them, and re-layouts, first_step(): jnp.einsum('sabc,sco->saob', block[0], branch[1], preferred_element_type=...  7.74 us
    unnamed x14, local copies, waits for them, and re-layouts  6.9 us
  transfers between devices with their start and end apart: 3, of which 2 were waited for; matrix products, arithmetic and copies ran while one was open for 17% of the time, Pallas kernels for 0%

commit v1 on v0

v1 whole, which is shorter than its diff:
```python
import jax
import jax.numpy as jnp
from jax import lax
from jax.experimental import pallas as pl
from jax.experimental.pallas import tpu as pltpu
from jax.sharding import Mesh
from jax.sharding import PartitionSpec as P

PLANE = ("xh", "y", "xl", "core")
OWNERS = ("z", "xh", "y")
NT = (((1,), (1,)), ((), ()))
TN = (((0,), (0,)), ((), ()))


def first_kernel(stem_ref, branch_ref, out_ref):
    row = lax.broadcasted_iota(jnp.int32, (256, 256), 0)
    col = lax.broadcasted_iota(jnp.int32, (256, 256), 1)
    regroup = (col == (row % 16) * 16 + row // 16).astype(jnp.bfloat16)
    br = [
        lax.dot_general(regroup, branch_ref[r, 0], NT, preferred_element_type=jnp.float32).astype(jnp.bfloat16)
        for r in range(2)
    ]
    lhs = jnp.concatenate(
        [jnp.concatenate([br[0], -br[1]], axis=1), jnp.concatenate([br[1], br[0]], axis=1)], axis=0
    )
    for w in range(4):
        rhs = jnp.concatenate([stem_ref[r, 0, :, w].reshape(256, 256) for r in range(2)], axis=1)
        res = lax.dot_general(lhs, rhs, NT, preferred_element_type=jnp.float32).astype(jnp.bfloat16)
        for r in range(2):
            out_ref[:, w, r, 0] = res[r * 256 : (r + 1) * 256].reshape(8, 2, 16, 256)


def first_step(stem, branch):
    slices = stem.shape[1]
    return pl.pallas_call(
        first_kernel,
        grid=(slices,),
        in_specs=[
            pl.BlockSpec((2, 1, 8, 4, 32, 256), lambda s: (0, s, 0, 0, 0, 0)),
            pl.BlockSpec((2, 1, 256, 256), lambda s: (0, s, 0, 0)),
        ],
        out_specs=pl.BlockSpec((8, 4, 2, 1, 2, 16, 256), lambda s: (0, 0, 0, s, 0, 0, 0)),
        out_shape=jax.ShapeDtypeStruct((8, 4, 2, slices, 2, 16, 256), jnp.bfloat16),
        compiler_params=pltpu.CompilerParams(vmem_limit_bytes=32 << 20),
        cost_estimate=pl.CostEstimate(flops=2400000000, bytes_accessed=9 << 20, transcendentals=0),
        name="first_step",
    )(stem, branch)


def second_kernel(x_ref, b_ref, out_ref):
    br = [b_ref[:, r].reshape(2048, 128) for r in range(2)]
    lhs = [jnp.concatenate([br[0], -br[1]], axis=0), jnp.concatenate([br[1], br[0]], axis=0)]
    parts = []
    rhs = []
    for lh in range(2):
        rhs.append(jnp.concatenate([x_ref[:, r, :, lh].reshape(2048, 256) for r in range(2)], axis=0))
    for r in range(2):
        for lh in range(2):
            parts.append(lax.dot_general(lhs[r], rhs[lh], TN, preferred_element_type=jnp.float32))
    for za in range(8):
        joined = jnp.concatenate([part[:, za * 32 : (za + 1) * 32] for part in parts], axis=1)
        out_ref[za] = joined.astype(jnp.bfloat16).reshape(2, 64, 128)


def second_step(x, b2):
    return pl.pallas_call(
        second_kernel,
        grid=(4,),
        in_specs=[
            pl.BlockSpec((32, 2, 4, 2, 16, 256), lambda t: (0, 0, 0, 0, 0, 0)),
            pl.BlockSpec((32, 2, 4, 16, 128), lambda t: (0, 0, 0, 0, t)),
        ],
        out_specs=pl.BlockSpec((8, 2, 64, 128), lambda t: (0, t, 0, 0)),
        out_shape=jax.ShapeDtypeStruct((8, 8, 64, 128), jnp.bfloat16),
        compiler_params=pltpu.CompilerParams(vmem_limit_bytes=48 << 20),
        cost_estimate=pl.CostEstimate(flops=4300000000, bytes_accessed=9 << 20, transcendentals=0),
        name="second_step",
    )(x, b2)


def total_kernel(in_ref, out_ref):
    sums = []
    for i in range(8):
        acc = in_ref[0, i].astype(jnp.float32)
        for z in range(1, 8):
            acc = acc + in_ref[z, i].astype(jnp.float32)
        sums.append(acc)
    for r in range(2):
        out_ref[r] = jnp.concatenate([acc[:, r * 64 : (r + 1) * 64] for acc in sums], axis=1)


def total_step(arrived):
    return pl.pallas_call(
        total_kernel,
        out_shape=jax.ShapeDtypeStruct((2, 64, 512), jnp.float32),
        compiler_params=pltpu.CompilerParams(vmem_limit_bytes=16 << 20),
        cost_estimate=pl.CostEstimate(flops=1000000, bytes_accessed=2 << 20, transcendentals=0),
        name="total_step",
    )(arrived)


def shards(stem_tensor, branch_first, branch_second):
    slices = stem_tensor.shape[1]
    stem = stem_tensor.reshape(2, slices, 8, 4, 32, 256)
    b2 = lax.all_gather(branch_second.reshape(2 * slices * 16, 512), PLANE, axis=0, tiled=False)
    b2 = b2.reshape(32, 2, slices, 16, 512)
    sent = first_step(stem, branch_first).reshape(32, 2 * slices * 2 * 16, 256)
    arrived = lax.all_to_all(sent, PLANE, split_axis=0, concat_axis=0, tiled=True)
    partial = second_step(arrived.reshape(32, 2, slices, 2, 16, 256), b2)
    owned = lax.all_to_all(partial.reshape(64, 64, 128), OWNERS, split_axis=0, concat_axis=0, tiled=True)
    out = total_step(owned.reshape(8, 8, 64, 128))
    return out.reshape(2, 64, 1, 512)


def solution(mesh):
    fine = Mesh(mesh.devices.reshape(2, 4, 8, 2, 2), ("xh", "y", "z", "xl", "core"))
    cuts, mode = ("xh", "y"), ("z", "xl", "core")
    in_specs = (
        P(None, cuts, mode, None, None, None),
        P(None, cuts, None, None),
        P(None, cuts, mode, None),
    )
    return jax.shard_map(
        shards, mesh=fine, in_specs=in_specs, out_specs=P(None, cuts, mode, None), check_vma=False
    )
```

time: 304 us -> 168 us (0.55); the launches traced: 300 us -> 168 us
  waiting for transfers between devices: 207 us -> 27.8 us
  blocking collectives: 0 us -> 108 us
  local copies, waits for them, and re-layouts: 53.8 us -> 6.57 us
  matrix products: 14.1 us -> 0 us
  Pallas kernels: 0 us -> 11.4 us
  starting transfers between devices: 9.99 us -> 0.01 us
    all_to_all x1 -> x0, waiting for transfers between devices: 117 us -> none  [shards(): lax.all_to_all(local_stem, 'mode', split_axis=2, concat_axis=2, tiled=True)]
    all_to_all x0 -> x2, blocking collectives: none -> 108 us  [the longest x1 66.1 us: shards(): lax.all_to_all(sent, PLANE, split_axis=0, concat_axis=0, tiled=True)]
    unnamed x3 -> x1, waiting for transfers between devices: 90.3 us -> 0.71 us
    all_gather x1, waiting for transfers between devices: 0.01 us -> 27.1 us  [shards(): lax.all_gather(branch_second.reshape(2 * slices * 16, 512), PLANE, axis=0...]
    squeeze x2 -> x0, local copies, waits for them, and re-layouts: 24.1 us -> none  [the longest x1 12.1 us: second_step(): regrouped[1]]
    dot_general x8 -> x0, matrix products: 14.1 us -> none  [the longest x1 3.03 us: second_step(): jnp.einsum('skj,skm->sjm', branch[0], regrouped[0], preferred_element_typ...]
    pallas_call x0 -> x3, Pallas kernels: none -> 11.4 us  [the longest x1 7.04 us: second_step(): pl.pallas_call(second_kernel, grid=(4,), in_specs=[pl.BlockSpec((32, 2, 4...]
    all_to_all x1 -> x0, starting transfers between devices: 9.91 us -> none  [shards(): lax.all_to_all(local_stem, 'mode', split_axis=2, concat_axis=2, tiled=True)]
  transfers between devices with their start and end apart: 3 -> 1, of which waited for: 2 -> 1; matrix products, arithmetic and copies ran while one was open for 17% -> 0% of each run, Pallas kernels for 0% -> 2%
where the time goes in v1:
time: 168 us
  blocking collectives  108 us (64%)
  waiting for transfers between devices  27.8 us (17%)
  between operations  13.4 us (8%)
  Pallas kernels  11.4 us (7%)
  local copies, waits for them, and re-layouts  6.57 us (4%)
    all_to_all x1, blocking collectives, shards(): lax.all_to_all(sent, PLANE, split_axis=0, concat_axis=0, tiled=True)  66.1 us
    all_to_all x1, blocking collectives, shards(): lax.all_to_all(partial.reshape(64, 64, 128), OWNERS, split_axis=0, concat...  42.3 us
    all_gather x1, waiting for transfers between devices, shards(): lax.all_gather(branch_second.reshape(2 * slices * 16, 512), PLANE, axis=0...  27.1 us
    pallas_call x1, Pallas kernels, second_step(): pl.pallas_call(second_kernel, grid=(4,), in_specs=[pl.BlockSpec((32, 2, 4...  7.04 us
    unnamed x6, local copies, waits for them, and re-layouts  5.59 us
    pallas_call x1, Pallas kernels, first_step(): pl.pallas_call(first_kernel, grid=(slices,), in_specs=[pl.BlockSpec((2, 1...  4.13 us
  transfers between devices with their start and end apart: 1, of which 1 were waited for; matrix products, arithmetic and copies ran while one was open for 0% of the time, Pallas kernels for 2%

profile of v1, /device:TPU:24, one launch (start us, length us, event | category | flops | bytes accessed | tf_op | source)
XLA Modules:
  0.0 167.6 jit_solution(13642718735281879625)
XLA Ops:
  6.5 0.0 all-gather.2.cloned.1.call-start
  6.5 0.7 all-gather.2.cloned.1.call-update
  7.3 0.0 copy-start
  7.3 2.2 %copy-done = bf16[2,4,1,32,32,256]{5,4,3,2,1,0:T(8,128)(2,1)S(1)} copy-done((bf16[2,4,1,32,32,256]{5,4,3,2,1,0:T(8,128)(2,1)S(1)}, bf16[2,4,1,32,32,256]{5,4,3,2,1,0:T(8,128)(2,1)}, u32[]{:S(2)}) %copy-start) | copy-done | bytes 4194328
  9.4 0.0 copy-start.2
  9.4 1.2 copy-done.2
  10.7 4.1 %first_step.1 = bf16[8,4,2,4,2,16,256]{6,5,4,3,2,1,0:T(8,128)(2,1)S(1)} custom-call(bf16[2,4,8,4,32,256]{5,4,3,2,1,0:T(8,128)(2,1)S(1)} %bitcast.10, bf16[2,4,256,256]{3,2,1,0:T(8,128)(2,1)S(1)} %copy-done.2), custom_call_target="tpu_custom_call" | custom-call | flops 2400000000 | bytes 9437184 | tf_op jit(solution)/shard_map/first_step/pallas_call | solution.py:35
  14.8 66.1 %all_to_all.10 = bf16[32,256,256]{2,1,0:T(8,128)(2,1)} all-to-all(bf16[32,256,256]{2,1,0:T(8,128)(2,1)S(1)} %bitcast.8), channel_id=1, replica_groups=mesh['xh'=2,'y'=4,'z'=8,'xl'=2,'core'=2] {'xh','y','xl','core'}, dimensions={0} | all-to-all | bytes 8388608 | tf_op jit(solution)/shard_map/all_to_all | solution.py:108
  80.9 27.1 %all-gather.2.cloned.1.call-done = bf16[32,128,512]{2,1,0:T(8,128)(2,1)} async-done(((bf16[1,128,512]{2,1,0:T(8,128)(2,1)}), bf16[32,128,512]{2,1,0:T(8,128)(2,1)}) %all-gather.2.cloned.1.call-update) | async-done | bytes 4194320 | tf_op jit(solution)/shard_map/all_gather | solution.py:105
  108.0 0.0 copy-start.1
  108.0 2.2 %copy-done.1 = bf16[32,256,256]{2,1,0:T(8,128)(2,1)S(1)} copy-done((bf16[32,256,256]{2,1,0:T(8,128)(2,1)S(1)}, bf16[32,256,256]{2,1,0:T(8,128)(2,1)}, u32[]{:S(2)}) %copy-start.1) | copy-done | bytes 4194328
  110.2 7.0 %second_step.1 = bf16[8,8,64,128]{3,2,1,0:T(8,128)(2,1)S(1)} custom-call(bf16[32,2,4,2,16,256]{5,4,3,2,1,0:T(8,128)(2,1)S(1)} %bitcast.11, bf16[32,2,4,16,512]{4,3,2,1,0:T(8,128)(2,1)} %bitcast.15), custom_call_target="tpu_custom_call" | custom-call | flops 4300000256 | bytes 9437184 | tf_op jit(solution)/shard_map/second_step/pallas_call | solution.py:66
  117.3 42.3 %all_to_all.11 = bf16[64,64,128]{2,1,0:T(8,128)(2,1)S(1)} all-to-all(bf16[64,64,128]{2,1,0:T(8,128)(2,1)S(1)} %bitcast.13), channel_id=1, replica_groups=mesh['xh'=2,'y'=4,'z'=8,'xl'=2,'core'=2] {'z','xh','y'}, dimensions={0} | all-to-all | bytes 2097152 | tf_op jit(solution)/shard_map/all_to_all | solution.py:110
  159.6 0.2 total_step.1
  159.8 1.0 copy.5
Async XLA Ops:
  6.5 101.5 %all-gather.2.cloned.1.call-start = ((), (), s32[]{:S(2)}) async-start(), calls=%async_computation.2 | async-start | bytes 4325376 | tf_op jit(solution)/shard_map/all_gather | solution.py:105
  7.3 2.2 %copy-start = (bf16[2,4,1,32,32,256]{5,4,3,2,1,0:T(8,128)(2,1)S(1)}, bf16[2,4,1,32,32,256]{5,4,3,2,1,0:T(8,128)(2,1)}, u32[]{:S(2)}) copy-start(bf16[2,4,1,32,32,256]{5,4,3,2,1,0:T(8,128)(2,1)} %param.3) | copy-start | bytes 12582916
  9.4 1.2 copy-start.2
  108.0 2.2 %copy-start.1 = (bf16[32,256,256]{2,1,0:T(8,128)(2,1)S(1)}, bf16[32,256,256]{2,1,0:T(8,128)(2,1)}, u32[]{:S(2)}) copy-start(bf16[32,256,256]{2,1,0:T(8,128)(2,1)} %all_to_all.10) | copy-start | bytes 12582916
Sparse Core Ops, SparseCore 0:
  9.2 98.7 all-gather.1

commit v2 on v1

--- a/solution.py
+++ b/solution.py
@@ -7,9 +7,11 @@
 from jax.sharding import PartitionSpec as P
 
 PLANE = ("xh", "y", "xl", "core")
-OWNERS = ("z", "xh", "y")
+ROWS = ("xh", "xl")
+OWNERS = ("xh", "y", "z")
 NT = (((1,), (1,)), ((), ()))
-TN = (((0,), (0,)), ((), ()))
+NN = (((1,), (0,)), ((), ()))
+RING = 4
 
 
 def first_kernel(stem_ref, branch_ref, out_ref):
@@ -41,49 +43,84 @@
         ],
         out_specs=pl.BlockSpec((8, 4, 2, 1, 2, 16, 256), lambda s: (0, 0, 0, s, 0, 0, 0)),
         out_shape=jax.ShapeDtypeStruct((8, 4, 2, slices, 2, 16, 256), jnp.bfloat16),
-        compiler_params=pltpu.CompilerParams(vmem_limit_bytes=32 << 20),
+        compiler_params=pltpu.CompilerParams(vmem_limit_bytes=60 << 20),
         cost_estimate=pl.CostEstimate(flops=2400000000, bytes_accessed=9 << 20, transcendentals=0),
         name="first_step",
     )(stem, branch)
 
 
-def second_kernel(x_ref, b_ref, out_ref):
-    br = [b_ref[:, r].reshape(2048, 128) for r in range(2)]
-    lhs = [jnp.concatenate([br[0], -br[1]], axis=0), jnp.concatenate([br[1], br[0]], axis=0)]
-    parts = []
+def turn_kernel(own_a, own_b, other_a, other_b, out_ref):
+    for dx in range(RING):
+        for dy in range(RING):
+            at = (dx * RING + dy) * 128
+            for r in range(2):
+                a = jnp.concatenate([own_a[dx, dy, r], other_a[dx, dy, r]], axis=0)
+                b = jnp.concatenate([own_b[dy, dx, r], other_b[dy, dx, r]], axis=0)
+                out_ref[r, 0:256, at : at + 128] = a.T
+                out_ref[r, 256:512, at : at + 128] = b.T
+
+
+def turn_step(own_a, own_b, other_a, other_b):
+    return pl.pallas_call(
+        turn_kernel,
+        out_shape=jax.ShapeDtypeStruct((2, 512, 2048), jnp.bfloat16),
+        compiler_params=pltpu.CompilerParams(vmem_limit_bytes=32 << 20),
+        cost_estimate=pl.CostEstimate(flops=4000000000, bytes_accessed=8 << 20, transcendentals=0),
+        name="turn_step",
+    )(own_a, own_b, other_a, other_b)
+
+
+def second_kernel(me_ref, x_ref, b_ref, out_ref):
+    lhs = [
+        jnp.concatenate([b_ref[0], -b_ref[1]], axis=1),
+        jnp.concatenate([b_ref[1], b_ref[0]], axis=1),
+    ]
     rhs = []
     for lh in range(2):
-        rhs.append(jnp.concatenate([x_ref[:, r, :, lh].reshape(2048, 256) for r in range(2)], axis=0))
+        pieces = []
+        for r in range(2):
+            for dx in range(RING):
+                x = (me_ref[0] + dx) % RING
+                for dy in range(RING):
+                    y = (me_ref[1] + dy) % RING
+                    for dc in range(2):
+                        c = (me_ref[2] + dc) % 2
+                        pieces.append(x_ref[x // 2, y, x % 2, c, r, :, lh].reshape(64, 256))
+        rhs.append(jnp.concatenate(pieces, axis=0))
+    parts = []
     for r in range(2):
         for lh in range(2):
-            parts.append(lax.dot_general(lhs[r], rhs[lh], TN, preferred_element_type=jnp.float32))
+            parts.append(lax.dot_general(lhs[r], rhs[lh], NN, preferred_element_type=jnp.float32))
     for za in range(8):
         joined = jnp.concatenate([part[:, za * 32 : (za + 1) * 32] for part in parts], axis=1)
-        out_ref[za] = joined.astype(jnp.bfloat16).reshape(2, 64, 128)
+        out_ref[:, za] = joined.astype(jnp.bfloat16).reshape(2, 64, 128)
 
 
-def second_step(x, b2):
+def second_step(me, x, b2):
     return pl.pallas_call(
         second_kernel,
-        grid=(4,),
-        in_specs=[
-            pl.BlockSpec((32, 2, 4, 2, 16, 256), lambda t: (0, 0, 0, 0, 0, 0)),
-            pl.BlockSpec((32, 2, 4, 16, 128), lambda t: (0, 0, 0, 0, t)),
-        ],
-        out_specs=pl.BlockSpec((8, 2, 64, 128), lambda t: (0, t, 0, 0)),
+        grid_spec=pltpu.PrefetchScalarGridSpec(
+            num_scalar_prefetch=1,
+            grid=(4,),
+            in_specs=[
+                pl.BlockSpec((2, 4, 2, 2, 2, 4, 2, 16, 256), lambda t, me: (0,) * 9),
+                pl.BlockSpec((2, 128, 2048), lambda t, me: (0, t, 0)),
+            ],
+            out_specs=pl.BlockSpec((2, 8, 64, 128), lambda t, me: (t, 0, 0, 0)),
+        ),
         out_shape=jax.ShapeDtypeStruct((8, 8, 64, 128), jnp.bfloat16),
-        compiler_params=pltpu.CompilerParams(vmem_limit_bytes=48 << 20),
+        compiler_params=pltpu.CompilerParams(vmem_limit_bytes=60 << 20),
         cost_estimate=pl.CostEstimate(flops=4300000000, bytes_accessed=9 << 20, transcendentals=0),
         name="second_step",
-    )(x, b2)
+    )(me, x, b2)
 
 
 def total_kernel(in_ref, out_ref):
     sums = []
     for i in range(8):
-        acc = in_ref[0, i].astype(jnp.float32)
+        acc = in_ref[i, 0].astype(jnp.float32)
         for z in range(1, 8):
-            acc = acc + in_ref[z, i].astype(jnp.float32)
+            acc = acc + in_ref[i, z].astype(jnp.float32)
         sums.append(acc)
     for r in range(2):
         out_ref[r] = jnp.concatenate([acc[:, r * 64 : (r + 1) * 64] for acc in sums], axis=1)
@@ -99,14 +136,27 @@
     )(arrived)
 
 
+def ring_gather(block, axis):
+    blocks = [block]
+    for d in range(1, RING):
+        blocks.append(lax.ppermute(block, axis, [(i, (i - d) % RING) for i in range(RING)]))
+    return jnp.concatenate(blocks, axis=0)
+
+
 def shards(stem_tensor, branch_first, branch_second):
     slices = stem_tensor.shape[1]
     stem = stem_tensor.reshape(2, slices, 8, 4, 32, 256)
-    b2 = lax.all_gather(branch_second.reshape(2 * slices * 16, 512), PLANE, axis=0, tiled=False)
-    b2 = b2.reshape(32, 2, slices, 16, 512)
+    b2 = branch_second.reshape(1, 2, slices * 16, 512)
+    half_a, half_b = ring_gather(b2[..., :256], "y"), ring_gather(b2[..., 256:], ROWS)
     sent = first_step(stem, branch_first).reshape(32, 2 * slices * 2 * 16, 256)
     arrived = lax.all_to_all(sent, PLANE, split_axis=0, concat_axis=0, tiled=True)
-    partial = second_step(arrived.reshape(32, 2, slices, 2, 16, 256), b2)
+    half_a, half_b = ring_gather(half_a, ROWS), ring_gather(half_b, "y")
+    swap = [(0, 1), (1, 0)]
+    other_a, other_b = lax.ppermute(half_a, "core", swap), lax.ppermute(half_b, "core", swap)
+    grid = (RING, RING, 2, slices * 16, 256)
+    turned = turn_step(*(half.reshape(grid) for half in (half_a, half_b, other_a, other_b)))
+    me = jnp.stack([lax.axis_index(ROWS), lax.axis_index("y"), lax.axis_index("core")]).astype(jnp.int32)
+    partial = second_step(me, arrived.reshape(2, 4, 2, 2, 2, slices, 2, 16, 256), turned)
     owned = lax.all_to_all(partial.reshape(64, 64, 128), OWNERS, split_axis=0, concat_axis=0, tiled=True)
     out = total_step(owned.reshape(8, 8, 64, 128))
     return out.reshape(2, 64, 1, 512)

time: 168 us -> 152 us (0.905)
  blocking collectives: 108 us -> 45.6 us
  waiting for transfers between devices: 27.8 us -> 55.8 us
  starting transfers between devices: 0.01 us -> 26.7 us
  between operations: 13.4 us -> 0.17 us
  Pallas kernels: 11.4 us -> 19.1 us
  local copies, waits for them, and re-layouts: 6.57 us -> 3.1 us
    all_to_all x1 -> x0, blocking collectives: 66.1 us -> none  [shards(): lax.all_to_all(sent, PLANE, split_axis=0, concat_axis=0, tiled=True)]
    ppermute x0 -> x14, waiting for transfers between devices: none -> 55.8 us  [the longest x12 53.7 us: ring_gather(): lax.ppermute(block, axis, [(i, (i - d) % RING) for i in range(RING)])]
    all_gather x1 -> x0, waiting for transfers between devices: 27.1 us -> none  [shards(): lax.all_gather(branch_second.reshape(2 * slices * 16, 512), PLANE, axis=0...]
    ppermute x0 -> x14, starting transfers between devices: none -> 19.2 us  [the longest x12 18.8 us: ring_gather(): lax.ppermute(block, axis, [(i, (i - d) % RING) for i in range(RING)])]
    all_to_all x0 -> x1, starting transfers between devices: none -> 7.5 us  [shards(): lax.all_to_all(sent, PLANE, split_axis=0, concat_axis=0, tiled=True)]
    pallas_call x1 -> x2, Pallas kernels: 7.04 us -> 12.2 us  [the longest x1 9.66 us: second_step(): pl.pallas_call(second_kernel, grid_spec=pltpu.PrefetchScalarGridSpec(num_...]
    unnamed x6 -> x14, local copies, waits for them, and re-layouts: 5.59 us -> 2.07 us
    all_to_all x1, blocking collectives: 42.3 us -> 45.6 us  [shards(): lax.all_to_all(partial.reshape(64, 64, 128), OWNERS, split_axis=0, concat...]
  transfers between devices with their start and end apart: 1 -> 15, of which waited for: 1 -> 8; matrix products, arithmetic and copies ran while one was open for 0% -> 1% of each run, Pallas kernels for 2% -> 2%
where the time goes in v2:
time: 152 us; the launch traced here: 151 us
  waiting for transfers between devices  55.8 us (37%)
  blocking collectives  45.6 us (30%)
  starting transfers between devices  26.7 us (18%)
  Pallas kernels  19.1 us (13%)
  local copies, waits for them, and re-layouts  3.1 us (2%)
    ppermute x12, waiting for transfers between devices, ring_gather(): lax.ppermute(block, axis, [(i, (i - d) % RING) for i in range(RING)])  53.7 us
    all_to_all x1, blocking collectives, shards(): lax.all_to_all(partial.reshape(64, 64, 128), OWNERS, split_axis=0, concat...  45.6 us
    ppermute x12, starting transfers between devices, ring_gather(): lax.ppermute(block, axis, [(i, (i - d) % RING) for i in range(RING)])  18.8 us
    pallas_call x1, Pallas kernels, second_step(): pl.pallas_call(second_kernel, grid_spec=pltpu.PrefetchScalarGridSpec(num_...  9.66 us
    all_to_all x1, starting transfers between devices, shards(): lax.all_to_all(sent, PLANE, split_axis=0, concat_axis=0, tiled=True)  7.5 us
    pallas_call x1, Pallas kernels, first_step(): pl.pallas_call(first_kernel, grid=(slices,), in_specs=[pl.BlockSpec((2, 1...  6.72 us
  transfers between devices with their start and end apart: 15, of which 8 were waited for; matrix products, arithmetic and copies ran while one was open for 1% of the time, Pallas kernels for 2%

profile of v2, /device:TPU:24, one launch (start us, length us, event | category | flops | bytes accessed | tf_op | source)
XLA Modules:
  0.0 151.2 jit_solution(10999490551680340819)
XLA Ops:
  0.0 6.7 %first_step.1 = bf16[8,4,2,4,2,16,256]{6,5,4,3,2,1,0:T(8,128)(2,1)} custom-call(bf16[2,4,8,4,32,256]{5,4,3,2,1,0:T(8,128)(2,1)} %bitcast.20, bf16[2,4,256,256]{3,2,1,0:T(8,128)(2,1)} %branch_ref.1), custom_call_target="tpu_custom_call" | custom-call | flops 2400000000 | bytes 9437184 | tf_op jit(solution)/shard_map/first_step/pallas_call | solution.py:37
  6.7 0.0 copy-start.1
  6.7 7.5 %all-to-all-start = ((bf16[32,256,256]{2,1,0:T(8,128)(2,1)}), bf16[32,256,256]{2,1,0:T(8,128)(2,1)}, u32[]{:S(2)}, u32[]{:S(2)}) async-start(bf16[32,256,256]{2,1,0:T(8,128)(2,1)} %bitcast.19), calls=%async_computation | async-start | bytes 8388608 | tf_op jit(solution)/shard_map/all_to_all | solution.py:152
  14.2 0.0 copy-done.1
  14.3 0.9 collective-permute-start
  15.2 0.9 collective-permute-start.1
  16.1 2.3 %collective-permute-start.2 = (bf16[1,2,64,256]{3,2,1,0:T(8,128)(2,1)S(1)}, bf16[1,2,64,256]{3,2,1,0:T(8,128)(2,1)S(1)}, u32[]{:S(2)}, u32[]{:S(2)}) collective-permute-start(bf16[1,2,64,256]{3,2,1,0:T(8,128)(2,1)S(1)} %get-tuple-element.8), channel_id=1, source_target_pairs={{0,32},{32,64},{64,96},{96,0},{1,33},{33,65},{65,97},{97,1},{2,34}... | collective-permute-start | bytes 196616 | tf_op jit(solution)/shard_map/ppermute | solution.py:142
  18.4 2.7 %collective-permute-start.6 = (bf16[1,2,64,256]{3,2,1,0:T(8,128)(2,1)S(1)}, bf16[1,2,64,256]{3,2,1,0:T(8,128)(2,1)S(1)}, u32[]{:S(2)}, u32[]{:S(2)}) collective-permute-start(bf16[1,2,64,256]{3,2,1,0:T(8,128)(2,1)S(1)} %get-tuple-element.5), channel_id=1, source_target_pairs={{0,130},{2,0},{128,2},{130,128},{1,131},{3,1},{129,3},{131,129},{4... | collective-permute-start | bytes 196616 | tf_op jit(solution)/shard_map/ppermute | solution.py:142
  21.1 0.8 collective-permute-start.7
  22.0 39.7 %collective-permute-done = bf16[1,2,64,256]{3,2,1,0:T(8,128)(2,1)S(1)} collective-permute-done((bf16[1,2,64,256]{3,2,1,0:T(8,128)(2,1)S(1)}, bf16[1,2,64,256]{3,2,1,0:T(8,128)(2,1)S(1)}, u32[]{:S(2)}, u32[]{:S(2)}) %collective-permute-start) | collective-permute-done | bytes 65568 | tf_op jit(solution)/shard_map/ppermute | solution.py:142
  61.6 0.6 collective-permute-start.8
  62.2 7.8 %collective-permute-done.1 = bf16[1,2,64,256]{3,2,1,0:T(8,128)(2,1)S(1)} collective-permute-done((bf16[1,2,64,256]{3,2,1,0:T(8,128)(2,1)S(1)}, bf16[1,2,64,256]{3,2,1,0:T(8,128)(2,1)S(1)}, u32[]{:S(2)}, u32[]{:S(2)}) %collective-permute-start.1) | collective-permute-done | bytes 65568 | tf_op jit(solution)/shard_map/ppermute | solution.py:142
  70.1 0.0 collective-permute-done.2
  70.1 0.2 collective-permute-start.3
  70.3 1.4 collective-permute-start.4
  71.7 0.0 collective-permute-done.6
  71.7 0.5 collective-permute-start.5
  72.2 0.0 collective-permute-done.7
  72.3 0.0 collective-permute-done.8
  72.3 0.1 collective-permute-start.9
  72.4 4.4 %collective-permute-start.10 = (bf16[4,2,64,256]{3,2,1,0:T(8,128)(2,1)S(1)}, bf16[4,2,64,256]{3,2,1,0:T(8,128)(2,1)S(1)}, u32[]{:S(2)}, u32[]{:S(2)}) collective-permute-start(bf16[4,2,64,256]{3,2,1,0:T(8,128)(2,1)S(1)} %pad_maximum_fusion.1), channel_id=1, source_target_pairs={{0,64},{32,96},{64,0},{96,32},{1,65},{33,97},{65,1},{97,33},{2,66}... | collective-permute-start | bytes 786440 | tf_op jit(solution)/shard_map/ppermute | solution.py:142
  76.8 2.6 %collective-permute-done.3 = bf16[4,2,64,256]{3,2,1,0:T(8,128)(2,1)S(1)} collective-permute-done((bf16[4,2,64,256]{3,2,1,0:T(8,128)(2,1)S(1)}, bf16[4,2,64,256]{3,2,1,0:T(8,128)(2,1)S(1)}, u32[]{:S(2)}, u32[]{:S(2)}) %collective-permute-start.3) | collective-permute-done | bytes 262176 | tf_op jit(solution)/shard_map/ppermute | solution.py:142
  79.4 3.9 %collective-permute-start.11 = (bf16[4,2,64,256]{3,2,1,0:T(8,128)(2,1)S(1)}, bf16[4,2,64,256]{3,2,1,0:T(8,128)(2,1)S(1)}, u32[]{:S(2)}, u32[]{:S(2)}) collective-permute-start(bf16[4,2,64,256]{3,2,1,0:T(8,128)(2,1)S(1)} %pad_maximum_fusion.1), channel_id=1, source_target_pairs={{0,32},{32,64},{64,96},{96,0},{1,33},{33,65},{65,97},{97,1},{2,34}... | collective-permute-start | bytes 786440 | tf_op jit(solution)/shard_map/ppermute | solution.py:142
  83.3 0.0 collective-permute-done.4
  83.3 2.1 %collective-permute-done.5 = bf16[4,2,64,256]{3,2,1,0:T(8,128)(2,1)S(1)} collective-permute-done((bf16[4,2,64,256]{3,2,1,0:T(8,128)(2,1)S(1)}, bf16[4,2,64,256]{3,2,1,0:T(8,128)(2,1)S(1)}, u32[]{:S(2)}, u32[]{:S(2)}) %collective-permute-start.5) | collective-permute-done | bytes 262176 | tf_op jit(solution)/shard_map/ppermute | solution.py:142
  85.5 0.1 collective-permute-start.12
  85.6 0.0 collective-permute-done.9
  85.6 1.0 collective-permute-done.10
  86.6 0.6 collective-permute-done.11
  87.2 0.3 collective-permute-start.13
  87.5 0.6 pad_add_fusion.me_ref
  88.1 0.1 collective-permute-done.12
  88.2 2.1 %collective-permute-done.13 = bf16[16,2,64,256]{3,2,1,0:T(8,128)(2,1)} collective-permute-done((bf16[16,2,64,256]{3,2,1,0:T(8,128)(2,1)S(1)}, bf16[16,2,64,256]{3,2,1,0:T(8,128)(2,1)}, u32[]{:S(2)}, u32[]{:S(2)}) %collective-permute-start.13) | collective-permute-done | bytes 1048608 | tf_op jit(solution)/shard_map/ppermute | solution.py:155
  90.3 2.5 %turn_step.1.b_ref = bf16[2,512,2048]{2,1,0:T(8,128)(2,1)S(1)} custom-call(bf16[4,4,2,64,256]{4,3,2,1,0:T(8,128)(2,1)S(1)} %bitcast.17, bf16[4,4,2,64,256]{4,3,2,1,0:T(8,128)(2,1)S(1)} %bitcast.16, bf16[4,4,2,64,256]{4,3,2,1,0:T(8,128)(2,1)S(1)} %bitcast.18, bf16[4,4,2,64,256]{4,3,2,1,0:T(8,128)(2,1)} %bitcast.10.other_b), custom_call_target="tpu_custom_call" | custom-call | flops 4000000000 | bytes 8388608 | tf_op jit(solution)/shard_map/turn_step/pallas_call | solution.py:64
  92.8 0.0 copy-start
  92.8 2.0 %copy-done = bf16[2,512,2048]{2,1,0:T(8,128)(2,1)} copy-done((bf16[2,512,2048]{2,1,0:T(8,128)(2,1)}, bf16[2,512,2048]{2,1,0:T(8,128)(2,1)S(1)}, u32[]{:S(2)}) %copy-start) | copy-done | bytes 4194328
  94.8 0.0 all-to-all-done
  94.8 9.7 %second_step.1 = bf16[8,8,64,128]{3,2,1,0:T(8,128)(2,1)} custom-call(s32[3]{0:T(128)} %pad_add_fusion.me_ref, bf16[2,4,2,2,2,4,2,16,256]{8,7,6,5,4,3,2,1,0:T(8,128)(2,1)} %bitcast.5.x_ref, bf16[2,512,2048]{2,1,0:T(8,128)(2,1)} %copy-done), custom_call_target="tpu_custom_call" | custom-call | flops 4300000256 | bytes 9437184 | tf_op jit(solution)/shard_map/second_step/pallas_call | solution.py:100
  104.4 45.6 %all_to_all.10 = bf16[64,64,128]{2,1,0:T(8,128)(2,1)S(1)} all-to-all(bf16[64,64,128]{2,1,0:T(8,128)(2,1)} %bitcast.21), channel_id=1, replica_groups=mesh['xh'=2,'y'=4,'z'=8,'xl'=2,'core'=2] {'xh','y','z'}, dimensions={0} | all-to-all | bytes 2097152 | tf_op jit(solution)/shard_map/all_to_all | solution.py:160
  150.1 0.2 total_step.1
  150.3 1.0 copy.4
  (15 shorter events, 0.2 us)
Async XLA Ops:
  6.7 7.5 %copy-start.1 = (bf16[2,4,16,512]{3,2,1,0:T(8,128)(2,1)S(1)}, bf16[2,4,16,512]{3,2,1,0:T(8,128)(2,1)}, u32[]{:S(2)}) copy-start(bf16[2,4,16,512]{3,2,1,0:T(8,128)(2,1)} %param.5) | copy-start | bytes 393220
  6.7 88.1 %all-to-all-start = ((bf16[32,256,256]{2,1,0:T(8,128)(2,1)}), bf16[32,256,256]{2,1,0:T(8,128)(2,1)}, u32[]{:S(2)}, u32[]{:S(2)}) async-start(bf16[32,256,256]{2,1,0:T(8,128)(2,1)} %bitcast.19), calls=%async_computation | async-start | bytes 8388608 | tf_op jit(solution)/shard_map/all_to_all | solution.py:152
  14.3 47.4 %collective-permute-start = (bf16[1,2,64,256]{3,2,1,0:T(8,128)(2,1)S(1)}, bf16[1,2,64,256]{3,2,1,0:T(8,128)(2,1)S(1)}, u32[]{:S(2)}, u32[]{:S(2)}) collective-permute-start(bf16[1,2,64,256]{3,2,1,0:T(8,128)(2,1)S(1)} %get-tuple-element.8), channel_id=1, source_target_pairs={{0,96},{32,0},{64,32},{96,64},{1,97},{33,1},{65,33},{97,65},{2,98}... | collective-permute-start | bytes 196616 | tf_op jit(solution)/shard_map/ppermute | solution.py:142
  15.2 54.9 %collective-permute-start.1 = (bf16[1,2,64,256]{3,2,1,0:T(8,128)(2,1)S(1)}, bf16[1,2,64,256]{3,2,1,0:T(8,128)(2,1)S(1)}, u32[]{:S(2)}, u32[]{:S(2)}) collective-permute-start(bf16[1,2,64,256]{3,2,1,0:T(8,128)(2,1)S(1)} %get-tuple-element.8), channel_id=1, source_target_pairs={{0,64},{32,96},{64,0},{96,32},{1,65},{33,97},{65,1},{97,33},{2,66}... | collective-permute-start | bytes 196616 | tf_op jit(solution)/shard_map/ppermute | solution.py:142
  16.1 54.0 %collective-permute-start.2 = (bf16[1,2,64,256]{3,2,1,0:T(8,128)(2,1)S(1)}, bf16[1,2,64,256]{3,2,1,0:T(8,128)(2,1)S(1)}, u32[]{:S(2)}, u32[]{:S(2)}) collective-permute-start(bf16[1,2,64,256]{3,2,1,0:T(8,128)(2,1)S(1)} %get-tuple-element.8), channel_id=1, source_target_pairs={{0,32},{32,64},{64,96},{96,0},{1,33},{33,65},{65,97},{97,1},{2,34}... | collective-permute-start | bytes 196616 | tf_op jit(solution)/shard_map/ppermute | solution.py:142
  18.4 53.3 %collective-permute-start.6 = (bf16[1,2,64,256]{3,2,1,0:T(8,128)(2,1)S(1)}, bf16[1,2,64,256]{3,2,1,0:T(8,128)(2,1)S(1)}, u32[]{:S(2)}, u32[]{:S(2)}) collective-permute-start(bf16[1,2,64,256]{3,2,1,0:T(8,128)(2,1)S(1)} %get-tuple-element.5), channel_id=1, source_target_pairs={{0,130},{2,0},{128,2},{130,128},{1,131},{3,1},{129,3},{131,129},{4... | collective-permute-start | bytes 196616 | tf_op jit(solution)/shard_map/ppermute | solution.py:142
  21.1 51.1 %collective-permute-start.7 = (bf16[1,2,64,256]{3,2,1,0:T(8,128)(2,1)S(1)}, bf16[1,2,64,256]{3,2,1,0:T(8,128)(2,1)S(1)}, u32[]{:S(2)}, u32[]{:S(2)}) collective-permute-start(bf16[1,2,64,256]{3,2,1,0:T(8,128)(2,1)S(1)} %get-tuple-element.5), channel_id=1, source_target_pairs={{0,128},{2,130},{128,0},{130,2},{1,129},{3,131},{129,1},{131,3},{4... | collective-permute-start | bytes 196616 | tf_op jit(solution)/shard_map/ppermute | solution.py:142
  61.6 10.6 %collective-permute-start.8 = (bf16[1,2,64,256]{3,2,1,0:T(8,128)(2,1)S(1)}, bf16[1,2,64,256]{3,2,1,0:T(8,128)(2,1)S(1)}, u32[]{:S(2)}, u32[]{:S(2)}) collective-permute-start(bf16[1,2,64,256]{3,2,1,0:T(8,128)(2,1)S(1)} %get-tuple-element.5), channel_id=1, source_target_pairs={{0,2},{2,128},{128,130},{130,0},{1,3},{3,129},{129,131},{131,1},{4... | collective-permute-start | bytes 196616 | tf_op jit(solution)/shard_map/ppermute | solution.py:142
  70.1 9.3 %collective-permute-start.3 = (bf16[4,2,64,256]{3,2,1,0:T(8,128)(2,1)S(1)}, bf16[4,2,64,256]{3,2,1,0:T(8,128)(2,1)S(1)}, u32[]{:S(2)}, u32[]{:S(2)}) collective-permute-start(bf16[4,2,64,256]{3,2,1,0:T(8,128)(2,1)S(1)} %pad_maximum_fusion), channel_id=1, source_target_pairs={{0,130},{2,0},{128,2},{130,128},{1,131},{3,1},{129,3},{131,129},{4... | collective-permute-start | bytes 786440 | tf_op jit(solution)/shard_map/ppermute | solution.py:142
  70.3 13.0 %collective-permute-start.4 = (bf16[4,2,64,256]{3,2,1,0:T(8,128)(2,1)S(1)}, bf16[4,2,64,256]{3,2,1,0:T(8,128)(2,1)S(1)}, u32[]{:S(2)}, u32[]{:S(2)}) collective-permute-start(bf16[4,2,64,256]{3,2,1,0:T(8,128)(2,1)S(1)} %pad_maximum_fusion), channel_id=1, source_target_pairs={{0,128},{2,130},{128,0},{130,2},{1,129},{3,131},{129,1},{131,3},{4... | collective-permute-start | bytes 786440 | tf_op jit(solution)/shard_map/ppermute | solution.py:142
  71.7 13.7 %collective-permute-start.5 = (bf16[4,2,64,256]{3,2,1,0:T(8,128)(2,1)S(1)}, bf16[4,2,64,256]{3,2,1,0:T(8,128)(2,1)S(1)}, u32[]{:S(2)}, u32[]{:S(2)}) collective-permute-start(bf16[4,2,64,256]{3,2,1,0:T(8,128)(2,1)S(1)} %pad_maximum_fusion), channel_id=1, source_target_pairs={{0,2},{2,128},{128,130},{130,0},{1,3},{3,129},{129,131},{131,1},{4... | collective-permute-start | bytes 786440 | tf_op jit(solution)/shard_map/ppermute | solution.py:142
  72.3 13.3 %collective-permute-start.9 = (bf16[4,2,64,256]{3,2,1,0:T(8,128)(2,1)S(1)}, bf16[4,2,64,256]{3,2,1,0:T(8,128)(2,1)S(1)}, u32[]{:S(2)}, u32[]{:S(2)}) collective-permute-start(bf16[4,2,64,256]{3,2,1,0:T(8,128)(2,1)S(1)} %pad_maximum_fusion.1), channel_id=1, source_target_pairs={{0,96},{32,0},{64,32},{96,64},{1,97},{33,1},{65,33},{97,65},{2,98}... | collective-permute-start | bytes 786440 | tf_op jit(solution)/shard_map/ppermute | solution.py:142
  72.4 14.2 %collective-permute-start.10 = (bf16[4,2,64,256]{3,2,1,0:T(8,128)(2,1)S(1)}, bf16[4,2,64,256]{3,2,1,0:T(8,128)(2,1)S(1)}, u32[]{:S(2)}, u32[]{:S(2)}) collective-permute-start(bf16[4,2,64,256]{3,2,1,0:T(8,128)(2,1)S(1)} %pad_maximum_fusion.1), channel_id=1, source_target_pairs={{0,64},{32,96},{64,0},{96,32},{1,65},{33,97},{65,1},{97,33},{2,66}... | collective-permute-start | bytes 786440 | tf_op jit(solution)/shard_map/ppermute | solution.py:142
  79.4 7.8 %collective-permute-start.11 = (bf16[4,2,64,256]{3,2,1,0:T(8,128)(2,1)S(1)}, bf16[4,2,64,256]{3,2,1,0:T(8,128)(2,1)S(1)}, u32[]{:S(2)}, u32[]{:S(2)}) collective-permute-start(bf16[4,2,64,256]{3,2,1,0:T(8,128)(2,1)S(1)} %pad_maximum_fusion.1), channel_id=1, source_target_pairs={{0,32},{32,64},{64,96},{96,0},{1,33},{33,65},{65,97},{97,1},{2,34}... | collective-permute-start | bytes 786440 | tf_op jit(solution)/shard_map/ppermute | solution.py:142
  85.5 2.7 %collective-permute-start.12 = (bf16[16,2,64,256]{3,2,1,0:T(8,128)(2,1)S(1)}, bf16[16,2,64,256]{3,2,1,0:T(8,128)(2,1)S(1)}, u32[]{:S(2)}, u32[]{:S(2)}) collective-permute-start(bf16[16,2,64,256]{3,2,1,0:T(8,128)(2,1)S(1)} %constant_dynamic-update-slice_fusion), channel_id=1, source_target_pairs={{0,1},{1,0},{2,3},{3,2},{4,5},{5,4},{6,7},{7,6},{8,9},{9,8},{10,11... | collective-permute-start | bytes 3145736 | tf_op jit(solution)/shard_map/ppermute | solution.py:155
  87.2 3.1 %collective-permute-start.13 = (bf16[16,2,64,256]{3,2,1,0:T(8,128)(2,1)S(1)}, bf16[16,2,64,256]{3,2,1,0:T(8,128)(2,1)}, u32[]{:S(2)}, u32[]{:S(2)}) collective-permute-start(bf16[16,2,64,256]{3,2,1,0:T(8,128)(2,1)S(1)} %constant_dynamic-update-slice_fusion.7), channel_id=1, source_target_pairs={{0,1},{1,0},{2,3},{3,2},{4,5},{5,4},{6,7},{7,6},{8,9},{9,8},{10,11... | collective-permute-start | bytes 3145736 | tf_op jit(solution)/shard_map/ppermute | solution.py:155
  92.8 2.0 %copy-start = (bf16[2,512,2048]{2,1,0:T(8,128)(2,1)}, bf16[2,512,2048]{2,1,0:T(8,128)(2,1)S(1)}, u32[]{:S(2)}) copy-start(bf16[2,512,2048]{2,1,0:T(8,128)(2,1)S(1)} %turn_step.1.b_ref) | copy-start | bytes 12582916

commit v3 on v1

v3 whole, which is shorter than its diff:
```python
import functools

import jax
import jax.numpy as jnp
from jax import lax
from jax.experimental import pallas as pl
from jax.experimental.pallas import tpu as pltpu
from jax.sharding import Mesh
from jax.sharding import PartitionSpec as P

PLANE = ("xh", "y", "xl", "core")
ROWS = ("xh", "xl")
OWNERS = ("z", "xh", "y")
NT = (((1,), (1,)), ((), ()))
NN = (((1,), (0,)), ((), ()))
RING = 4


def first_kernel(begin, count, stem_hbm, branch_hbm, *refs):
    out_hbm, stem, branch, lhs, out, in_sem, branch_sem, out_sem = refs[-8:]
    part = pl.ds(begin, count)
    branch_copy = pltpu.make_async_copy(branch_hbm.at[:, part], branch, branch_sem)
    branch_copy.start()
    copies = [
        pltpu.make_async_copy(stem_hbm.at[:, part, :, w], stem.at[:, :, :, w], in_sem.at[w]) for w in range(4)
    ]
    for copy in copies:
        copy.start()
    row = lax.broadcasted_iota(jnp.int32, (256, 256), 0)
    col = lax.broadcasted_iota(jnp.int32, (256, 256), 1)
    regroup = (col == (row % 16) * 16 + row // 16).astype(jnp.bfloat16)
    branch_copy.wait()
    for s in range(count):
        br = [
            lax.dot_general(regroup, branch[r, s], NT, preferred_element_type=jnp.float32).astype(jnp.bfloat16)
            for r in range(2)
        ]
        lhs[s, 0:256, 0:256] = br[0]
        lhs[s, 0:256, 256:512] = -br[1]
        lhs[s, 256:512, 0:256] = br[1]
        lhs[s, 256:512, 256:512] = br[0]
    sends = []
    for w in range(4):
        copies[w].wait()
        for s in range(count):
            rhs = jnp.concatenate([stem[r, s, :, w].reshape(256, 256) for r in range(2)], axis=1)
            res = lax.dot_general(lhs[s], rhs, NT, preferred_element_type=jnp.float32).astype(jnp.bfloat16)
            for r in range(2):
                out[:, w, :, r, s] = res[r * 256 : (r + 1) * 256].reshape(8, 2, 16, 256)
        sends.append(pltpu.make_async_copy(out.at[:, w], out_hbm.at[:, w, :, :, part], out_sem.at[w]))
        sends[-1].start()
    for send in sends:
        send.wait()


def first_step(stem, branch, begin, count, filled=None):
    slices = stem.shape[1]
    operands = [stem, branch] + ([] if filled is None else [filled])
    return pl.pallas_call(
        functools.partial(first_kernel, begin, count),
        in_specs=[pl.BlockSpec(memory_space=pl.ANY)] * len(operands),
        out_specs=pl.BlockSpec(memory_space=pl.ANY),
        out_shape=jax.ShapeDtypeStruct((8, 4, 2, 2, slices, 16, 256), jnp.bfloat16),
        scratch_shapes=[
            pltpu.VMEM((2, count, 8, 4, 32, 256), jnp.bfloat16),
            pltpu.VMEM((2, count, 256, 256), jnp.bfloat16),
            pltpu.VMEM((count, 512, 512), jnp.bfloat16),
            pltpu.VMEM((8, 4, 2, 2, count, 16, 256), jnp.bfloat16),
            pltpu.SemaphoreType.DMA((4,)),
            pltpu.SemaphoreType.DMA,
            pltpu.SemaphoreType.DMA((4,)),
        ],
        input_output_aliases={} if filled is None else {2: 0},
        compiler_params=pltpu.CompilerParams(vmem_limit_bytes=56 << 20),
        cost_estimate=pl.CostEstimate(flops=12000000000, bytes_accessed=5 << 20, transcendentals=0),
        name="first_step",
    )(*operands)


def turn_kernel(me_ref, own_ref, other_ref, out_ref):
    first_core = me_ref[2] == 0
    for dx in range(RING):
        x = (me_ref[0] + dx) % RING
        for dy in range(RING):
            y = (me_ref[1] + dy) % RING
            at = pl.multiple_of((((x // 2) * RING + y) * 2 + x % 2) * 128, 128)
            for r in range(2):
                low = jnp.where(first_core, own_ref[dx, dy, r], other_ref[dx, dy, r])
                high = jnp.where(first_core, other_ref[dy, dx, r], own_ref[dy, dx, r])
                out_ref[r, :, pl.ds(at, 128)] = jnp.concatenate([low, high], axis=0).T


def turn_step(me, own, other):
    return pl.pallas_call(
        turn_kernel,
        in_specs=[pl.BlockSpec(memory_space=pltpu.SMEM)] + [pl.BlockSpec(memory_space=pltpu.VMEM)] * 2,
        out_specs=pl.BlockSpec(memory_space=pltpu.VMEM),
        out_shape=jax.ShapeDtypeStruct((2, 512, 2048), jnp.bfloat16),
        compiler_params=pltpu.CompilerParams(vmem_limit_bytes=32 << 20),
        cost_estimate=pl.CostEstimate(flops=18000000000, bytes_accessed=8 << 20, transcendentals=0),
        name="turn_step",
    )(me, own, other)


def second_kernel(x_hbm, b_hbm, out_hbm, x, b, held, out, x_sem, b_sem, out_sem):
    x_copies = [pltpu.make_async_copy(x_hbm.at[:, lh], x.at[lh], x_sem.at[lh]) for lh in range(2)]
    b_copies = [
        pltpu.make_async_copy(b_hbm.at[:, pl.ds(t * 128, 128)], b.at[:, pl.ds(t * 128, 128)], b_sem.at[t])
        for t in range(4)
    ]
    x_copies[0].start()
    b_copies[0].start()

    def dot(left, right):
        return lax.dot_general(left, right, NN, preferred_element_type=jnp.float32)

    sends = []
    for lh in range(2):
        x_copies[lh].wait()
        xr, xi = (x[lh, :, r].reshape(2048, 256) for r in range(2))
        for t in range(4):
            if lh == 0:
                b_copies[t].wait()
                if t == 0:
                    for copy in (*b_copies[1:], x_copies[1]):
                        copy.start()
            rows = slice(t * 128, (t + 1) * 128)
            br, bi = b[0, rows], b[1, rows]
            res = [dot(br, xr) + dot(-bi, xi), dot(bi, xr) + dot(br, xi)]
            res = [part.astype(jnp.bfloat16) for part in res]
            if lh == 0:
                for r in range(2):
                    held[r, rows] = res[r]
            else:
                parts = [held[0, rows], res[0], held[1, rows], res[1]]
                for za in range(8):
                    joined = jnp.concatenate([part[:, za * 32 : (za + 1) * 32] for part in parts], axis=1)
                    out[za, t * 2 : (t + 1) * 2] = joined.reshape(2, 64, 128)
                blocks = pl.ds(t * 2, 2)
                sends.append(pltpu.make_async_copy(out.at[:, blocks], out_hbm.at[:, blocks], out_sem.at[t]))
                sends[-1].start()
    for send in sends:
        send.wait()


def second_step(x, b2):
    shape = (8, 8, 64, 128)
    return pl.pallas_call(
        second_kernel,
        in_specs=[pl.BlockSpec(memory_space=pl.ANY)] * 2,
        out_specs=pl.BlockSpec(memory_space=pl.ANY),
        out_shape=jax.ShapeDtypeStruct(shape, jnp.bfloat16),
        scratch_shapes=[
            pltpu.VMEM((2, 32, 2, 64, 256), jnp.bfloat16),
            pltpu.VMEM((2, 512, 2048), jnp.bfloat16),
            pltpu.VMEM((2, 512, 256), jnp.bfloat16),
            pltpu.VMEM(shape, jnp.bfloat16),
            pltpu.SemaphoreType.DMA((2,)),
            pltpu.SemaphoreType.DMA((4,)),
            pltpu.SemaphoreType.DMA((4,)),
        ],
        compiler_params=pltpu.CompilerParams(vmem_limit_bytes=60 << 20),
        cost_estimate=pl.CostEstimate(flops=4300000000, bytes_accessed=9 << 20, transcendentals=0),
        name="second_step",
    )(x, b2)


def total_kernel(in_ref, out_ref):
    sums = []
    for i in range(8):
        acc = in_ref[0, i].astype(jnp.float32)
        for z in range(1, 8):
            acc = acc + in_ref[z, i].astype(jnp.float32)
        sums.append(acc)
    for r in range(2):
        out_ref[r, :, 0] = jnp.concatenate([acc[:, r * 64 : (r + 1) * 64] for acc in sums], axis=1)


def total_step(arrived):
    return pl.pallas_call(
        total_kernel,
        out_shape=jax.ShapeDtypeStruct((2, 64, 1, 512), jnp.float32),
        compiler_params=pltpu.CompilerParams(vmem_limit_bytes=16 << 20),
        cost_estimate=pl.CostEstimate(flops=1000000, bytes_accessed=2 << 20, transcendentals=0),
        name="total_step",
    )(arrived)


def place(x, y, core):
    return ((x // 2 * RING + y) * 2 + x % 2) * 2 + core


def ring_blocks(block, stage):
    blocks = [block]
    for d in range(1, RING):
        pairs = []
        for x in range(RING):
            for y in range(RING):
                for core in range(2):
                    along_y = core == stage
                    source = place(x, (y + d) % RING, core) if along_y else place((x + d) % RING, y, core)
                    pairs.append((source, place(x, y, core)))
        blocks.append(lax.ppermute(block, PLANE, pairs))
    return blocks


def pack_kernel(*refs):
    rows = refs[0].shape[0]
    for n, ref in enumerate(refs[:-1]):
        refs[-1][n * rows : (n + 1) * rows] = ref[...]


def pack(blocks):
    return pl.pallas_call(
        pack_kernel,
        in_specs=[pl.BlockSpec(memory_space=pltpu.VMEM)] * len(blocks),
        out_specs=pl.BlockSpec(memory_space=pltpu.VMEM),
        out_shape=jax.ShapeDtypeStruct((len(blocks) * blocks[0].shape[0], *blocks[0].shape[1:]), blocks[0].dtype),
        compiler_params=pltpu.CompilerParams(vmem_limit_bytes=24 << 20),
        cost_estimate=pl.CostEstimate(flops=1000000, bytes_accessed=1 << 20, transcendentals=0),
        name="pack",
    )(*blocks)


def shards(stem_tensor, branch_first, branch_second):
    slices = stem_tensor.shape[1]
    me = jnp.stack([lax.axis_index(ROWS), lax.axis_index("y"), lax.axis_index("core")]).astype(jnp.int32)
    stem = stem_tensor.reshape(2, slices, 8, 4, 32, 256)
    near = ring_blocks(branch_second.reshape(1, 2, slices * 16, 512), 0)
    sent = first_step(stem, branch_first, 0, slices).reshape(32, 2 * 2 * slices * 16, 256)
    sent, near = lax.optimization_barrier((sent, near))
    own = pack(ring_blocks(pack(near), 1))
    arrived = lax.all_to_all(sent, PLANE, split_axis=0, concat_axis=0, tiled=True)
    other = lax.ppermute(own, "core", [(0, 1), (1, 0)])
    grid = (RING, RING, 2, slices * 16, 512)
    turned = turn_step(me, own.reshape(grid), other.reshape(grid))
    partial = second_step(arrived.reshape(32, 2, 2, slices * 16, 256), turned)
    owned = lax.all_to_all(partial.reshape(64, 64, 128), OWNERS, split_axis=0, concat_axis=0, tiled=True)
    return total_step(owned.reshape(8, 8, 64, 128))


def solution(mesh):
    fine = Mesh(mesh.devices.reshape(2, 4, 8, 2, 2), ("xh", "y", "z", "xl", "core"))
    cuts, mode = ("xh", "y"), ("z", "xl", "core")
    in_specs = (
        P(None, cuts, mode, None, None, None),
        P(None, cuts, None, None),
        P(None, cuts, mode, None),
    )
    return jax.shard_map(
        shards, mesh=fine, in_specs=in_specs, out_specs=P(None, cuts, mode, None), check_vma=False
    )
```

time: 168 us -> 132 us (0.79)
  blocking collectives: 108 us -> 43.4 us
  waiting for transfers between devices: 27.8 us -> 45.2 us
  starting transfers between devices: 0.01 us -> 17.1 us
  between operations: 13.4 us -> 0.09 us
  Pallas kernels: 11.4 us -> 19.3 us
    all_to_all x1 -> x0, blocking collectives: 66.1 us -> none  [shards(): lax.all_to_all(sent, PLANE, split_axis=0, concat_axis=0, tiled=True)]
    all_to_all x0 -> x1, waiting for transfers between devices: none -> 36.3 us  [shards(): lax.all_to_all(sent, PLANE, split_axis=0, concat_axis=0, tiled=True)]
    all_gather x1 -> x0, waiting for transfers between devices: 27.1 us -> none  [shards(): lax.all_gather(branch_second.reshape(2 * slices * 16, 512), PLANE, axis=0...]
    ppermute x0 -> x7, starting transfers between devices: none -> 9.35 us  [the longest x6 8.09 us: ring_blocks(): blocks.append(lax.ppermute(block, PLANE, pairs))]
    ppermute x0 -> x7, waiting for transfers between devices: none -> 8.87 us  [the longest x6 5.02 us: ring_blocks(): blocks.append(lax.ppermute(block, PLANE, pairs))]
    pallas_call x3 -> x6, Pallas kernels: 11.4 us -> 19.3 us  [the longest x1 8.55 us: second_step(): pl.pallas_call(second_kernel, in_specs=[pl.BlockSpec(memory_space=pl.ANY)...]
    all_to_all x0 -> x1, starting transfers between devices: none -> 7.75 us  [shards(): lax.all_to_all(sent, PLANE, split_axis=0, concat_axis=0, tiled=True)]
    unnamed x6 -> x12, local copies, waits for them, and re-layouts: 5.59 us -> 5.69 us
  transfers between devices with their start and end apart: 1 -> 8, of which waited for: 1 -> 5; matrix products, arithmetic and copies ran while one was open for 0% -> 0% of each run, Pallas kernels for 2% -> 7%
where the time goes in v3:
time: 132 us; the launch traced here: 131 us
  waiting for transfers between devices  45.2 us (34%)
  blocking collectives  43.4 us (33%)
  Pallas kernels  19.3 us (15%)
  starting transfers between devices  17.1 us (13%)
  local copies, waits for them, and re-layouts  5.69 us (4%)
    all_to_all x1, blocking collectives, shards(): lax.all_to_all(partial.reshape(64, 64, 128), OWNERS, split_axis=0, concat...  43.4 us
    all_to_all x1, waiting for transfers between devices, shards(): lax.all_to_all(sent, PLANE, split_axis=0, concat_axis=0, tiled=True)  36.3 us
    pallas_call x1, Pallas kernels, second_step(): pl.pallas_call(second_kernel, in_specs=[pl.BlockSpec(memory_space=pl.ANY)...  8.55 us
    ppermute x6, starting transfers between devices, ring_blocks(): blocks.append(lax.ppermute(block, PLANE, pairs))  8.09 us
    all_to_all x1, starting transfers between devices, shards(): lax.all_to_all(sent, PLANE, split_axis=0, concat_axis=0, tiled=True)  7.75 us
    pallas_call x1, Pallas kernels, first_step(): pl.pallas_call(functools.partial(first_kernel, begin, count), in_specs=[p...  6.72 us
    unnamed x12, local copies, waits for them, and re-layouts  5.69 us
    ppermute x6, waiting for transfers between devices, ring_blocks(): blocks.append(lax.ppermute(block, PLANE, pairs))  5.02 us
  transfers between devices with their start and end apart: 8, of which 5 were waited for; matrix products, arithmetic and copies ran while one was open for 0% of the time, Pallas kernels for 7%

profile of v3, /device:TPU:24, one launch (start us, length us, event | category | flops | bytes accessed | tf_op | source)
XLA Modules:
  0.0 130.9 jit_solution(8741855128067156277)
XLA Ops:
  0.0 2.0 %collective-permute-start.2 = (bf16[1,2,64,512]{3,2,1,0:T(8,128)(2,1)}, bf16[1,2,64,512]{3,2,1,0:T(8,128)(2,1)S(1)}, u32[]{:S(2)}, u32[]{:S(2)}) collective-permute-start(bf16[1,2,64,512]{3,2,1,0:T(8,128)(2,1)} %bitcast.13), channel_id=1, source_target_pairs={{96,0},{131,1},{0,32},{163,33},{32,64},{195,65},{64,96},{227,97},{... | collective-permute-start | bytes 393224 | tf_op jit(solution)/shard_map/ppermute | solution.py:203
  2.0 0.9 collective-permute-start.1
  2.8 0.0 collective-permute-start
  2.8 0.0 copy-start.4
  2.8 6.7 %first_step.1 = bf16[8,4,2,2,4,16,256]{6,5,4,3,2,1,0:T(8,128)(2,1)} custom-call(bf16[2,4,8,4,32,256]{5,4,3,2,1,0:T(8,128)(2,1)} %bitcast.19, bf16[2,4,256,256]{3,2,1,0:T(8,128)(2,1)} %branch_hbm.1), custom_call_target="tpu_custom_call" | custom-call | flops 12000000000 | bytes 5242880 | tf_op jit(solution)/shard_map/first_step/pallas_call | solution.py:59
  9.6 0.0 collective-permute-done.2.refs_3_
  9.6 0.0 collective-permute-done.1.refs_2_
  9.6 0.5 collective-permute-done.refs_1_
  10.0 0.0 copy-done.4
  10.1 1.1 collective-permute-start.5
  11.2 2.7 %collective-permute-start.4 = (bf16[4,2,64,512]{3,2,1,0:T(8,128)(2,1)S(1)}, bf16[4,2,64,512]{3,2,1,0:T(8,128)(2,1)S(1)}, u32[]{:S(2)}, u32[]{:S(2)}) collective-permute-start(bf16[4,2,64,512]{3,2,1,0:T(8,128)(2,1)S(1)} %pack.2.refs_0_), channel_id=1, source_target_pairs={{128,0},{65,1},{160,32},{97,33},{192,64},{1,65},{224,96},{33,97},{... | collective-permute-start | bytes 1572872 | tf_op jit(solution)/shard_map/ppermute | solution.py:203
  13.9 1.4 %collective-permute-start.3 = (bf16[4,2,64,512]{3,2,1,0:T(8,128)(2,1)S(1)}, bf16[4,2,64,512]{3,2,1,0:T(8,128)(2,1)S(1)}, u32[]{:S(2)}, u32[]{:S(2)}) collective-permute-start(bf16[4,2,64,512]{3,2,1,0:T(8,128)(2,1)S(1)} %pack.2.refs_0_), channel_id=1, source_target_pairs={{2,0},{33,1},{34,32},{65,33},{66,64},{97,65},{98,96},{1,97},{128,2... | collective-permute-start | bytes 1572872 | tf_op jit(solution)/shard_map/ppermute | solution.py:203
  15.4 7.8 %all-to-all-start = ((bf16[32,256,256]{2,1,0:T(8,128)(2,1)}), bf16[32,256,256]{2,1,0:T(8,128)(2,1)}, u32[]{:S(2)}, u32[]{:S(2)}) async-start(bf16[32,256,256]{2,1,0:T(8,128)(2,1)} %bitcast.17), calls=%async_computation | async-start | bytes 8388608 | tf_op jit(solution)/shard_map/all_to_all | solution.py:233
  23.1 0.0 collective-permute-done.5.refs_3_
  23.1 3.6 %collective-permute-done.4.refs_2_ = bf16[4,2,64,512]{3,2,1,0:T(8,128)(2,1)S(1)} collective-permute-done((bf16[4,2,64,512]{3,2,1,0:T(8,128)(2,1)S(1)}, bf16[4,2,64,512]{3,2,1,0:T(8,128)(2,1)S(1)}, u32[]{:S(2)}, u32[]{:S(2)}) %collective-permute-start.4) | collective-permute-done | bytes 524320 | tf_op jit(solution)/shard_map/ppermute | solution.py:203
  26.7 0.0 copy-start
  26.7 0.8 copy-done
  27.5 1.0 collective-permute-done.3.refs_1_
  28.5 0.0 copy-start.2
  28.5 0.8 copy-done.2
  29.3 0.0 copy-start.1
  29.3 1.0 copy-done.1
  30.4 0.0 copy-start.3
  30.4 1.0 copy-done.3
  31.4 0.1 pack.3
  31.6 1.3 collective-permute-start.6
  32.8 0.1 pad_add_fusion.me_ref
  32.9 3.8 %collective-permute-done.6 = bf16[16,2,64,512]{3,2,1,0:T(8,128)(2,1)} collective-permute-done((bf16[16,2,64,512]{3,2,1,0:T(8,128)(2,1)S(1)}, bf16[16,2,64,512]{3,2,1,0:T(8,128)(2,1)}, u32[]{:S(2)}, u32[]{:S(2)}) %collective-permute-start.6) | collective-permute-done | bytes 2097184 | tf_op jit(solution)/shard_map/ppermute | solution.py:234
  36.7 2.9 %turn_step.1.b_hbm = bf16[2,512,2048]{2,1,0:T(8,128)(2,1)S(1)} custom-call(s32[3]{0:T(128)S(1)} %pad_add_fusion.me_ref, bf16[4,4,2,64,512]{4,3,2,1,0:T(8,128)(2,1)S(1)} %bitcast.12, bf16[4,4,2,64,512]{4,3,2,1,0:T(8,128)(2,1)} %bitcast.8.other_ref), custom_call_target="tpu_custom_call" | custom-call | flops 17999998976 | bytes 8388608 | tf_op jit(solution)/shard_map/turn_step/pallas_call | solution.py:94
  39.7 0.0 copy-start.5
  39.7 2.0 %copy-done.5 = bf16[2,512,2048]{2,1,0:T(8,128)(2,1)} copy-done((bf16[2,512,2048]{2,1,0:T(8,128)(2,1)}, bf16[2,512,2048]{2,1,0:T(8,128)(2,1)S(1)}, u32[]{:S(2)}) %copy-start.5) | copy-done | bytes 4194328
  41.6 36.3 %all-to-all-done = bf16[32,256,256]{2,1,0:T(8,128)(2,1)} async-done(((bf16[32,256,256]{2,1,0:T(8,128)(2,1)}), bf16[32,256,256]{2,1,0:T(8,128)(2,1)}, u32[]{:S(2)}, u32[]{:S(2)}) %all-to-all-start) | async-done | bytes 4194336 | tf_op jit(solution)/shard_map/all_to_all | solution.py:233
  78.0 8.5 %second_step.1 = bf16[8,8,64,128]{3,2,1,0:T(8,128)(2,1)} custom-call(bf16[32,2,2,64,256]{4,3,2,1,0:T(8,128)(2,1)} %bitcast.3.x_hbm, bf16[2,512,2048]{2,1,0:T(8,128)(2,1)} %copy-done.5), custom_call_target="tpu_custom_call" | custom-call | flops 4300000256 | bytes 9437184 | tf_op jit(solution)/shard_map/second_step/pallas_call | solution.py:148
  86.5 43.4 %all_to_all.10 = bf16[64,64,128]{2,1,0:T(8,128)(2,1)S(1)} all-to-all(bf16[64,64,128]{2,1,0:T(8,128)(2,1)} %bitcast.18), channel_id=1, replica_groups=mesh['xh'=2,'y'=4,'z'=8,'xl'=2,'core'=2] {'z','xh','y'}, dimensions={0} | all-to-all | bytes 2097152 | tf_op jit(solution)/shard_map/all_to_all | solution.py:238
  130.0 0.9 total_step.1
  (1 shorter events, 0.0 us)
Async XLA Ops:
  0.0 9.6 %collective-permute-start.2 = (bf16[1,2,64,512]{3,2,1,0:T(8,128)(2,1)}, bf16[1,2,64,512]{3,2,1,0:T(8,128)(2,1)S(1)}, u32[]{:S(2)}, u32[]{:S(2)}) collective-permute-start(bf16[1,2,64,512]{3,2,1,0:T(8,128)(2,1)} %bitcast.13), channel_id=1, source_target_pairs={{96,0},{131,1},{0,32},{163,33},{32,64},{195,65},{64,96},{227,97},{... | collective-permute-start | bytes 393224 | tf_op jit(solution)/shard_map/ppermute | solution.py:203
  2.0 7.6 %collective-permute-start.1 = (bf16[1,2,64,512]{3,2,1,0:T(8,128)(2,1)}, bf16[1,2,64,512]{3,2,1,0:T(8,128)(2,1)S(1)}, u32[]{:S(2)}, u32[]{:S(2)}) collective-permute-start(bf16[1,2,64,512]{3,2,1,0:T(8,128)(2,1)} %bitcast.14), channel_id=1, source_target_pairs={{64,0},{129,1},{96,32},{161,33},{0,64},{193,65},{32,96},{225,97},{... | collective-permute-start | bytes 393224 | tf_op jit(solution)/shard_map/ppermute | solution.py:203
  2.8 7.2 %collective-permute-start = (bf16[1,2,64,512]{3,2,1,0:T(8,128)(2,1)}, bf16[1,2,64,512]{3,2,1,0:T(8,128)(2,1)S(1)}, u32[]{:S(2)}, u32[]{:S(2)}) collective-permute-start(bf16[1,2,64,512]{3,2,1,0:T(8,128)(2,1)} %bitcast.15), channel_id=1, source_target_pairs={{32,0},{3,1},{64,32},{35,33},{96,64},{67,65},{0,96},{99,97},{34,2}... | collective-permute-start | bytes 393224 | tf_op jit(solution)/shard_map/ppermute | solution.py:203
  2.8 7.2 %copy-start.4 = (bf16[2,4,16,512]{3,2,1,0:T(8,128)(2,1)S(1)}, bf16[2,4,16,512]{3,2,1,0:T(8,128)(2,1)}, u32[]{:S(2)}) copy-start(bf16[2,4,16,512]{3,2,1,0:T(8,128)(2,1)} %param.5) | copy-start | bytes 393220
  10.1 13.0 %collective-permute-start.5 = (bf16[4,2,64,512]{3,2,1,0:T(8,128)(2,1)S(1)}, bf16[4,2,64,512]{3,2,1,0:T(8,128)(2,1)S(1)}, u32[]{:S(2)}, u32[]{:S(2)}) collective-permute-start(bf16[4,2,64,512]{3,2,1,0:T(8,128)(2,1)S(1)} %pack.2.refs_0_), channel_id=1, source_target_pairs={{130,0},{97,1},{162,32},{1,33},{194,64},{33,65},{226,96},{65,97},{... | collective-permute-start | bytes 1572872 | tf_op jit(solution)/shard_map/ppermute | solution.py:203
  11.2 15.5 %collective-permute-start.4 = (bf16[4,2,64,512]{3,2,1,0:T(8,128)(2,1)S(1)}, bf16[4,2,64,512]{3,2,1,0:T(8,128)(2,1)S(1)}, u32[]{:S(2)}, u32[]{:S(2)}) collective-permute-start(bf16[4,2,64,512]{3,2,1,0:T(8,128)(2,1)S(1)} %pack.2.refs_0_), channel_id=1, source_target_pairs={{128,0},{65,1},{160,32},{97,33},{192,64},{1,65},{224,96},{33,97},{... | collective-permute-start | bytes 1572872 | tf_op jit(solution)/shard_map/ppermute | solution.py:203
  13.9 14.6 %collective-permute-start.3 = (bf16[4,2,64,512]{3,2,1,0:T(8,128)(2,1)S(1)}, bf16[4,2,64,512]{3,2,1,0:T(8,128)(2,1)S(1)}, u32[]{:S(2)}, u32[]{:S(2)}) collective-permute-start(bf16[4,2,64,512]{3,2,1,0:T(8,128)(2,1)S(1)} %pack.2.refs_0_), channel_id=1, source_target_pairs={{2,0},{33,1},{34,32},{65,33},{66,64},{97,65},{98,96},{1,97},{128,2... | collective-permute-start | bytes 1572872 | tf_op jit(solution)/shard_map/ppermute | solution.py:203
  15.4 62.6 %all-to-all-start = ((bf16[32,256,256]{2,1,0:T(8,128)(2,1)}), bf16[32,256,256]{2,1,0:T(8,128)(2,1)}, u32[]{:S(2)}, u32[]{:S(2)}) async-start(bf16[32,256,256]{2,1,0:T(8,128)(2,1)} %bitcast.17), calls=%async_computation | async-start | bytes 8388608 | tf_op jit(solution)/shard_map/all_to_all | solution.py:233
  26.7 0.8 copy-start
  28.5 0.8 copy-start.2
  29.3 1.0 copy-start.1
  30.4 1.0 copy-start.3
  31.6 5.2 %collective-permute-start.6 = (bf16[16,2,64,512]{3,2,1,0:T(8,128)(2,1)S(1)}, bf16[16,2,64,512]{3,2,1,0:T(8,128)(2,1)}, u32[]{:S(2)}, u32[]{:S(2)}) collective-permute-start(bf16[16,2,64,512]{3,2,1,0:T(8,128)(2,1)S(1)} %pack.3), channel_id=1, source_target_pairs={{0,1},{1,0},{2,3},{3,2},{4,5},{5,4},{6,7},{7,6},{8,9},{9,8},{10,11... | collective-permute-start | bytes 6291464 | tf_op jit(solution)/shard_map/ppermute | solution.py:234
  39.7 2.0 %copy-start.5 = (bf16[2,512,2048]{2,1,0:T(8,128)(2,1)}, bf16[2,512,2048]{2,1,0:T(8,128)(2,1)S(1)}, u32[]{:S(2)}) copy-start(bf16[2,512,2048]{2,1,0:T(8,128)(2,1)S(1)} %turn_step.1.b_hbm) | copy-start | bytes 12582916

commit v4 on v3

v4 whole, which is shorter than its diff:
```python
import functools

import jax
import jax.numpy as jnp
from jax import lax
from jax.experimental import pallas as pl
from jax.experimental.pallas import tpu as pltpu
from jax.sharding import Mesh
from jax.sharding import PartitionSpec as P

PLANE = ("xh", "y", "xl", "core")
CUTS = ("xh", "y")
MODE = ("z", "xl", "core")
ROWS = ("xh", "xl")
NT = (((1,), (1,)), ((), ()))
NN = (((1,), (0,)), ((), ()))
RING = 4
DEPTH = 8
ANY = pl.BlockSpec(memory_space=pl.ANY)
VMEM = pl.BlockSpec(memory_space=pltpu.VMEM)
SMEM = pl.BlockSpec(memory_space=pltpu.SMEM)


def first_kernel(lh, stem_hbm, branch_hbm, out_hbm, stem, branch, lhs, out, in_sem, branch_sem, out_sem):
    slices = stem.shape[1]
    stem_copies, branch_copies, sends = [], [], []
    for s in range(slices):
        branch_copies.append(pltpu.make_async_copy(branch_hbm.at[:, s], branch.at[:, s], branch_sem.at[s]))
        stem_copies.append(pltpu.make_async_copy(stem_hbm.at[:, s], stem.at[:, s], in_sem.at[s]))
        branch_copies[s].start()
        stem_copies[s].start()
    row = lax.broadcasted_iota(jnp.int32, (128, 256), 0)
    col = lax.broadcasted_iota(jnp.int32, (128, 256), 1)
    regroup = (col == (row % 16) * 16 + row // 16 * 2 + lh).astype(jnp.bfloat16)
    for s in range(slices):
        branch_copies[s].wait()
        br = [
            lax.dot_general(regroup, branch[r, s], NT, preferred_element_type=jnp.float32).astype(jnp.bfloat16)
            for r in range(2)
        ]
        lhs[s, 0:128, 0:256] = br[0]
        lhs[s, 0:128, 256:512] = -br[1]
        lhs[s, 128:256, 0:256] = br[1]
        lhs[s, 128:256, 256:512] = br[0]
        stem_copies[s].wait()
        for w in range(4):
            rhs = jnp.concatenate([stem[r, s, :, w].reshape(256, 256) for r in range(2)], axis=1)
            res = lax.dot_general(lhs[s], rhs, NT, preferred_element_type=jnp.float32).astype(jnp.bfloat16)
            for r in range(2):
                out[:, w, r, s] = res[r * 128 : (r + 1) * 128].reshape(8, 16, 256)
        sends.append(pltpu.make_async_copy(out.at[:, :, :, s], out_hbm.at[:, :, :, s], out_sem.at[s]))
        sends[s].start()
    for send in sends:
        send.wait()


def first_step(stem, branch, lh, flops):
    slices = stem.shape[1]
    shape = (8, 4, 2, slices, 16, 256)
    return pl.pallas_call(
        functools.partial(first_kernel, lh),
        in_specs=[ANY] * 2,
        out_specs=ANY,
        out_shape=jax.ShapeDtypeStruct(shape, jnp.bfloat16),
        scratch_shapes=[
            pltpu.VMEM(stem.shape, jnp.bfloat16),
            pltpu.VMEM(branch.shape, jnp.bfloat16),
            pltpu.VMEM((slices, 256, 512), jnp.bfloat16),
            pltpu.VMEM(shape, jnp.bfloat16),
            pltpu.SemaphoreType.DMA((slices,)),
            pltpu.SemaphoreType.DMA((slices,)),
            pltpu.SemaphoreType.DMA((slices,)),
        ],
        compiler_params=pltpu.CompilerParams(vmem_limit_bytes=56 << 20),
        cost_estimate=pl.CostEstimate(flops=flops, bytes_accessed=7 << 20, transcendentals=0),
        name="first_step",
    )(stem, branch)


def turn_kernel(me_ref, own_ref, other_ref, out_ref):
    first_core = me_ref[2] == 0
    for dx in range(RING):
        x = me_ref[0] ^ dx
        for dy in range(RING):
            y = me_ref[1] ^ dy
            at = pl.multiple_of((((x // 2) * RING + y) * 2 + x % 2) * 128, 128)
            for r in range(2):
                low = jnp.where(first_core, own_ref[dx, dy, r], other_ref[dx, dy, r])
                high = jnp.where(first_core, other_ref[dy, dx, r], own_ref[dy, dx, r])
                out_ref[r, :, pl.ds(at, 128)] = jnp.concatenate([low, high], axis=0).T


def turn_step(me, own, other):
    return pl.pallas_call(
        turn_kernel,
        in_specs=[SMEM, VMEM, VMEM],
        out_specs=VMEM,
        out_shape=jax.ShapeDtypeStruct((2, 512, 2048), jnp.bfloat16),
        compiler_params=pltpu.CompilerParams(vmem_limit_bytes=32 << 20),
        cost_estimate=pl.CostEstimate(flops=4000000000, bytes_accessed=8 << 20, transcendentals=0),
        name="turn_step",
    )(me, own, other)


def second_kernel(split, me_ref, x_hbm, b_hbm, *refs):
    x, b, out, x_sem, b_sem, out_sem = refs[-6:]
    out_hbm = refs[:-6]
    copies = [pltpu.make_async_copy(x_hbm, x, x_sem), pltpu.make_async_copy(b_hbm, b, b_sem)]
    for copy in copies:
        copy.start()

    def dot(left, right):
        return lax.dot_general(left, right, NN, preferred_element_type=jnp.float32)

    for copy in copies:
        copy.wait()
    xr, xi = (x[:, r].reshape(2048, 256) for r in range(2))
    for t in range(4):
        rows = slice(t * 128, (t + 1) * 128)
        br, bi = b[0, rows], b[1, rows]
        res = [dot(br, xr) + dot(-bi, xi), dot(bi, xr) + dot(br, xi)]
        res = [part.astype(jnp.bfloat16) for part in res]
        for q in range(2):
            parts = [res[r][q * 64 + jh * 32 : q * 64 + (jh + 1) * 32] for jh in range(2) for r in range(2)]
            for za in range(DEPTH):
                out[za, t * 2 + q] = jnp.concatenate([part[:, za * 32 : (za + 1) * 32] for part in parts], axis=1)
    sends = []
    for d in range(DEPTH):
        if split:
            sends.append(pltpu.make_async_copy(out.at[me_ref[3] ^ d], out_hbm[d], out_sem.at[d]))
        else:
            sends.append(pltpu.make_async_copy(out.at[d], out_hbm[0].at[d], out_sem.at[d]))
        sends[d].start()
    for send in sends:
        send.wait()


def second_step(me, x, b2, split):
    shape = (DEPTH, 8, 32, 128)
    if split:
        out_shape = [jax.ShapeDtypeStruct(shape[1:], jnp.bfloat16)] * DEPTH
    else:
        out_shape = [jax.ShapeDtypeStruct(shape, jnp.bfloat16)]
    return pl.pallas_call(
        functools.partial(second_kernel, split),
        in_specs=[SMEM, ANY, ANY],
        out_specs=[ANY] * len(out_shape),
        out_shape=out_shape,
        scratch_shapes=[
            pltpu.VMEM((32, 2, 64, 256), jnp.bfloat16),
            pltpu.VMEM((2, 512, 2048), jnp.bfloat16),
            pltpu.VMEM(shape, jnp.bfloat16),
            pltpu.SemaphoreType.DMA,
            pltpu.SemaphoreType.DMA,
            pltpu.SemaphoreType.DMA((DEPTH,)),
        ],
        compiler_params=pltpu.CompilerParams(vmem_limit_bytes=60 << 20),
        cost_estimate=pl.CostEstimate(flops=2150000000, bytes_accessed=7 << 20, transcendentals=0),
        name="second_step",
    )(me, x, b2)


def total_kernel(me_ref, *refs):
    blocks, outs, sums = refs[:DEPTH], refs[DEPTH:-1], refs[-1]
    acc = blocks[0][...].astype(jnp.float32)
    for block in blocks[1:]:
        acc = acc + block[...].astype(jnp.float32)
    sums[...] = acc
    for dy in range(RING):
        for dx in range(2):
            outs[dy][dx] = sums[(me_ref[0] // 2 ^ dx) * RING + (me_ref[1] ^ dy)]


def total_step(me, blocks):
    return pl.pallas_call(
        total_kernel,
        in_specs=[SMEM] + [VMEM] * DEPTH,
        out_specs=[VMEM] * RING,
        out_shape=[jax.ShapeDtypeStruct((2, 32, 128), jnp.float32)] * RING,
        scratch_shapes=[pltpu.VMEM((8, 32, 128), jnp.float32)],
        compiler_params=pltpu.CompilerParams(vmem_limit_bytes=16 << 20),
        cost_estimate=pl.CostEstimate(flops=10000000000, bytes_accessed=1 << 20, transcendentals=0),
        name="total_step",
    )(me, *blocks)


def pick_kernel(*refs):
    for n, ref in enumerate(refs[:-1]):
        refs[-1][n] = ref[1]


def pick_step(sums):
    return pl.pallas_call(
        pick_kernel,
        in_specs=[VMEM] * RING,
        out_specs=VMEM,
        out_shape=jax.ShapeDtypeStruct((RING, 32, 128), jnp.float32),
        compiler_params=pltpu.CompilerParams(vmem_limit_bytes=16 << 20),
        cost_estimate=pl.CostEstimate(flops=1000000, bytes_accessed=1 << 17, transcendentals=0),
        name="pick_step",
    )(*sums)


def lay_kernel(me_ref, later_ref, across_ref, *refs):
    out_ref, held = refs[-2:]
    xh = me_ref[0] // 2
    for dy in range(RING):
        held[xh * RING + (me_ref[1] ^ dy)] = refs[dy][0]
        held[(1 - xh) * RING + (me_ref[1] ^ dy)] = across_ref[dy]
    sums = []
    for i in range(8):
        acc = later_ref[0, i].astype(jnp.float32)
        for z in range(1, DEPTH):
            acc = acc + later_ref[z, i].astype(jnp.float32)
        sums.append((held[i], acc))
    for r in range(2):
        for jh in range(2):
            at = jh * 64 + r * 32
            out_ref[r, jh * 32 : (jh + 1) * 32, 0] = jnp.concatenate(
                [half[:, at : at + 32] for pair in sums for half in pair], axis=1
            )


def lay_step(me, later, across, sums):
    return pl.pallas_call(
        lay_kernel,
        in_specs=[SMEM] + [VMEM] * (2 + RING),
        out_specs=VMEM,
        out_shape=jax.ShapeDtypeStruct((2, 64, 1, 512), jnp.float32),
        scratch_shapes=[pltpu.VMEM((8, 32, 128), jnp.float32)],
        compiler_params=pltpu.CompilerParams(vmem_limit_bytes=16 << 20),
        cost_estimate=pl.CostEstimate(flops=1000000, bytes_accessed=1 << 20, transcendentals=0),
        name="lay_step",
    )(me, later, across, *sums)


def place(x, y, core):
    return ((x // 2 * RING + y) * 2 + x % 2) * 2 + core


def ring_blocks(block, stage):
    blocks = [block]
    for d in range(1, RING):
        pairs = []
        for x in range(RING):
            for y in range(RING):
                for core in range(2):
                    along_y = core == stage
                    source = place(x, y ^ d, core) if along_y else place(x ^ d, y, core)
                    pairs.append((source, place(x, y, core)))
        blocks.append(lax.ppermute(block, PLANE, pairs))
    return blocks


def pack_kernel(*refs):
    rows = refs[0].shape[0]
    for n, ref in enumerate(refs[:-1]):
        refs[-1][n * rows : (n + 1) * rows] = ref[...]


def pack(blocks):
    return pl.pallas_call(
        pack_kernel,
        in_specs=[VMEM] * len(blocks),
        out_specs=VMEM,
        out_shape=jax.ShapeDtypeStruct((len(blocks) * blocks[0].shape[0], *blocks[0].shape[1:]), blocks[0].dtype),
        compiler_params=pltpu.CompilerParams(vmem_limit_bytes=24 << 20),
        cost_estimate=pl.CostEstimate(flops=1000000, bytes_accessed=1 << 20, transcendentals=0),
        name="pack",
    )(*blocks)


def exchange(block, axes):
    return lax.all_to_all(block, axes, split_axis=0, concat_axis=0, tiled=True)


def shards(stem_tensor, branch_first, branch_second):
    slices = stem_tensor.shape[1]
    me = [lax.axis_index(axis) for axis in (ROWS, "y", "core", "z")]
    me = jnp.stack(me).astype(jnp.int32)
    stem = stem_tensor.reshape(2, slices, 8, 4, 32, 256)
    near = ring_blocks(branch_second.reshape(1, 2, slices * 16, 512), 0)
    sent = first_step(stem, branch_first, 0, 1200000000)
    sent, near, stem = lax.optimization_barrier((sent, near, stem))
    own = pack(ring_blocks(pack(near), 1))
    arrived = exchange(sent.reshape(32, 2 * slices * 16, 256), PLANE)
    later = first_step(stem, branch_first, 1, 20000000000)
    arrived, later = lax.optimization_barrier((arrived, later))
    other = lax.ppermute(own, "core", [(0, 1), (1, 0)])
    blocks = (RING, RING, 2, slices * 16, 512)
    turned = turn_step(me, own.reshape(blocks), other.reshape(blocks))
    later = exchange(later.reshape(32, 2 * slices * 16, 256), PLANE)
    half = list(second_step(me, arrived.reshape(32, 2, slices * 16, 256), turned, True))
    for d in range(1, DEPTH):
        half[d] = lax.ppermute(half[d], "z", [(z, z ^ d) for z in range(DEPTH)])
    early = (0, 1, 2, 3)
    later, *done = lax.optimization_barrier((later, *[half[d] for d in early]))
    for d, block in zip(early, done):
        half[d] = block
    (rest,) = second_step(me, later.reshape(32, 2, slices * 16, 256), turned, False)
    rest = exchange(rest.reshape(64, 32, 128), ("z",) + CUTS)
    sums = list(total_step(me, half))
    for dy in range(1, RING):
        sums[dy] = lax.ppermute(sums[dy], "y", [(y, y ^ dy) for y in range(RING)])
    across = lax.ppermute(pick_step(sums), "xh", [(0, 1), (1, 0)])
    return lay_step(me, rest.reshape(DEPTH, 8, 32, 128), across, sums)


def solution(mesh):
    fine = Mesh(mesh.devices.reshape(2, RING, DEPTH, 2, 2), ("xh", "y", "z", "xl", "core"))
    in_specs = (
        P(None, CUTS, MODE, None, None, None),
        P(None, CUTS, None, None),
        P(None, CUTS, MODE, None),
    )
    return jax.shard_map(
        shards, mesh=fine, in_specs=in_specs, out_specs=P(None, CUTS, MODE, None), check_vma=False
    )
```

time: 132 us -> 126 us (0.955)
  blocking collectives: 43.4 us -> 0 us
  starting transfers between devices: 17.1 us -> 57.1 us
  waiting for transfers between devices: 45.2 us -> 34 us
  Pallas kernels: 19.3 us -> 28.8 us
    all_to_all x1 -> x0, blocking collectives: 43.4 us -> none  [shards(): lax.all_to_all(partial.reshape(64, 64, 128), OWNERS, split_axis=0, concat...]
    ppermute x0 -> x11, starting transfers between devices: none -> 25.5 us  [the longest x7 18.1 us: shards(): half[d] = lax.ppermute(half[d], 'z', [(z, z ^ d) for z in range(DEPTH)])]
    all_to_all x1 -> x3, waiting for transfers between devices: 36.3 us -> 10.8 us  [exchange(): return lax.all_to_all(block, axes, split_axis=0, concat_axis=0, tiled=True)]
    all_to_all x1 -> x3, starting transfers between devices: 7.75 us -> 21.9 us  [exchange(): return lax.all_to_all(block, axes, split_axis=0, concat_axis=0, tiled=True)]
    ppermute x6, waiting for transfers between devices: 5.02 us -> 16.7 us  [ring_blocks(): blocks.append(lax.ppermute(block, PLANE, pairs))]
    pallas_call x6 -> x10, Pallas kernels: 19.3 us -> 28.8 us  [the longest x2 13.8 us: second_step(): pl.pallas_call(functools.partial(second_kernel, split), in_specs=[SMEM, A...]
    ppermute x0 -> x11, waiting for transfers between devices: none -> 6.42 us  [the longest x1 3.47 us: shards(): across = lax.ppermute(pick_step(sums), 'xh', [(0, 1), (1, 0)])]
    ppermute x1, waiting for transfers between devices: 3.84 us -> 0.01 us  [shards(): other = lax.ppermute(own, 'core', [(0, 1), (1, 0)])]
  transfers between devices with their start and end apart: 8 -> 21, of which waited for: 5 -> 8; matrix products, arithmetic and copies ran while one was open for 0% -> 0% of each run, Pallas kernels for 7% -> 22%
where the time goes in v4:
time: 126 us
  starting transfers between devices  57.1 us (45%)
  waiting for transfers between devices  34 us (27%)
  Pallas kernels  28.8 us (23%)
  local copies, waits for them, and re-layouts  5.64 us (4%)
    all_to_all x3, starting transfers between devices, exchange(): return lax.all_to_all(block, axes, split_axis=0, concat_axis=0, tiled=True)  21.9 us
    ppermute x7, starting transfers between devices, shards(): half[d] = lax.ppermute(half[d], 'z', [(z, z ^ d) for z in range(DEPTH)])  18.1 us
    ppermute x6, waiting for transfers between devices, ring_blocks(): blocks.append(lax.ppermute(block, PLANE, pairs))  16.7 us
    pallas_call x2, Pallas kernels, second_step(): pl.pallas_call(functools.partial(second_kernel, split), in_specs=[SMEM, A...  13.8 us
    all_to_all x3, waiting for transfers between devices, exchange(): return lax.all_to_all(block, axes, split_axis=0, concat_axis=0, tiled=True)  10.8 us
    pallas_call x2, Pallas kernels, first_step(): pl.pallas_call(functools.partial(first_kernel, lh), in_specs=[ANY] * 2, o...  9.7 us
    ppermute x6, starting transfers between devices, ring_blocks(): blocks.append(lax.ppermute(block, PLANE, pairs))  9.48 us
    unnamed x18, local copies, waits for them, and re-layouts  5.64 us
  transfers between devices with their start and end apart: 21, of which 8 were waited for; matrix products, arithmetic and copies ran while one was open for 0% of the time, Pallas kernels for 22%

profile of v4, /device:TPU:24, one launch (start us, length us, event | category | flops | bytes accessed | tf_op | source)
XLA Modules:
  0.0 125.8 jit_solution(1232390567323590363)
XLA Ops:
  0.0 0.7 collective-permute-start
  0.7 2.7 %collective-permute-start.1 = (bf16[1,2,64,512]{3,2,1,0:T(8,128)(2,1)}, bf16[1,2,64,512]{3,2,1,0:T(8,128)(2,1)S(1)}, u32[]{:S(2)}, u32[]{:S(2)}) collective-permute-start(bf16[1,2,64,512]{3,2,1,0:T(8,128)(2,1)} %bitcast.17), channel_id=1, source_target_pairs={{64,0},{129,1},{96,32},{161,33},{0,64},{193,65},{32,96},{225,97},{... | collective-permute-start | bytes 393224 | tf_op jit(solution)/shard_map/ppermute | solution.py:251
  3.4 1.3 %collective-permute-start.2 = (bf16[1,2,64,512]{3,2,1,0:T(8,128)(2,1)}, bf16[1,2,64,512]{3,2,1,0:T(8,128)(2,1)S(1)}, u32[]{:S(2)}, u32[]{:S(2)}) collective-permute-start(bf16[1,2,64,512]{3,2,1,0:T(8,128)(2,1)} %bitcast.18), channel_id=1, source_target_pairs={{96,0},{131,1},{64,32},{163,33},{32,64},{195,65},{0,96},{227,97},{... | collective-permute-start | bytes 393224 | tf_op jit(solution)/shard_map/ppermute | solution.py:251
  4.7 0.0 copy-start.4
  4.7 4.9 %first_step.2 = bf16[8,4,2,4,16,256]{5,4,3,2,1,0:T(8,128)(2,1)} custom-call(bf16[2,4,8,4,32,256]{5,4,3,2,1,0:T(8,128)(2,1)} %bitcast.21, bf16[2,4,256,256]{3,2,1,0:T(8,128)(2,1)} %branch_hbm.3), custom_call_target="tpu_custom_call" | custom-call | flops 1200000000 | bytes 7340032 | tf_op jit(solution)/shard_map/first_step/pallas_call | solution.py:60
  9.6 0.0 collective-permute-done.refs_1_
  9.6 0.0 collective-permute-done.1.refs_2_
  9.6 0.2 collective-permute-done.2.refs_3_
  9.8 0.0 copy-done.4
  9.9 1.4 %collective-permute-start.3 = (bf16[4,2,64,512]{3,2,1,0:T(8,128)(2,1)S(1)}, bf16[4,2,64,512]{3,2,1,0:T(8,128)(2,1)S(1)}, u32[]{:S(2)}, u32[]{:S(2)}) collective-permute-start(bf16[4,2,64,512]{3,2,1,0:T(8,128)(2,1)S(1)} %pack.2.refs_0_), channel_id=1, source_target_pairs={{2,0},{33,1},{34,32},{1,33},{66,64},{97,65},{98,96},{65,97},{0,2},... | collective-permute-start | bytes 1572872 | tf_op jit(solution)/shard_map/ppermute | solution.py:251
  11.2 2.7 %collective-permute-start.4 = (bf16[4,2,64,512]{3,2,1,0:T(8,128)(2,1)S(1)}, bf16[4,2,64,512]{3,2,1,0:T(8,128)(2,1)S(1)}, u32[]{:S(2)}, u32[]{:S(2)}) collective-permute-start(bf16[4,2,64,512]{3,2,1,0:T(8,128)(2,1)S(1)} %pack.2.refs_0_), channel_id=1, source_target_pairs={{128,0},{65,1},{160,32},{97,33},{192,64},{1,65},{224,96},{33,97},{... | collective-permute-start | bytes 1572872 | tf_op jit(solution)/shard_map/ppermute | solution.py:251
  14.0 0.7 collective-permute-start.5
  14.6 6.7 %all-to-all-start = ((bf16[32,128,256]{2,1,0:T(8,128)(2,1)}), bf16[32,128,256]{2,1,0:T(8,128)(2,1)}, u32[]{:S(2)}, u32[]{:S(2)}) async-start(bf16[32,128,256]{2,1,0:T(8,128)(2,1)} %bitcast.20), calls=%async_computation | async-start | bytes 4194304 | tf_op jit(solution)/shard_map/all_to_all | solution.py:274
  21.4 0.0 collective-permute-done.3.refs_1_
  21.4 6.7 %collective-permute-done.4.refs_2_ = bf16[4,2,64,512]{3,2,1,0:T(8,128)(2,1)S(1)} collective-permute-done((bf16[4,2,64,512]{3,2,1,0:T(8,128)(2,1)S(1)}, bf16[4,2,64,512]{3,2,1,0:T(8,128)(2,1)S(1)}, u32[]{:S(2)}, u32[]{:S(2)}) %collective-permute-start.4) | collective-permute-done | bytes 524320 | tf_op jit(solution)/shard_map/ppermute | solution.py:251
  28.0 0.0 copy-start
  28.0 0.8 copy-done
  28.8 9.8 %collective-permute-done.5.refs_3_ = bf16[4,2,64,512]{3,2,1,0:T(8,128)(2,1)S(1)} collective-permute-done((bf16[4,2,64,512]{3,2,1,0:T(8,128)(2,1)S(1)}, bf16[4,2,64,512]{3,2,1,0:T(8,128)(2,1)S(1)}, u32[]{:S(2)}, u32[]{:S(2)}) %collective-permute-start.5) | collective-permute-done | bytes 524320 | tf_op jit(solution)/shard_map/ppermute | solution.py:251
  38.7 0.8 copy-done.2
  39.5 1.0 copy-done.1
  40.5 1.0 copy-done.3
  41.5 0.1 pack.3
  41.7 0.1 collective-permute-start.6
  41.8 4.8 %first_step.3 = bf16[8,4,2,4,16,256]{5,4,3,2,1,0:T(8,128)(2,1)} custom-call(bf16[2,4,8,4,32,256]{5,4,3,2,1,0:T(8,128)(2,1)} %bitcast.22, bf16[2,4,256,256]{3,2,1,0:T(8,128)(2,1)} %branch_hbm.3), custom_call_target="tpu_custom_call" | custom-call | flops 20000000000 | bytes 7340032 | tf_op jit(solution)/shard_map/first_step/pallas_call | solution.py:60
  46.6 6.8 %all-to-all-done = bf16[32,128,256]{2,1,0:T(8,128)(2,1)} async-done(((bf16[32,128,256]{2,1,0:T(8,128)(2,1)}), bf16[32,128,256]{2,1,0:T(8,128)(2,1)}, u32[]{:S(2)}, u32[]{:S(2)}) %all-to-all-start) | async-done | bytes 2097184 | tf_op jit(solution)/shard_map/all_to_all | solution.py:274
  53.5 5.4 %all-to-all-start.1 = ((bf16[32,128,256]{2,1,0:T(8,128)(2,1)}), bf16[32,128,256]{2,1,0:T(8,128)(2,1)}, u32[]{:S(2)}, u32[]{:S(2)}) async-start(bf16[32,128,256]{2,1,0:T(8,128)(2,1)} %bitcast.23), calls=%async_computation.1 | async-start | bytes 4194304 | tf_op jit(solution)/shard_map/all_to_all | solution.py:274
  58.9 0.1 pad_add_fusion.me_ref
  59.0 0.0 collective-permute-done.6
  59.0 2.9 %turn_step.1.b_hbm = bf16[2,512,2048]{2,1,0:T(8,128)(2,1)S(1)} custom-call(s32[4]{0:T(128)S(1)} %pad_add_fusion.me_ref, bf16[4,4,2,64,512]{4,3,2,1,0:T(8,128)(2,1)S(1)} %bitcast.15, bf16[4,4,2,64,512]{4,3,2,1,0:T(8,128)(2,1)} %bitcast.10.other_ref), custom_call_target="tpu_custom_call" | custom-call | flops 4000000000 | bytes 8388608 | tf_op jit(solution)/shard_map/turn_step/pallas_call | solution.py:94
  61.9 0.0 copy-done.5
  61.9 0.0 copy-start.7
  61.9 1.9 %copy-done.7 = bf16[2,512,2048]{2,1,0:T(8,128)(2,1)} copy-done((bf16[2,512,2048]{2,1,0:T(8,128)(2,1)}, bf16[2,512,2048]{2,1,0:T(8,128)(2,1)S(1)}, u32[]{:S(2)}) %copy-start.7) | copy-done | bytes 4194328
  63.9 6.8 %second_step.2 = (bf16[8,32,128]{2,1,0:T(8,128)(2,1)}, bf16[8,32,128]{2,1,0:T(8,128)(2,1)}, bf16[8,32,128]{2,1,0:T(8,128)(2,1)}, bf16[8,32,128]{2,1,0:T(8,128)(2...) custom-call(s32[4]{0:T(128)} %copy-done.5, ...), custom_call_target="tpu_custom_call" | custom-call | flops 2150000128 | bytes 7340032 | tf_op jit(solution)/shard_map/second_step/pallas_call | solution.py:144
  70.7 1.8 %collective-permute-start.7 = (bf16[8,32,128]{2,1,0:T(8,128)(2,1)}, bf16[8,32,128]{2,1,0:T(8,128)(2,1)S(1)}, u32[]{:S(2)}, u32[]{:S(2)}) collective-permute-start(bf16[8,32,128]{2,1,0:T(8,128)(2,1)} %get-tuple-element.39), channel_id=1, source_target_pairs={{0,4},{4,0},{8,12},{12,8},{16,20},{20,16},{24,28},{28,24},{1,5},{5... | collective-permute-start | bytes 196616 | tf_op jit(solution)/shard_map/ppermute | solution.py:295
  72.5 3.3 %collective-permute-start.8 = (bf16[8,32,128]{2,1,0:T(8,128)(2,1)}, bf16[8,32,128]{2,1,0:T(8,128)(2,1)S(1)}, u32[]{:S(2)}, u32[]{:S(2)}) collective-permute-start(bf16[8,32,128]{2,1,0:T(8,128)(2,1)} %get-tuple-element.40), channel_id=1, source_target_pairs={{0,8},{4,12},{8,0},{12,4},{16,24},{20,28},{24,16},{28,20},{1,9},{5... | collective-permute-start | bytes 196616 | tf_op jit(solution)/shard_map/ppermute | solution.py:295
  75.8 0.0 collective-permute-start.9
  75.8 6.4 %collective-permute-start.10 = (bf16[8,32,128]{2,1,0:T(8,128)(2,1)}, bf16[8,32,128]{2,1,0:T(8,128)(2,1)S(1)}, u32[]{:S(2)}, u32[]{:S(2)}) collective-permute-start(bf16[8,32,128]{2,1,0:T(8,128)(2,1)} %get-tuple-element.47), channel_id=1, source_target_pairs={{0,16},{4,20},{8,24},{12,28},{16,0},{20,4},{24,8},{28,12},{1,17},{... | collective-permute-start | bytes 196616 | tf_op jit(solution)/shard_map/ppermute | solution.py:295
  82.2 0.0 collective-permute-start.11
  82.2 0.0 collective-permute-done.7.refs_1_
  82.2 4.6 %collective-permute-start.12 = (bf16[8,32,128]{2,1,0:T(8,128)(2,1)}, bf16[8,32,128]{2,1,0:T(8,128)(2,1)S(1)}, u32[]{:S(2)}, u32[]{:S(2)}) collective-permute-start(bf16[8,32,128]{2,1,0:T(8,128)(2,1)} %get-tuple-element.49), channel_id=1, source_target_pairs={{0,24},{4,28},{8,16},{12,20},{16,8},{20,12},{24,0},{28,4},{1,25},{... | collective-permute-start | bytes 196616 | tf_op jit(solution)/shard_map/ppermute | solution.py:295
  86.8 0.0 collective-permute-done.8.refs_2_
  86.8 2.1 %collective-permute-start.13 = (bf16[8,32,128]{2,1,0:T(8,128)(2,1)}, bf16[8,32,128]{2,1,0:T(8,128)(2,1)S(1)}, u32[]{:S(2)}, u32[]{:S(2)}) collective-permute-start(bf16[8,32,128]{2,1,0:T(8,128)(2,1)} %get-tuple-element.50), channel_id=1, source_target_pairs={{0,28},{4,24},{8,20},{12,16},{16,12},{20,8},{24,4},{28,0},{1,29},{... | collective-permute-start | bytes 196616 | tf_op jit(solution)/shard_map/ppermute | solution.py:295
  88.9 0.0 collective-permute-done.9.refs_3_
  88.9 0.0 all-to-all-done.1
  88.9 0.0 copy-start.8
  88.9 7.0 %second_step.3 = bf16[8,8,32,128]{3,2,1,0:T(8,128)(2,1)} custom-call(s32[4]{0:T(128)} %copy-done.5, bf16[32,2,64,256]{3,2,1,0:T(8,128)(2,1)} %bitcast.11.x_hbm, bf16[2,512,2048]{2,1,0:T(8,128)(2,1)} %copy-done.7), custom_call_target="tpu_custom_call" | custom-call | flops 2150000128 | bytes 7340032 | tf_op jit(solution)/shard_map/second_step/pallas_call | solution.py:144
  95.9 9.8 %all-to-all-start.2 = ((bf16[64,32,128]{2,1,0:T(8,128)(2,1)}), bf16[64,32,128]{2,1,0:T(8,128)(2,1)S(1)}, u32[]{:S(2)}, u32[]{:S(2)}) async-start(bf16[64,32,128]{2,1,0:T(8,128)(2,1)} %bitcast.24), calls=%async_computation.2 | async-start | bytes 1048576 | tf_op jit(solution)/shard_map/all_to_all | solution.py:274
  105.7 0.0 collective-permute-done.10.refs_4_
  105.7 0.0 collective-permute-done.11.refs_5_
  105.7 0.0 collective-permute-done.12.refs_6_
  105.8 0.0 collective-permute-done.13.refs_7_
  105.8 0.0 copy-done.6
  105.8 0.0 copy-done.8
  105.8 0.6 total_step.1
  106.4 0.9 collective-permute-start.14
  107.4 1.1 collective-permute-start.15
  108.4 2.8 %collective-permute-start.16 = (f32[2,32,128]{2,1,0:T(8,128)S(1)}, f32[2,32,128]{2,1,0:T(8,128)S(1)}, u32[]{:S(2)}, u32[]{:S(2)}) collective-permute-start(f32[2,32,128]{2,1,0:T(8,128)S(1)} %get-tuple-element.54), channel_id=1, source_target_pairs={{0,96},{32,64},{64,32},{96,0},{1,97},{33,65},{65,33},{97,1},{2,98}... | collective-permute-start | bytes 98312 | tf_op jit(solution)/shard_map/ppermute | solution.py:304
  111.2 0.0 collective-permute-done.14.refs_1_
  111.2 2.1 %collective-permute-done.15.refs_2_ = f32[2,32,128]{2,1,0:T(8,128)S(1)} collective-permute-done((f32[2,32,128]{2,1,0:T(8,128)S(1)}, f32[2,32,128]{2,1,0:T(8,128)S(1)}, u32[]{:S(2)}, u32[]{:S(2)}) %collective-permute-start.15) | collective-permute-done | bytes 32800 | tf_op jit(solution)/shard_map/ppermute | solution.py:304
  113.3 0.9 collective-permute-done.16.refs_3_
  114.2 2.6 %collective-permute-start.17 = (f32[4,32,128]{2,1,0:T(8,128)S(1)}, f32[4,32,128]{2,1,0:T(8,128)S(1)}, u32[]{:S(2)}, u32[]{:S(2)}) collective-permute-start(f32[4,32,128]{2,1,0:T(8,128)S(1)} %pick_step.1), channel_id=1, source_target_pairs={{0,128},{128,0},{1,129},{129,1},{2,130},{130,2},{3,131},{131,3},{4... | collective-permute-start | bytes 196616 | tf_op jit(solution)/shard_map/ppermute | solution.py:305
  116.8 3.5 %collective-permute-done.17.across_ref = f32[4,32,128]{2,1,0:T(8,128)S(1)} collective-permute-done((f32[4,32,128]{2,1,0:T(8,128)S(1)}, f32[4,32,128]{2,1,0:T(8,128)S(1)}, u32[]{:S(2)}, u32[]{:S(2)}) %collective-permute-start.17) | collective-permute-done | bytes 65568 | tf_op jit(solution)/shard_map/ppermute | solution.py:305
  120.3 4.0 %all-to-all-done.2 = bf16[64,32,128]{2,1,0:T(8,128)(2,1)S(1)} async-done(((bf16[64,32,128]{2,1,0:T(8,128)(2,1)}), bf16[64,32,128]{2,1,0:T(8,128)(2,1)S(1)}, u32[]{:S(2)}, u32[]{:S(2)}) %all-to-all-start.2) | async-done | bytes 524320 | tf_op jit(solution)/shard_map/all_to_all | solution.py:274
  124.3 1.5 %lay_step.1 = f32[2,64,1,512]{3,2,1,0:T(1,128)} custom-call(s32[4]{0:T(128)S(1)} %copy-done.6, bf16[8,8,32,128]{3,2,1,0:T(8,128)(2,1)S(1)} %bitcast.14, f32[4,32,128]{2,1,0:T(8,128)S(1)} %collective-permute-done.17.across_ref, f32[2,32,128]{2,1,0:T(8,128)S(1)} %get-tuple-element.51.refs_0_, f32[2,32,128]{2,1,0:T(8,128)S(1)} %collective-permute-done.14.refs_1_, ...), custom_call_target="tpu_custom_call" | custom-call | flops 1000000 | bytes 1048576 | tf_op jit(solution)/shard_map/lay_step/pallas_call | solution.py:225
  (7 shorter events, 0.0 us)
Async XLA Ops:
  0.0 9.6 %collective-permute-start = (bf16[1,2,64,512]{3,2,1,0:T(8,128)(2,1)}, bf16[1,2,64,512]{3,2,1,0:T(8,128)(2,1)S(1)}, u32[]{:S(2)}, u32[]{:S(2)}) collective-permute-start(bf16[1,2,64,512]{3,2,1,0:T(8,128)(2,1)} %bitcast.16), channel_id=1, source_target_pairs={{32,0},{3,1},{0,32},{35,33},{96,64},{67,65},{64,96},{99,97},{34,2}... | collective-permute-start | bytes 393224 | tf_op jit(solution)/shard_map/ppermute | solution.py:251
  0.7 8.8 %collective-permute-start.1 = (bf16[1,2,64,512]{3,2,1,0:T(8,128)(2,1)}, bf16[1,2,64,512]{3,2,1,0:T(8,128)(2,1)S(1)}, u32[]{:S(2)}, u32[]{:S(2)}) collective-permute-start(bf16[1,2,64,512]{3,2,1,0:T(8,128)(2,1)} %bitcast.17), channel_id=1, source_target_pairs={{64,0},{129,1},{96,32},{161,33},{0,64},{193,65},{32,96},{225,97},{... | collective-permute-start | bytes 393224 | tf_op jit(solution)/shard_map/ppermute | solution.py:251
  3.4 6.4 %collective-permute-start.2 = (bf16[1,2,64,512]{3,2,1,0:T(8,128)(2,1)}, bf16[1,2,64,512]{3,2,1,0:T(8,128)(2,1)S(1)}, u32[]{:S(2)}, u32[]{:S(2)}) collective-permute-start(bf16[1,2,64,512]{3,2,1,0:T(8,128)(2,1)} %bitcast.18), channel_id=1, source_target_pairs={{96,0},{131,1},{64,32},{163,33},{32,64},{195,65},{0,96},{227,97},{... | collective-permute-start | bytes 393224 | tf_op jit(solution)/shard_map/ppermute | solution.py:251
  4.7 5.1 %copy-start.4 = (bf16[2,4,16,512]{3,2,1,0:T(8,128)(2,1)S(1)}, bf16[2,4,16,512]{3,2,1,0:T(8,128)(2,1)}, u32[]{:S(2)}) copy-start(bf16[2,4,16,512]{3,2,1,0:T(8,128)(2,1)} %param.5) | copy-start | bytes 393220
  9.9 11.5 %collective-permute-start.3 = (bf16[4,2,64,512]{3,2,1,0:T(8,128)(2,1)S(1)}, bf16[4,2,64,512]{3,2,1,0:T(8,128)(2,1)S(1)}, u32[]{:S(2)}, u32[]{:S(2)}) collective-permute-start(bf16[4,2,64,512]{3,2,1,0:T(8,128)(2,1)S(1)} %pack.2.refs_0_), channel_id=1, source_target_pairs={{2,0},{33,1},{34,32},{1,33},{66,64},{97,65},{98,96},{65,97},{0,2},... | collective-permute-start | bytes 1572872 | tf_op jit(solution)/shard_map/ppermute | solution.py:251
  11.2 16.8 %collective-permute-start.4 = (bf16[4,2,64,512]{3,2,1,0:T(8,128)(2,1)S(1)}, bf16[4,2,64,512]{3,2,1,0:T(8,128)(2,1)S(1)}, u32[]{:S(2)}, u32[]{:S(2)}) collective-permute-start(bf16[4,2,64,512]{3,2,1,0:T(8,128)(2,1)S(1)} %pack.2.refs_0_), channel_id=1, source_target_pairs={{128,0},{65,1},{160,32},{97,33},{192,64},{1,65},{224,96},{33,97},{... | collective-permute-start | bytes 1572872 | tf_op jit(solution)/shard_map/ppermute | solution.py:251
  14.0 24.7 %collective-permute-start.5 = (bf16[4,2,64,512]{3,2,1,0:T(8,128)(2,1)S(1)}, bf16[4,2,64,512]{3,2,1,0:T(8,128)(2,1)S(1)}, u32[]{:S(2)}, u32[]{:S(2)}) collective-permute-start(bf16[4,2,64,512]{3,2,1,0:T(8,128)(2,1)S(1)} %pack.2.refs_0_), channel_id=1, source_target_pairs={{130,0},{97,1},{162,32},{65,33},{194,64},{33,65},{226,96},{1,97},{... | collective-permute-start | bytes 1572872 | tf_op jit(solution)/shard_map/ppermute | solution.py:251
  14.6 38.8 %all-to-all-start = ((bf16[32,128,256]{2,1,0:T(8,128)(2,1)}), bf16[32,128,256]{2,1,0:T(8,128)(2,1)}, u32[]{:S(2)}, u32[]{:S(2)}) async-start(bf16[32,128,256]{2,1,0:T(8,128)(2,1)} %bitcast.20), calls=%async_computation | async-start | bytes 4194304 | tf_op jit(solution)/shard_map/all_to_all | solution.py:274
  28.0 0.8 copy-start
  38.7 0.8 copy-start.2
  39.5 1.0 copy-start.1
  40.5 1.0 copy-start.3
  41.7 17.3 %collective-permute-start.6 = (bf16[16,2,64,512]{3,2,1,0:T(8,128)(2,1)S(1)}, bf16[16,2,64,512]{3,2,1,0:T(8,128)(2,1)}, u32[]{:S(2)}, u32[]{:S(2)}) collective-permute-start(bf16[16,2,64,512]{3,2,1,0:T(8,128)(2,1)S(1)} %pack.3), channel_id=1, source_target_pairs={{0,1},{1,0},{2,3},{3,2},{4,5},{5,4},{6,7},{7,6},{8,9},{9,8},{10,11... | collective-permute-start | bytes 6291464 | tf_op jit(solution)/shard_map/ppermute | solution.py:289
  53.5 35.4 %all-to-all-start.1 = ((bf16[32,128,256]{2,1,0:T(8,128)(2,1)}), bf16[32,128,256]{2,1,0:T(8,128)(2,1)}, u32[]{:S(2)}, u32[]{:S(2)}) async-start(bf16[32,128,256]{2,1,0:T(8,128)(2,1)} %bitcast.23), calls=%async_computation.1 | async-start | bytes 4194304 | tf_op jit(solution)/shard_map/all_to_all | solution.py:274
  59.0 2.9 %copy-start.5 = (s32[4]{0:T(128)}, s32[4]{0:T(128)S(1)}, u32[]{:S(2)}) copy-start(s32[4]{0:T(128)S(1)} %pad_add_fusion.me_ref) | copy-start | bytes 52
  61.9 2.0 %copy-start.7 = (bf16[2,512,2048]{2,1,0:T(8,128)(2,1)}, bf16[2,512,2048]{2,1,0:T(8,128)(2,1)S(1)}, u32[]{:S(2)}) copy-start(bf16[2,512,2048]{2,1,0:T(8,128)(2,1)S(1)} %turn_step.1.b_hbm) | copy-start | bytes 12582916
  70.7 11.4 %collective-permute-start.7 = (bf16[8,32,128]{2,1,0:T(8,128)(2,1)}, bf16[8,32,128]{2,1,0:T(8,128)(2,1)S(1)}, u32[]{:S(2)}, u32[]{:S(2)}) collective-permute-start(bf16[8,32,128]{2,1,0:T(8,128)(2,1)} %get-tuple-element.39), channel_id=1, source_target_pairs={{0,4},{4,0},{8,12},{12,8},{16,20},{20,16},{24,28},{28,24},{1,5},{5... | collective-permute-start | bytes 196616 | tf_op jit(solution)/shard_map/ppermute | solution.py:295
  72.5 14.3 %collective-permute-start.8 = (bf16[8,32,128]{2,1,0:T(8,128)(2,1)}, bf16[8,32,128]{2,1,0:T(8,128)(2,1)S(1)}, u32[]{:S(2)}, u32[]{:S(2)}) collective-permute-start(bf16[8,32,128]{2,1,0:T(8,128)(2,1)} %get-tuple-element.40), channel_id=1, source_target_pairs={{0,8},{4,12},{8,0},{12,4},{16,24},{20,28},{24,16},{28,20},{1,9},{5... | collective-permute-start | bytes 196616 | tf_op jit(solution)/shard_map/ppermute | solution.py:295
  75.8 13.1 %collective-permute-start.9 = (bf16[8,32,128]{2,1,0:T(8,128)(2,1)}, bf16[8,32,128]{2,1,0:T(8,128)(2,1)S(1)}, u32[]{:S(2)}, u32[]{:S(2)}) collective-permute-start(bf16[8,32,128]{2,1,0:T(8,128)(2,1)} %get-tuple-element.41), channel_id=1, source_target_pairs={{0,12},{4,8},{8,4},{12,0},{16,28},{20,24},{24,20},{28,16},{1,13},{... | collective-permute-start | bytes 196616 | tf_op jit(solution)/shard_map/ppermute | solution.py:295
  75.8 30.0 %collective-permute-start.10 = (bf16[8,32,128]{2,1,0:T(8,128)(2,1)}, bf16[8,32,128]{2,1,0:T(8,128)(2,1)S(1)}, u32[]{:S(2)}, u32[]{:S(2)}) collective-permute-start(bf16[8,32,128]{2,1,0:T(8,128)(2,1)} %get-tuple-element.47), channel_id=1, source_target_pairs={{0,16},{4,20},{8,24},{12,28},{16,0},{20,4},{24,8},{28,12},{1,17},{... | collective-permute-start | bytes 196616 | tf_op jit(solution)/shard_map/ppermute | solution.py:295
  82.2 23.6 %collective-permute-start.11 = (bf16[8,32,128]{2,1,0:T(8,128)(2,1)}, bf16[8,32,128]{2,1,0:T(8,128)(2,1)S(1)}, u32[]{:S(2)}, u32[]{:S(2)}) collective-permute-start(bf16[8,32,128]{2,1,0:T(8,128)(2,1)} %get-tuple-element.48), channel_id=1, source_target_pairs={{0,20},{4,16},{8,28},{12,24},{16,4},{20,0},{24,12},{28,8},{1,21},{... | collective-permute-start | bytes 196616 | tf_op jit(solution)/shard_map/ppermute | solution.py:295
  82.2 23.6 %collective-permute-start.12 = (bf16[8,32,128]{2,1,0:T(8,128)(2,1)}, bf16[8,32,128]{2,1,0:T(8,128)(2,1)S(1)}, u32[]{:S(2)}, u32[]{:S(2)}) collective-permute-start(bf16[8,32,128]{2,1,0:T(8,128)(2,1)} %get-tuple-element.49), channel_id=1, source_target_pairs={{0,24},{4,28},{8,16},{12,20},{16,8},{20,12},{24,0},{28,4},{1,25},{... | collective-permute-start | bytes 196616 | tf_op jit(solution)/shard_map/ppermute | solution.py:295
  86.8 19.0 %collective-permute-start.13 = (bf16[8,32,128]{2,1,0:T(8,128)(2,1)}, bf16[8,32,128]{2,1,0:T(8,128)(2,1)S(1)}, u32[]{:S(2)}, u32[]{:S(2)}) collective-permute-start(bf16[8,32,128]{2,1,0:T(8,128)(2,1)} %get-tuple-element.50), channel_id=1, source_target_pairs={{0,28},{4,24},{8,20},{12,16},{16,12},{20,8},{24,4},{28,0},{1,29},{... | collective-permute-start | bytes 196616 | tf_op jit(solution)/shard_map/ppermute | solution.py:295
  88.9 16.9 %copy-start.6 = (s32[4]{0:T(128)S(1)}, s32[4]{0:T(128)}, u32[]{:S(2)}) copy-start(s32[4]{0:T(128)} %copy-done.5) | copy-start | bytes 52
  88.9 16.9 %copy-start.8 = (bf16[8,32,128]{2,1,0:T(8,128)(2,1)S(1)}, bf16[8,32,128]{2,1,0:T(8,128)(2,1)}, u32[]{:S(2)}) copy-start(bf16[8,32,128]{2,1,0:T(8,128)(2,1)} %get-tuple-element.43.refs_0_) | copy-start | bytes 196612
  95.9 28.4 %all-to-all-start.2 = ((bf16[64,32,128]{2,1,0:T(8,128)(2,1)}), bf16[64,32,128]{2,1,0:T(8,128)(2,1)S(1)}, u32[]{:S(2)}, u32[]{:S(2)}) async-start(bf16[64,32,128]{2,1,0:T(8,128)(2,1)} %bitcast.24), calls=%async_computation.2 | async-start | bytes 1048576 | tf_op jit(solution)/shard_map/all_to_all | solution.py:274
  106.4 4.8 %collective-permute-start.14 = (f32[2,32,128]{2,1,0:T(8,128)S(1)}, f32[2,32,128]{2,1,0:T(8,128)S(1)}, u32[]{:S(2)}, u32[]{:S(2)}) collective-permute-start(f32[2,32,128]{2,1,0:T(8,128)S(1)} %get-tuple-element.52), channel_id=1, source_target_pairs={{0,32},{32,0},{64,96},{96,64},{1,33},{33,1},{65,97},{97,65},{2,34}... | collective-permute-start | bytes 98312 | tf_op jit(solution)/shard_map/ppermute | solution.py:304
  107.4 5.9 %collective-permute-start.15 = (f32[2,32,128]{2,1,0:T(8,128)S(1)}, f32[2,32,128]{2,1,0:T(8,128)S(1)}, u32[]{:S(2)}, u32[]{:S(2)}) collective-permute-start(f32[2,32,128]{2,1,0:T(8,128)S(1)} %get-tuple-element.53), channel_id=1, source_target_pairs={{0,64},{32,96},{64,0},{96,32},{1,65},{33,97},{65,1},{97,33},{2,66}... | collective-permute-start | bytes 98312 | tf_op jit(solution)/shard_map/ppermute | solution.py:304
  108.4 5.7 %collective-permute-start.16 = (f32[2,32,128]{2,1,0:T(8,128)S(1)}, f32[2,32,128]{2,1,0:T(8,128)S(1)}, u32[]{:S(2)}, u32[]{:S(2)}) collective-permute-start(f32[2,32,128]{2,1,0:T(8,128)S(1)} %get-tuple-element.54), channel_id=1, source_target_pairs={{0,96},{32,64},{64,32},{96,0},{1,97},{33,65},{65,33},{97,1},{2,98}... | collective-permute-start | bytes 98312 | tf_op jit(solution)/shard_map/ppermute | solution.py:304
  114.2 6.1 %collective-permute-start.17 = (f32[4,32,128]{2,1,0:T(8,128)S(1)}, f32[4,32,128]{2,1,0:T(8,128)S(1)}, u32[]{:S(2)}, u32[]{:S(2)}) collective-permute-start(f32[4,32,128]{2,1,0:T(8,128)S(1)} %pick_step.1), channel_id=1, source_target_pairs={{0,128},{128,0},{1,129},{129,1},{2,130},{130,2},{3,131},{131,3},{4... | collective-permute-start | bytes 196616 | tf_op jit(solution)/shard_map/ppermute | solution.py:305

commit v5 on v4

--- a/solution.py
+++ b/solution.py
@@ -77,45 +77,58 @@
     )(stem, branch)
 
 
-def turn_kernel(me_ref, own_ref, other_ref, out_ref):
+def turn_kernel(me_ref, *refs):
+    own, other, (out_hbm, out, out_sem) = refs[:RING], refs[RING : 2 * RING], refs[2 * RING :]
     first_core = me_ref[2] == 0
-    for dx in range(RING):
-        x = me_ref[0] ^ dx
-        for dy in range(RING):
-            y = me_ref[1] ^ dy
-            at = pl.multiple_of((((x // 2) * RING + y) * 2 + x % 2) * 128, 128)
-            for r in range(2):
-                low = jnp.where(first_core, own_ref[dx, dy, r], other_ref[dx, dy, r])
-                high = jnp.where(first_core, other_ref[dy, dx, r], own_ref[dy, dx, r])
-                out_ref[r, :, pl.ds(at, 128)] = jnp.concatenate([low, high], axis=0).T
+    sends = []
+    for r in range(2):
+        for dx in range(RING):
+            x = me_ref[0] ^ dx
+            for dy in range(RING):
+                y = me_ref[1] ^ dy
+                at = pl.multiple_of((((x // 2) * RING + y) * 2 + x % 2) * 128, 128)
+                low = jnp.where(first_core, own[dx][dy, r], other[dx][dy, r])
+                high = jnp.where(first_core, other[dy][dx, r], own[dy][dx, r])
+                out[r, :, pl.ds(at, 128)] = jnp.concatenate([low, high], axis=0).T
+        sends.append(pltpu.make_async_copy(out.at[r], out_hbm.at[r], out_sem.at[r]))
+        sends[r].start()
+    for send in sends:
+        send.wait()
 
 
 def turn_step(me, own, other):
     return pl.pallas_call(
         turn_kernel,
-        in_specs=[SMEM, VMEM, VMEM],
-        out_specs=VMEM,
+        in_specs=[SMEM] + [VMEM] * (2 * RING),
+        out_specs=ANY,
         out_shape=jax.ShapeDtypeStruct((2, 512, 2048), jnp.bfloat16),
-        compiler_params=pltpu.CompilerParams(vmem_limit_bytes=32 << 20),
-        cost_estimate=pl.CostEstimate(flops=4000000000, bytes_accessed=8 << 20, transcendentals=0),
+        scratch_shapes=[pltpu.VMEM((2, 512, 2048), jnp.bfloat16), pltpu.SemaphoreType.DMA((2,))],
+        compiler_params=pltpu.CompilerParams(vmem_limit_bytes=56 << 20),
+        cost_estimate=pl.CostEstimate(flops=10000000000, bytes_accessed=8 << 20, transcendentals=0),
         name="turn_step",
-    )(me, own, other)
+    )(me, *own, *other)
 
 
 def second_kernel(split, me_ref, x_hbm, b_hbm, *refs):
     x, b, out, x_sem, b_sem, out_sem = refs[-6:]
     out_hbm = refs[:-6]
-    copies = [pltpu.make_async_copy(x_hbm, x, x_sem), pltpu.make_async_copy(b_hbm, b, b_sem)]
-    for copy in copies:
+    x_copy = pltpu.make_async_copy(x_hbm, x, x_sem)
+    b_copies = [
+        pltpu.make_async_copy(b_hbm.at[:, pl.ds(h * 256, 256)], b.at[:, pl.ds(h * 256, 256)], b_sem.at[h])
+        for h in range(2)
+    ]
+    for copy in (x_copy, *b_copies):
         copy.start()
 
     def dot(left, right):
         return lax.dot_general(left, right, NN, preferred_element_type=jnp.float32)
 
-    for copy in copies:
-        copy.wait()
+    x_copy.wait()
     xr, xi = (x[:, r].reshape(2048, 256) for r in range(2))
+    sends = []
     for t in range(4):
+        if t % 2 == 0:
+            b_copies[t // 2].wait()
         rows = slice(t * 128, (t + 1) * 128)
         br, bi = b[0, rows], b[1, rows]
         res = [dot(br, xr) + dot(-bi, xi), dot(bi, xr) + dot(br, xi)]
@@ -124,13 +137,14 @@
             parts = [res[r][q * 64 + jh * 32 : q * 64 + (jh + 1) * 32] for jh in range(2) for r in range(2)]
             for za in range(DEPTH):
                 out[za, t * 2 + q] = jnp.concatenate([part[:, za * 32 : (za + 1) * 32] for part in parts], axis=1)
-    sends = []
-    for d in range(DEPTH):
-        if split:
+        if t % 2 == 1 and not split:
+            part = pl.ds(t * 2 - 2, 4)
+            sends.append(pltpu.make_async_copy(out.at[:, part], out_hbm[0].at[:, part], out_sem.at[t // 2]))
+            sends[-1].start()
+    if split:
+        for d in range(DEPTH):
             sends.append(pltpu.make_async_copy(out.at[me_ref[3] ^ d], out_hbm[d], out_sem.at[d]))
-        else:
-            sends.append(pltpu.make_async_copy(out.at[d], out_hbm[0].at[d], out_sem.at[d]))
-        sends[d].start()
+            sends[-1].start()
     for send in sends:
         send.wait()
 
@@ -151,10 +165,10 @@
             pltpu.VMEM((2, 512, 2048), jnp.bfloat16),
             pltpu.VMEM(shape, jnp.bfloat16),
             pltpu.SemaphoreType.DMA,
-            pltpu.SemaphoreType.DMA,
+            pltpu.SemaphoreType.DMA((2,)),
             pltpu.SemaphoreType.DMA((DEPTH,)),
         ],
-        compiler_params=pltpu.CompilerParams(vmem_limit_bytes=60 << 20),
+        compiler_params=pltpu.CompilerParams(vmem_limit_bytes=(24 if split else 60) << 20),
         cost_estimate=pl.CostEstimate(flops=2150000000, bytes_accessed=7 << 20, transcendentals=0),
         name="second_step",
     )(me, x, b2)
@@ -282,13 +296,14 @@
     near = ring_blocks(branch_second.reshape(1, 2, slices * 16, 512), 0)
     sent = first_step(stem, branch_first, 0, 1200000000)
     sent, near, stem = lax.optimization_barrier((sent, near, stem))
-    own = pack(ring_blocks(pack(near), 1))
+    own = ring_blocks(pack(near), 1)
     arrived = exchange(sent.reshape(32, 2 * slices * 16, 256), PLANE)
-    later = first_step(stem, branch_first, 1, 20000000000)
-    arrived, later = lax.optimization_barrier((arrived, later))
-    other = lax.ppermute(own, "core", [(0, 1), (1, 0)])
-    blocks = (RING, RING, 2, slices * 16, 512)
-    turned = turn_step(me, own.reshape(blocks), other.reshape(blocks))
+    later = first_step(stem, branch_first, 1, 10000000000)
+    other = [lax.ppermute(block, "core", [(0, 1), (1, 0)]) for block in own]
+    blocks = (RING, 2, slices * 16, 512)
+    own, other = ([block.reshape(blocks) for block in part] for part in (own, other))
+    turned = turn_step(me, own, other)
+    arrived, later, turned = lax.optimization_barrier((arrived, later, turned))
     later = exchange(later.reshape(32, 2 * slices * 16, 256), PLANE)
     half = list(second_step(me, arrived.reshape(32, 2, slices * 16, 256), turned, True))
     for d in range(1, DEPTH):

time: 126 us -> 124 us (0.984)
  waiting for transfers between devices: 34 us -> 30.6 us
  starting transfers between devices: 57.1 us -> 59.9 us
  local copies, waits for them, and re-layouts: 5.64 us -> 4.09 us
    ppermute x6, waiting for transfers between devices: 16.7 us -> 7.15 us  [ring_blocks(): blocks.append(lax.ppermute(block, PLANE, pairs))]
    all_to_all x3, waiting for transfers between devices: 10.8 us -> 17.3 us  [exchange(): return lax.all_to_all(block, axes, split_axis=0, concat_axis=0, tiled=True)]
    all_to_all x3, starting transfers between devices: 21.9 us -> 25.1 us  [exchange(): return lax.all_to_all(block, axes, split_axis=0, concat_axis=0, tiled=True)]
    pallas_call x2, Pallas kernels: 13.8 us -> 11.5 us  [second_step(): pl.pallas_call(functools.partial(second_kernel, split), in_specs=[SMEM, A...]
    pallas_call x1, Pallas kernels: 2.93 us -> 4.84 us  [turn_step(): pl.pallas_call(turn_kernel, in_specs=[SMEM] + [VMEM] * (2 * RING), out_sp...]
    unnamed x18 -> x20, local copies, waits for them, and re-layouts: 5.64 us -> 4.09 us
  transfers between devices with their start and end apart: 21 -> 24, of which waited for: 8 -> 8; matrix products, arithmetic and copies ran while one was open for 0% -> 1% of each run, Pallas kernels for 22% -> 22%
where the time goes in v5:
time: 124 us
  starting transfers between devices  59.9 us (48%)
  waiting for transfers between devices  30.6 us (25%)
  Pallas kernels  28.3 us (23%)
  local copies, waits for them, and re-layouts  4.09 us (3%)
    all_to_all x3, starting transfers between devices, exchange(): return lax.all_to_all(block, axes, split_axis=0, concat_axis=0, tiled=True)  25.1 us
    ppermute x7, starting transfers between devices, shards(): half[d] = lax.ppermute(half[d], 'z', [(z, z ^ d) for z in range(DEPTH)])  18.2 us
    all_to_all x3, waiting for transfers between devices, exchange(): return lax.all_to_all(block, axes, split_axis=0, concat_axis=0, tiled=True)  17.3 us
    pallas_call x2, Pallas kernels, second_step(): pl.pallas_call(functools.partial(second_kernel, split), in_specs=[SMEM, A...  11.5 us
    pallas_call x2, Pallas kernels, first_step(): pl.pallas_call(functools.partial(first_kernel, lh), in_specs=[ANY] * 2, o...  9.73 us
    ppermute x6, starting transfers between devices, ring_blocks(): blocks.append(lax.ppermute(block, PLANE, pairs))  8.27 us
    ppermute x6, waiting for transfers between devices, ring_blocks(): blocks.append(lax.ppermute(block, PLANE, pairs))  7.15 us
    pallas_call x1, Pallas kernels, turn_step(): pl.pallas_call(turn_kernel, in_specs=[SMEM] + [VMEM] * (2 * RING), out_sp...  4.84 us
  transfers between devices with their start and end apart: 24, of which 8 were waited for; matrix products, arithmetic and copies ran while one was open for 1% of the time, Pallas kernels for 22%

profile of v5, /device:TPU:24, one launch (start us, length us, event | category | flops | bytes accessed | tf_op | source)
XLA Modules:
  0.0 123.8 jit_solution(4404723545375404576)
XLA Ops:
  0.0 2.0 %collective-permute-start.2 = (bf16[1,2,64,512]{3,2,1,0:T(8,128)(2,1)}, bf16[1,2,64,512]{3,2,1,0:T(8,128)(2,1)S(1)}, u32[]{:S(2)}, u32[]{:S(2)}) collective-permute-start(bf16[1,2,64,512]{3,2,1,0:T(8,128)(2,1)} %bitcast.14), channel_id=1, source_target_pairs={{96,0},{131,1},{64,32},{163,33},{32,64},{195,65},{0,96},{227,97},{... | collective-permute-start | bytes 393224 | tf_op jit(solution)/shard_map/ppermute | solution.py:265
  2.0 0.9 collective-permute-start.1
  2.8 1.3 %collective-permute-start = (bf16[1,2,64,512]{3,2,1,0:T(8,128)(2,1)}, bf16[1,2,64,512]{3,2,1,0:T(8,128)(2,1)S(1)}, u32[]{:S(2)}, u32[]{:S(2)}) collective-permute-start(bf16[1,2,64,512]{3,2,1,0:T(8,128)(2,1)} %bitcast.16), channel_id=1, source_target_pairs={{32,0},{3,1},{0,32},{35,33},{96,64},{67,65},{64,96},{99,97},{34,2}... | collective-permute-start | bytes 393224 | tf_op jit(solution)/shard_map/ppermute | solution.py:265
  4.1 4.8 %first_step.2 = bf16[8,4,2,4,16,256]{5,4,3,2,1,0:T(8,128)(2,1)} custom-call(bf16[2,4,8,4,32,256]{5,4,3,2,1,0:T(8,128)(2,1)} %bitcast.19, bf16[2,4,256,256]{3,2,1,0:T(8,128)(2,1)} %branch_hbm.3), custom_call_target="tpu_custom_call" | custom-call | flops 1200000000 | bytes 7340032 | tf_op jit(solution)/shard_map/first_step/pallas_call | solution.py:60
  8.9 0.0 collective-permute-done.2.refs_3_
  9.0 0.0 collective-permute-done.1.refs_2_
  9.0 0.0 collective-permute-done.refs_1_
  9.0 0.0 copy-done.1
  9.0 2.8 %collective-permute-start.5 = (bf16[4,2,64,512]{3,2,1,0:T(8,128)(2,1)S(1)}, bf16[4,2,64,512]{3,2,1,0:T(8,128)(2,1)S(1)}, u32[]{:S(2)}, u32[]{:S(2)}) collective-permute-start(bf16[4,2,64,512]{3,2,1,0:T(8,128)(2,1)S(1)} %pack.1.refs_0_), channel_id=1, source_target_pairs={{130,0},{97,1},{162,32},{65,33},{194,64},{33,65},{226,96},{1,97},{... | collective-permute-start | bytes 1572872 | tf_op jit(solution)/shard_map/ppermute | solution.py:265
  11.9 0.8 collective-permute-start.4
  12.7 0.5 collective-permute-start.3
  13.2 7.3 %all-to-all-start = ((bf16[32,128,256]{2,1,0:T(8,128)(2,1)}), bf16[32,128,256]{2,1,0:T(8,128)(2,1)S(1)}, u32[]{:S(2)}, u32[]{:S(2)}) async-start(bf16[32,128,256]{2,1,0:T(8,128)(2,1)} %bitcast.18), calls=%async_computation | async-start | bytes 4194304 | tf_op jit(solution)/shard_map/all_to_all | solution.py:288
  20.6 0.7 pad_add_fusion.me_ref
  21.2 0.1 collective-permute-start.6
  21.4 7.1 %collective-permute-done.5.refs_3_ = bf16[4,2,64,512]{3,2,1,0:T(8,128)(2,1)S(1)} collective-permute-done((bf16[4,2,64,512]{3,2,1,0:T(8,128)(2,1)S(1)}, bf16[4,2,64,512]{3,2,1,0:T(8,128)(2,1)S(1)}, u32[]{:S(2)}, u32[]{:S(2)}) %collective-permute-start.5) | collective-permute-done | bytes 524320 | tf_op jit(solution)/shard_map/ppermute | solution.py:265
  28.4 0.0 collective-permute-start.9
  28.4 0.0 collective-permute-done.4.refs_2_
  28.4 0.5 collective-permute-start.8
  28.9 0.1 collective-permute-done.3.refs_1_
  29.0 0.0 collective-permute-start.7
  29.0 4.9 %first_step.3 = bf16[8,4,2,4,16,256]{5,4,3,2,1,0:T(8,128)(2,1)} custom-call(bf16[2,4,8,4,32,256]{5,4,3,2,1,0:T(8,128)(2,1)} %bitcast.20, bf16[2,4,256,256]{3,2,1,0:T(8,128)(2,1)} %branch_hbm.3), custom_call_target="tpu_custom_call" | custom-call | flops 10000000000 | bytes 7340032 | tf_op jit(solution)/shard_map/first_step/pallas_call | solution.py:60
  33.9 0.0 collective-permute-done.6.refs_4_
  34.0 0.0 copy-start.6
  34.0 0.0 collective-permute-done.9.refs_7_
  34.0 0.0 collective-permute-done.8.refs_6_
  34.0 0.0 collective-permute-done.7.refs_5_
  34.0 0.7 copy-done.6
  34.7 0.2 copy-done.7
  35.0 0.1 copy-done.8
  35.1 0.8 copy-done.9
  35.9 4.8 %turn_step.1.b_hbm = bf16[2,512,2048]{2,1,0:T(8,128)(2,1)} custom-call(s32[4]{0:T(128)} %pad_add_fusion.me_ref, bf16[4,2,64,512]{3,2,1,0:T(8,128)(2,1)} %copy-done, bf16[4,2,64,512]{3,2,1,0:T(8,128)(2,1)} %collective-permute-done.3.refs_1_, bf16[4,2,64,512]{3,2,1,0:T(8,128)(2,1)} %collective-permute-done.4.refs_2_, bf16[4,2,64,512]{3,2,1,0:T(8,128)(2,1)} %copy-done.5, ...), custom_call_target="tpu_custom_call" | custom-call | flops 10000000000 | bytes 8388608 | tf_op jit(solution)/shard_map/turn_step/pallas_call | solution.py:100
  40.7 11.0 %all-to-all-done = bf16[32,128,256]{2,1,0:T(8,128)(2,1)S(1)} async-done(((bf16[32,128,256]{2,1,0:T(8,128)(2,1)}), bf16[32,128,256]{2,1,0:T(8,128)(2,1)S(1)}, u32[]{:S(2)}, u32[]{:S(2)}) %all-to-all-start) | async-done | bytes 2097184 | tf_op jit(solution)/shard_map/all_to_all | solution.py:288
  51.7 4.9 %all-to-all-start.1 = ((bf16[32,128,256]{2,1,0:T(8,128)(2,1)}), bf16[32,128,256]{2,1,0:T(8,128)(2,1)}, u32[]{:S(2)}, u32[]{:S(2)}) async-start(bf16[32,128,256]{2,1,0:T(8,128)(2,1)} %bitcast.21), calls=%async_computation.1 | async-start | bytes 4194304 | tf_op jit(solution)/shard_map/all_to_all | solution.py:288
  56.6 2.2 %copy-done.4 = bf16[2,512,2048]{2,1,0:T(8,128)(2,1)S(1)} copy-done((bf16[2,512,2048]{2,1,0:T(8,128)(2,1)S(1)}, bf16[2,512,2048]{2,1,0:T(8,128)(2,1)}, u32[]{:S(2)}) %copy-start.4) | copy-done | bytes 4194328
  58.8 4.7 %second_step.2 = (bf16[8,32,128]{2,1,0:T(8,128)(2,1)S(1)}, bf16[8,32,128]{2,1,0:T(8,128)(2,1)S(1)}, bf16[8,32,128]{2,1,0:T(8,128)(2,1)S(1)}, bf16[8,32,128]{2,1,...) custom-call(s32[4]{0:T(128)S(1)} %copy-done.2, ...), custom_call_target="tpu_custom_call" | custom-call | flops 2150000128 | bytes 7340032 | tf_op jit(solution)/shard_map/second_step/pallas_call | solution.py:158
  63.5 2.0 %collective-permute-start.10 = (bf16[8,32,128]{2,1,0:T(8,128)(2,1)S(1)}, bf16[8,32,128]{2,1,0:T(8,128)(2,1)S(1)}, u32[]{:S(2)}, u32[]{:S(2)}) collective-permute-start(bf16[8,32,128]{2,1,0:T(8,128)(2,1)S(1)} %get-tuple-element.41), channel_id=1, source_target_pairs={{0,4},{4,0},{8,12},{12,8},{16,20},{20,16},{24,28},{28,24},{1,5},{5... | collective-permute-start | bytes 196616 | tf_op jit(solution)/shard_map/ppermute | solution.py:310
  65.6 3.3 %collective-permute-start.11 = (bf16[8,32,128]{2,1,0:T(8,128)(2,1)S(1)}, bf16[8,32,128]{2,1,0:T(8,128)(2,1)S(1)}, u32[]{:S(2)}, u32[]{:S(2)}) collective-permute-start(bf16[8,32,128]{2,1,0:T(8,128)(2,1)S(1)} %get-tuple-element.42), channel_id=1, source_target_pairs={{0,8},{4,12},{8,0},{12,4},{16,24},{20,28},{24,16},{28,20},{1,9},{5... | collective-permute-start | bytes 196616 | tf_op jit(solution)/shard_map/ppermute | solution.py:310
  68.8 0.0 collective-permute-start.12
  68.8 6.4 %collective-permute-start.13 = (bf16[8,32,128]{2,1,0:T(8,128)(2,1)S(1)}, bf16[8,32,128]{2,1,0:T(8,128)(2,1)S(1)}, u32[]{:S(2)}, u32[]{:S(2)}) collective-permute-start(bf16[8,32,128]{2,1,0:T(8,128)(2,1)S(1)} %get-tuple-element.49), channel_id=1, source_target_pairs={{0,16},{4,20},{8,24},{12,28},{16,0},{20,4},{24,8},{28,12},{1,17},{... | collective-permute-start | bytes 196616 | tf_op jit(solution)/shard_map/ppermute | solution.py:310
  75.2 0.0 collective-permute-start.14
  75.2 0.0 collective-permute-done.10.refs_1_
  75.2 4.6 %collective-permute-start.15 = (bf16[8,32,128]{2,1,0:T(8,128)(2,1)S(1)}, bf16[8,32,128]{2,1,0:T(8,128)(2,1)S(1)}, u32[]{:S(2)}, u32[]{:S(2)}) collective-permute-start(bf16[8,32,128]{2,1,0:T(8,128)(2,1)S(1)} %get-tuple-element.51), channel_id=1, source_target_pairs={{0,24},{4,28},{8,16},{12,20},{16,8},{20,12},{24,0},{28,4},{1,25},{... | collective-permute-start | bytes 196616 | tf_op jit(solution)/shard_map/ppermute | solution.py:310
  79.8 0.0 collective-permute-done.11.refs_2_
  79.8 1.9 %collective-permute-start.16 = (bf16[8,32,128]{2,1,0:T(8,128)(2,1)S(1)}, bf16[8,32,128]{2,1,0:T(8,128)(2,1)S(1)}, u32[]{:S(2)}, u32[]{:S(2)}) collective-permute-start(bf16[8,32,128]{2,1,0:T(8,128)(2,1)S(1)} %get-tuple-element.52), channel_id=1, source_target_pairs={{0,28},{4,24},{8,20},{12,16},{16,12},{20,8},{24,4},{28,0},{1,29},{... | collective-permute-start | bytes 196616 | tf_op jit(solution)/shard_map/ppermute | solution.py:310
  81.7 0.0 collective-permute-done.12.refs_3_
  81.7 2.1 %all-to-all-done.1 = bf16[32,128,256]{2,1,0:T(8,128)(2,1)} async-done(((bf16[32,128,256]{2,1,0:T(8,128)(2,1)}), bf16[32,128,256]{2,1,0:T(8,128)(2,1)}, u32[]{:S(2)}, u32[]{:S(2)}) %all-to-all-start.1) | async-done | bytes 2097184 | tf_op jit(solution)/shard_map/all_to_all | solution.py:288
  83.8 6.8 %second_step.3 = bf16[8,8,32,128]{3,2,1,0:T(8,128)(2,1)} custom-call(s32[4]{0:T(128)} %pad_add_fusion.me_ref, bf16[32,2,64,256]{3,2,1,0:T(8,128)(2,1)} %bitcast.9.x_hbm, bf16[2,512,2048]{2,1,0:T(8,128)(2,1)} %turn_step.1.b_hbm), custom_call_target="tpu_custom_call" | custom-call | flops 2150000128 | bytes 7340032 | tf_op jit(solution)/shard_map/second_step/pallas_call | solution.py:158
  90.6 12.9 %all-to-all-start.2 = ((bf16[64,32,128]{2,1,0:T(8,128)(2,1)}), bf16[64,32,128]{2,1,0:T(8,128)(2,1)S(1)}, u32[]{:S(2)}, u32[]{:S(2)}) async-start(bf16[64,32,128]{2,1,0:T(8,128)(2,1)} %bitcast.22), calls=%async_computation.2 | async-start | bytes 1048576 | tf_op jit(solution)/shard_map/all_to_all | solution.py:288
  103.5 0.0 collective-permute-done.13.refs_4_
  103.6 0.0 collective-permute-done.14.refs_5_
  103.6 0.0 collective-permute-done.15.refs_6_
  103.6 0.0 collective-permute-done.16.refs_7_
  103.6 0.0 copy-done.3
  103.6 0.6 total_step.1
  104.2 0.9 collective-permute-start.17
  105.2 1.1 collective-permute-start.18
  106.2 2.8 %collective-permute-start.19 = (f32[2,32,128]{2,1,0:T(8,128)S(1)}, f32[2,32,128]{2,1,0:T(8,128)S(1)}, u32[]{:S(2)}, u32[]{:S(2)}) collective-permute-start(f32[2,32,128]{2,1,0:T(8,128)S(1)} %get-tuple-element.56), channel_id=1, source_target_pairs={{0,96},{32,64},{64,32},{96,0},{1,97},{33,65},{65,33},{97,1},{2,98}... | collective-permute-start | bytes 98312 | tf_op jit(solution)/shard_map/ppermute | solution.py:319
  109.0 0.0 collective-permute-done.17.refs_1_
  109.0 2.0 %collective-permute-done.18.refs_2_ = f32[2,32,128]{2,1,0:T(8,128)S(1)} collective-permute-done((f32[2,32,128]{2,1,0:T(8,128)S(1)}, f32[2,32,128]{2,1,0:T(8,128)S(1)}, u32[]{:S(2)}, u32[]{:S(2)}) %collective-permute-start.18) | collective-permute-done | bytes 32800 | tf_op jit(solution)/shard_map/ppermute | solution.py:319
  111.0 0.8 collective-permute-done.19.refs_3_
  111.9 2.9 %collective-permute-start.20 = (f32[4,32,128]{2,1,0:T(8,128)S(1)}, f32[4,32,128]{2,1,0:T(8,128)S(1)}, u32[]{:S(2)}, u32[]{:S(2)}) collective-permute-start(f32[4,32,128]{2,1,0:T(8,128)S(1)} %pick_step.1), channel_id=1, source_target_pairs={{0,128},{128,0},{1,129},{129,1},{2,130},{130,2},{3,131},{131,3},{4... | collective-permute-start | bytes 196616 | tf_op jit(solution)/shard_map/ppermute | solution.py:320
  114.7 3.3 %collective-permute-done.20.across_ref = f32[4,32,128]{2,1,0:T(8,128)S(1)} collective-permute-done((f32[4,32,128]{2,1,0:T(8,128)S(1)}, f32[4,32,128]{2,1,0:T(8,128)S(1)}, u32[]{:S(2)}, u32[]{:S(2)}) %collective-permute-start.20) | collective-permute-done | bytes 65568 | tf_op jit(solution)/shard_map/ppermute | solution.py:320
  118.0 4.2 %all-to-all-done.2 = bf16[64,32,128]{2,1,0:T(8,128)(2,1)S(1)} async-done(((bf16[64,32,128]{2,1,0:T(8,128)(2,1)}), bf16[64,32,128]{2,1,0:T(8,128)(2,1)S(1)}, u32[]{:S(2)}, u32[]{:S(2)}) %all-to-all-start.2) | async-done | bytes 524320 | tf_op jit(solution)/shard_map/all_to_all | solution.py:288
  122.2 1.5 %lay_step.1 = f32[2,64,1,512]{3,2,1,0:T(1,128)} custom-call(s32[4]{0:T(128)S(1)} %copy-done.3, bf16[8,8,32,128]{3,2,1,0:T(8,128)(2,1)S(1)} %bitcast.12, f32[4,32,128]{2,1,0:T(8,128)S(1)} %collective-permute-done.20.across_ref, f32[2,32,128]{2,1,0:T(8,128)S(1)} %get-tuple-element.53.refs_0_, f32[2,32,128]{2,1,0:T(8,128)S(1)} %collective-permute-done.17.refs_1_, ...), custom_call_target="tpu_custom_call" | custom-call | flops 1000000 | bytes 1048576 | tf_op jit(solution)/shard_map/lay_step/pallas_call | solution.py:239
  (14 shorter events, 0.1 us)
Async XLA Ops:
  0.0 9.0 %collective-permute-start.2 = (bf16[1,2,64,512]{3,2,1,0:T(8,128)(2,1)}, bf16[1,2,64,512]{3,2,1,0:T(8,128)(2,1)S(1)}, u32[]{:S(2)}, u32[]{:S(2)}) collective-permute-start(bf16[1,2,64,512]{3,2,1,0:T(8,128)(2,1)} %bitcast.14), channel_id=1, source_target_pairs={{96,0},{131,1},{64,32},{163,33},{32,64},{195,65},{0,96},{227,97},{... | collective-permute-start | bytes 393224 | tf_op jit(solution)/shard_map/ppermute | solution.py:265
  2.0 7.0 %collective-permute-start.1 = (bf16[1,2,64,512]{3,2,1,0:T(8,128)(2,1)}, bf16[1,2,64,512]{3,2,1,0:T(8,128)(2,1)S(1)}, u32[]{:S(2)}, u32[]{:S(2)}) collective-permute-start(bf16[1,2,64,512]{3,2,1,0:T(8,128)(2,1)} %bitcast.15), channel_id=1, source_target_pairs={{64,0},{129,1},{96,32},{161,33},{0,64},{193,65},{32,96},{225,97},{... | collective-permute-start | bytes 393224 | tf_op jit(solution)/shard_map/ppermute | solution.py:265
  2.8 6.2 %collective-permute-start = (bf16[1,2,64,512]{3,2,1,0:T(8,128)(2,1)}, bf16[1,2,64,512]{3,2,1,0:T(8,128)(2,1)S(1)}, u32[]{:S(2)}, u32[]{:S(2)}) collective-permute-start(bf16[1,2,64,512]{3,2,1,0:T(8,128)(2,1)} %bitcast.16), channel_id=1, source_target_pairs={{32,0},{3,1},{0,32},{35,33},{96,64},{67,65},{64,96},{99,97},{34,2}... | collective-permute-start | bytes 393224 | tf_op jit(solution)/shard_map/ppermute | solution.py:265
  4.1 4.9 %copy-start.1 = (bf16[2,4,16,512]{3,2,1,0:T(8,128)(2,1)S(1)}, bf16[2,4,16,512]{3,2,1,0:T(8,128)(2,1)}, u32[]{:S(2)}) copy-start(bf16[2,4,16,512]{3,2,1,0:T(8,128)(2,1)} %param.5) | copy-start | bytes 393220
  9.0 12.2 %copy-start = (bf16[4,2,64,512]{3,2,1,0:T(8,128)(2,1)}, bf16[4,2,64,512]{3,2,1,0:T(8,128)(2,1)S(1)}, u32[]{:S(2)}) copy-start(bf16[4,2,64,512]{3,2,1,0:T(8,128)(2,1)S(1)} %pack.1.refs_0_) | copy-start | bytes 1572868
  9.0 19.4 %collective-permute-start.5 = (bf16[4,2,64,512]{3,2,1,0:T(8,128)(2,1)S(1)}, bf16[4,2,64,512]{3,2,1,0:T(8,128)(2,1)S(1)}, u32[]{:S(2)}, u32[]{:S(2)}) collective-permute-start(bf16[4,2,64,512]{3,2,1,0:T(8,128)(2,1)S(1)} %pack.1.refs_0_), channel_id=1, source_target_pairs={{130,0},{97,1},{162,32},{65,33},{194,64},{33,65},{226,96},{1,97},{... | collective-permute-start | bytes 1572872 | tf_op jit(solution)/shard_map/ppermute | solution.py:265
  11.9 16.5 %collective-permute-start.4 = (bf16[4,2,64,512]{3,2,1,0:T(8,128)(2,1)S(1)}, bf16[4,2,64,512]{3,2,1,0:T(8,128)(2,1)}, u32[]{:S(2)}, u32[]{:S(2)}) collective-permute-start(bf16[4,2,64,512]{3,2,1,0:T(8,128)(2,1)S(1)} %pack.1.refs_0_), channel_id=1, source_target_pairs={{128,0},{65,1},{160,32},{97,33},{192,64},{1,65},{224,96},{33,97},{... | collective-permute-start | bytes 1572872 | tf_op jit(solution)/shard_map/ppermute | solution.py:265
  12.7 16.3 %collective-permute-start.3 = (bf16[4,2,64,512]{3,2,1,0:T(8,128)(2,1)S(1)}, bf16[4,2,64,512]{3,2,1,0:T(8,128)(2,1)}, u32[]{:S(2)}, u32[]{:S(2)}) collective-permute-start(bf16[4,2,64,512]{3,2,1,0:T(8,128)(2,1)S(1)} %pack.1.refs_0_), channel_id=1, source_target_pairs={{2,0},{33,1},{34,32},{1,33},{66,64},{97,65},{98,96},{65,97},{0,2},... | collective-permute-start | bytes 1572872 | tf_op jit(solution)/shard_map/ppermute | solution.py:265
  13.2 38.5 %all-to-all-start = ((bf16[32,128,256]{2,1,0:T(8,128)(2,1)}), bf16[32,128,256]{2,1,0:T(8,128)(2,1)S(1)}, u32[]{:S(2)}, u32[]{:S(2)}) async-start(bf16[32,128,256]{2,1,0:T(8,128)(2,1)} %bitcast.18), calls=%async_computation | async-start | bytes 4194304 | tf_op jit(solution)/shard_map/all_to_all | solution.py:288
  21.2 12.7 %collective-permute-start.6 = (bf16[4,2,64,512]{3,2,1,0:T(8,128)(2,1)S(1)}, bf16[4,2,64,512]{3,2,1,0:T(8,128)(2,1)S(1)}, u32[]{:S(2)}, u32[]{:S(2)}) collective-permute-start(bf16[4,2,64,512]{3,2,1,0:T(8,128)(2,1)S(1)} %pack.1.refs_0_), channel_id=1, source_target_pairs={{0,1},{1,0},{2,3},{3,2},{4,5},{5,4},{6,7},{7,6},{8,9},{9,8},{10,11... | collective-permute-start | bytes 1572872 | tf_op jit(solution)/shard_map/ppermute | solution.py:302
  28.4 5.5 %copy-start.5 = (bf16[4,2,64,512]{3,2,1,0:T(8,128)(2,1)}, bf16[4,2,64,512]{3,2,1,0:T(8,128)(2,1)S(1)}, u32[]{:S(2)}) copy-start(bf16[4,2,64,512]{3,2,1,0:T(8,128)(2,1)S(1)} %collective-permute-done.5.refs_3_) | copy-start | bytes 1572868
  28.4 5.5 %collective-permute-start.9 = (bf16[4,2,64,512]{3,2,1,0:T(8,128)(2,1)S(1)}, bf16[4,2,64,512]{3,2,1,0:T(8,128)(2,1)S(1)}, u32[]{:S(2)}, u32[]{:S(2)}) collective-permute-start(bf16[4,2,64,512]{3,2,1,0:T(8,128)(2,1)S(1)} %collective-permute-done.5.refs_3_), channel_id=1, source_target_pairs={{0,1},{1,0},{2,3},{3,2},{4,5},{5,4},{6,7},{7,6},{8,9},{9,8},{10,11... | collective-permute-start | bytes 1572872 | tf_op jit(solution)/shard_map/ppermute | solution.py:302
  28.4 5.6 %collective-permute-start.8 = (bf16[4,2,64,512]{3,2,1,0:T(8,128)(2,1)}, bf16[4,2,64,512]{3,2,1,0:T(8,128)(2,1)S(1)}, u32[]{:S(2)}, u32[]{:S(2)}) collective-permute-start(bf16[4,2,64,512]{3,2,1,0:T(8,128)(2,1)} %collective-permute-done.4.refs_2_), channel_id=1, source_target_pairs={{0,1},{1,0},{2,3},{3,2},{4,5},{5,4},{6,7},{7,6},{8,9},{9,8},{10,11... | collective-permute-start | bytes 1572872 | tf_op jit(solution)/shard_map/ppermute | solution.py:302
  29.0 5.0 %collective-permute-start.7 = (bf16[4,2,64,512]{3,2,1,0:T(8,128)(2,1)}, bf16[4,2,64,512]{3,2,1,0:T(8,128)(2,1)S(1)}, u32[]{:S(2)}, u32[]{:S(2)}) collective-permute-start(bf16[4,2,64,512]{3,2,1,0:T(8,128)(2,1)} %collective-permute-done.3.refs_1_), channel_id=1, source_target_pairs={{0,1},{1,0},{2,3},{3,2},{4,5},{5,4},{6,7},{7,6},{8,9},{9,8},{10,11... | collective-permute-start | bytes 1572872 | tf_op jit(solution)/shard_map/ppermute | solution.py:302
  34.0 0.8 copy-start.6
  34.0 1.0 copy-start.7
  34.0 1.1 copy-start.8
  35.1 0.8 copy-start.9
  51.7 4.9 %copy-start.2 = (s32[4]{0:T(128)S(1)}, s32[4]{0:T(128)}, u32[]{:S(2)}) copy-start(s32[4]{0:T(128)} %pad_add_fusion.me_ref) | copy-start | bytes 52
  51.7 32.1 %all-to-all-start.1 = ((bf16[32,128,256]{2,1,0:T(8,128)(2,1)}), bf16[32,128,256]{2,1,0:T(8,128)(2,1)}, u32[]{:S(2)}, u32[]{:S(2)}) async-start(bf16[32,128,256]{2,1,0:T(8,128)(2,1)} %bitcast.21), calls=%async_computation.1 | async-start | bytes 4194304 | tf_op jit(solution)/shard_map/all_to_all | solution.py:288
  56.6 2.2 %copy-start.4 = (bf16[2,512,2048]{2,1,0:T(8,128)(2,1)S(1)}, bf16[2,512,2048]{2,1,0:T(8,128)(2,1)}, u32[]{:S(2)}) copy-start(bf16[2,512,2048]{2,1,0:T(8,128)(2,1)} %turn_step.1.b_hbm) | copy-start | bytes 12582916
  63.5 11.7 %collective-permute-start.10 = (bf16[8,32,128]{2,1,0:T(8,128)(2,1)S(1)}, bf16[8,32,128]{2,1,0:T(8,128)(2,1)S(1)}, u32[]{:S(2)}, u32[]{:S(2)}) collective-permute-start(bf16[8,32,128]{2,1,0:T(8,128)(2,1)S(1)} %get-tuple-element.41), channel_id=1, source_target_pairs={{0,4},{4,0},{8,12},{12,8},{16,20},{20,16},{24,28},{28,24},{1,5},{5... | collective-permute-start | bytes 196616 | tf_op jit(solution)/shard_map/ppermute | solution.py:310
  65.6 14.3 %collective-permute-start.11 = (bf16[8,32,128]{2,1,0:T(8,128)(2,1)S(1)}, bf16[8,32,128]{2,1,0:T(8,128)(2,1)S(1)}, u32[]{:S(2)}, u32[]{:S(2)}) collective-permute-start(bf16[8,32,128]{2,1,0:T(8,128)(2,1)S(1)} %get-tuple-element.42), channel_id=1, source_target_pairs={{0,8},{4,12},{8,0},{12,4},{16,24},{20,28},{24,16},{28,20},{1,9},{5... | collective-permute-start | bytes 196616 | tf_op jit(solution)/shard_map/ppermute | solution.py:310
  68.8 12.9 %collective-permute-start.12 = (bf16[8,32,128]{2,1,0:T(8,128)(2,1)S(1)}, bf16[8,32,128]{2,1,0:T(8,128)(2,1)S(1)}, u32[]{:S(2)}, u32[]{:S(2)}) collective-permute-start(bf16[8,32,128]{2,1,0:T(8,128)(2,1)S(1)} %get-tuple-element.43), channel_id=1, source_target_pairs={{0,12},{4,8},{8,4},{12,0},{16,28},{20,24},{24,20},{28,16},{1,13},{... | collective-permute-start | bytes 196616 | tf_op jit(solution)/shard_map/ppermute | solution.py:310
  68.8 34.7 %collective-permute-start.13 = (bf16[8,32,128]{2,1,0:T(8,128)(2,1)S(1)}, bf16[8,32,128]{2,1,0:T(8,128)(2,1)S(1)}, u32[]{:S(2)}, u32[]{:S(2)}) collective-permute-start(bf16[8,32,128]{2,1,0:T(8,128)(2,1)S(1)} %get-tuple-element.49), channel_id=1, source_target_pairs={{0,16},{4,20},{8,24},{12,28},{16,0},{20,4},{24,8},{28,12},{1,17},{... | collective-permute-start | bytes 196616 | tf_op jit(solution)/shard_map/ppermute | solution.py:310
  75.2 28.3 %collective-permute-start.14 = (bf16[8,32,128]{2,1,0:T(8,128)(2,1)S(1)}, bf16[8,32,128]{2,1,0:T(8,128)(2,1)S(1)}, u32[]{:S(2)}, u32[]{:S(2)}) collective-permute-start(bf16[8,32,128]{2,1,0:T(8,128)(2,1)S(1)} %get-tuple-element.50), channel_id=1, source_target_pairs={{0,20},{4,16},{8,28},{12,24},{16,4},{20,0},{24,12},{28,8},{1,21},{... | collective-permute-start | bytes 196616 | tf_op jit(solution)/shard_map/ppermute | solution.py:310
  75.2 28.3 %collective-permute-start.15 = (bf16[8,32,128]{2,1,0:T(8,128)(2,1)S(1)}, bf16[8,32,128]{2,1,0:T(8,128)(2,1)S(1)}, u32[]{:S(2)}, u32[]{:S(2)}) collective-permute-start(bf16[8,32,128]{2,1,0:T(8,128)(2,1)S(1)} %get-tuple-element.51), channel_id=1, source_target_pairs={{0,24},{4,28},{8,16},{12,20},{16,8},{20,12},{24,0},{28,4},{1,25},{... | collective-permute-start | bytes 196616 | tf_op jit(solution)/shard_map/ppermute | solution.py:310
  79.8 23.8 %collective-permute-start.16 = (bf16[8,32,128]{2,1,0:T(8,128)(2,1)S(1)}, bf16[8,32,128]{2,1,0:T(8,128)(2,1)S(1)}, u32[]{:S(2)}, u32[]{:S(2)}) collective-permute-start(bf16[8,32,128]{2,1,0:T(8,128)(2,1)S(1)} %get-tuple-element.52), channel_id=1, source_target_pairs={{0,28},{4,24},{8,20},{12,16},{16,12},{20,8},{24,4},{28,0},{1,29},{... | collective-permute-start | bytes 196616 | tf_op jit(solution)/shard_map/ppermute | solution.py:310
  83.8 19.8 %copy-start.3 = (s32[4]{0:T(128)S(1)}, s32[4]{0:T(128)}, u32[]{:S(2)}) copy-start(s32[4]{0:T(128)} %pad_add_fusion.me_ref) | copy-start | bytes 52
  90.6 31.6 %all-to-all-start.2 = ((bf16[64,32,128]{2,1,0:T(8,128)(2,1)}), bf16[64,32,128]{2,1,0:T(8,128)(2,1)S(1)}, u32[]{:S(2)}, u32[]{:S(2)}) async-start(bf16[64,32,128]{2,1,0:T(8,128)(2,1)} %bitcast.22), calls=%async_computation.2 | async-start | bytes 1048576 | tf_op jit(solution)/shard_map/all_to_all | solution.py:288
  104.2 4.8 %collective-permute-start.17 = (f32[2,32,128]{2,1,0:T(8,128)S(1)}, f32[2,32,128]{2,1,0:T(8,128)S(1)}, u32[]{:S(2)}, u32[]{:S(2)}) collective-permute-start(f32[2,32,128]{2,1,0:T(8,128)S(1)} %get-tuple-element.54), channel_id=1, source_target_pairs={{0,32},{32,0},{64,96},{96,64},{1,33},{33,1},{65,97},{97,65},{2,34}... | collective-permute-start | bytes 98312 | tf_op jit(solution)/shard_map/ppermute | solution.py:319
  105.2 5.9 %collective-permute-start.18 = (f32[2,32,128]{2,1,0:T(8,128)S(1)}, f32[2,32,128]{2,1,0:T(8,128)S(1)}, u32[]{:S(2)}, u32[]{:S(2)}) collective-permute-start(f32[2,32,128]{2,1,0:T(8,128)S(1)} %get-tuple-element.55), channel_id=1, source_target_pairs={{0,64},{32,96},{64,0},{96,32},{1,65},{33,97},{65,1},{97,33},{2,66}... | collective-permute-start | bytes 98312 | tf_op jit(solution)/shard_map/ppermute | solution.py:319
  106.2 5.6 %collective-permute-start.19 = (f32[2,32,128]{2,1,0:T(8,128)S(1)}, f32[2,32,128]{2,1,0:T(8,128)S(1)}, u32[]{:S(2)}, u32[]{:S(2)}) collective-permute-start(f32[2,32,128]{2,1,0:T(8,128)S(1)} %get-tuple-element.56), channel_id=1, source_target_pairs={{0,96},{32,64},{64,32},{96,0},{1,97},{33,65},{65,33},{97,1},{2,98}... | collective-permute-start | bytes 98312 | tf_op jit(solution)/shard_map/ppermute | solution.py:319
  111.9 6.2 %collective-permute-start.20 = (f32[4,32,128]{2,1,0:T(8,128)S(1)}, f32[4,32,128]{2,1,0:T(8,128)S(1)}, u32[]{:S(2)}, u32[]{:S(2)}) collective-permute-start(f32[4,32,128]{2,1,0:T(8,128)S(1)} %pick_step.1), channel_id=1, source_target_pairs={{0,128},{128,0},{1,129},{129,1},{2,130},{130,2},{3,131},{131,3},{4... | collective-permute-start | bytes 196616 | tf_op jit(solution)/shard_map/ppermute | solution.py:320

commit v6 on v5

--- a/solution.py
+++ b/solution.py
@@ -78,32 +78,26 @@
 
 
 def turn_kernel(me_ref, *refs):
-    own, other, (out_hbm, out, out_sem) = refs[:RING], refs[RING : 2 * RING], refs[2 * RING :]
+    own, other, out_ref = refs[:RING], refs[RING:-1], refs[-1]
     first_core = me_ref[2] == 0
-    sends = []
-    for r in range(2):
-        for dx in range(RING):
-            x = me_ref[0] ^ dx
-            for dy in range(RING):
-                y = me_ref[1] ^ dy
-                at = pl.multiple_of((((x // 2) * RING + y) * 2 + x % 2) * 128, 128)
+    for dx in range(RING):
+        x = me_ref[0] ^ dx
+        for dy in range(RING):
+            y = me_ref[1] ^ dy
+            at = pl.multiple_of((((x // 2) * RING + y) * 2 + x % 2) * 128, 128)
+            for r in range(2):
                 low = jnp.where(first_core, own[dx][dy, r], other[dx][dy, r])
                 high = jnp.where(first_core, other[dy][dx, r], own[dy][dx, r])
-                out[r, :, pl.ds(at, 128)] = jnp.concatenate([low, high], axis=0).T
-        sends.append(pltpu.make_async_copy(out.at[r], out_hbm.at[r], out_sem.at[r]))
-        sends[r].start()
-    for send in sends:
-        send.wait()
+                out_ref[r, :, pl.ds(at, 128)] = jnp.concatenate([low, high], axis=0).T
 
 
 def turn_step(me, own, other):
     return pl.pallas_call(
         turn_kernel,
         in_specs=[SMEM] + [VMEM] * (2 * RING),
-        out_specs=ANY,
+        out_specs=VMEM,
         out_shape=jax.ShapeDtypeStruct((2, 512, 2048), jnp.bfloat16),
-        scratch_shapes=[pltpu.VMEM((2, 512, 2048), jnp.bfloat16), pltpu.SemaphoreType.DMA((2,))],
-        compiler_params=pltpu.CompilerParams(vmem_limit_bytes=56 << 20),
+        compiler_params=pltpu.CompilerParams(vmem_limit_bytes=24 << 20),
         cost_estimate=pl.CostEstimate(flops=10000000000, bytes_accessed=8 << 20, transcendentals=0),
         name="turn_step",
     )(me, *own, *other)
@@ -298,12 +292,12 @@
     sent, near, stem = lax.optimization_barrier((sent, near, stem))
     own = ring_blocks(pack(near), 1)
     arrived = exchange(sent.reshape(32, 2 * slices * 16, 256), PLANE)
-    later = first_step(stem, branch_first, 1, 10000000000)
+    later = first_step(stem, branch_first, 1, 1000000)
     other = [lax.ppermute(block, "core", [(0, 1), (1, 0)]) for block in own]
     blocks = (RING, 2, slices * 16, 512)
     own, other = ([block.reshape(blocks) for block in part] for part in (own, other))
     turned = turn_step(me, own, other)
-    arrived, later, turned = lax.optimization_barrier((arrived, later, turned))
+    arrived, later = lax.optimization_barrier((arrived, later))
     later = exchange(later.reshape(32, 2 * slices * 16, 256), PLANE)
     half = list(second_step(me, arrived.reshape(32, 2, slices * 16, 256), turned, True))
     for d in range(1, DEPTH):

time: 124 us -> 122 us (0.984)
  local copies, waits for them, and re-layouts: 4.09 us -> 0.02 us
  starting transfers between devices: 59.9 us -> 62.9 us
  Pallas kernels: 28.3 us -> 26.6 us
    ppermute x6, waiting for transfers between devices: 7.15 us -> 0.02 us  [ring_blocks(): blocks.append(lax.ppermute(block, PLANE, pairs))]
    all_to_all x3, waiting for transfers between devices: 17.3 us -> 22.5 us  [exchange(): return lax.all_to_all(block, axes, split_axis=0, concat_axis=0, tiled=True)]
    unnamed x20 -> x8, local copies, waits for them, and re-layouts: 4.09 us -> 0.02 us
    ppermute x4, waiting for transfers between devices: 0.01 us -> 3.39 us  [shards(): other = [lax.ppermute(block, 'core', [(0, 1), (1, 0)]) for block in own]]
    all_to_all x3, starting transfers between devices: 25.1 us -> 27.7 us  [exchange(): return lax.all_to_all(block, axes, split_axis=0, concat_axis=0, tiled=True)]
    pallas_call x1, Pallas kernels: 4.84 us -> 3.17 us  [turn_step(): pl.pallas_call(turn_kernel, in_specs=[SMEM] + [VMEM] * (2 * RING), out_sp...]
  transfers between devices with their start and end apart: 24 -> 24, of which waited for: 8 -> 9; matrix products, arithmetic and copies ran while one was open for 1% -> 0% of each run, Pallas kernels for 22% -> 21%
where the time goes in v6:
time: 122 us; the launch traced here: 121 us
  starting transfers between devices  62.9 us (52%)
  waiting for transfers between devices  31.6 us (26%)
  Pallas kernels  26.6 us (22%)
    all_to_all x3, starting transfers between devices, exchange(): return lax.all_to_all(block, axes, split_axis=0, concat_axis=0, tiled=True)  27.7 us
    all_to_all x3, waiting for transfers between devices, exchange(): return lax.all_to_all(block, axes, split_axis=0, concat_axis=0, tiled=True)  22.5 us
    ppermute x7, starting transfers between devices, shards(): half[d] = lax.ppermute(half[d], 'z', [(z, z ^ d) for z in range(DEPTH)])  18.1 us
    pallas_call x2, Pallas kernels, second_step(): pl.pallas_call(functools.partial(second_kernel, split), in_specs=[SMEM, A...  11.5 us
    pallas_call x2, Pallas kernels, first_step(): pl.pallas_call(functools.partial(first_kernel, lh), in_specs=[ANY] * 2, o...  9.71 us
    ppermute x6, starting transfers between devices, ring_blocks(): blocks.append(lax.ppermute(block, PLANE, pairs))  8.27 us
    ppermute x3, starting transfers between devices, shards(): sums[dy] = lax.ppermute(sums[dy], 'y', [(y, y ^ dy) for y in range(RING)])  4.79 us
    ppermute x4, waiting for transfers between devices, shards(): other = [lax.ppermute(block, 'core', [(0, 1), (1, 0)]) for block in own]  3.39 us
  transfers between devices with their start and end apart: 24, of which 9 were waited for; matrix products, arithmetic and copies ran while one was open for 0% of the time, Pallas kernels for 21%

profile of v6, /device:TPU:24, one launch (start us, length us, event | category | flops | bytes accessed | tf_op | source)
XLA Modules:
  0.0 121.5 jit_solution(4168699388100116614)
XLA Ops:
  0.0 2.0 %collective-permute-start.2 = (bf16[1,2,64,512]{3,2,1,0:T(8,128)(2,1)}, bf16[1,2,64,512]{3,2,1,0:T(8,128)(2,1)S(1)}, u32[]{:S(2)}, u32[]{:S(2)}) collective-permute-start(bf16[1,2,64,512]{3,2,1,0:T(8,128)(2,1)} %bitcast.14), channel_id=1, source_target_pairs={{96,0},{131,1},{64,32},{163,33},{32,64},{195,65},{0,96},{227,97},{... | collective-permute-start | bytes 393224 | tf_op jit(solution)/shard_map/ppermute | solution.py:259
  2.0 0.9 collective-permute-start.1
  2.8 1.3 %collective-permute-start = (bf16[1,2,64,512]{3,2,1,0:T(8,128)(2,1)}, bf16[1,2,64,512]{3,2,1,0:T(8,128)(2,1)S(1)}, u32[]{:S(2)}, u32[]{:S(2)}) collective-permute-start(bf16[1,2,64,512]{3,2,1,0:T(8,128)(2,1)} %bitcast.16), channel_id=1, source_target_pairs={{32,0},{3,1},{0,32},{35,33},{96,64},{67,65},{64,96},{99,97},{34,2}... | collective-permute-start | bytes 393224 | tf_op jit(solution)/shard_map/ppermute | solution.py:259
  4.1 4.8 %first_step.2 = bf16[8,4,2,4,16,256]{5,4,3,2,1,0:T(8,128)(2,1)} custom-call(bf16[2,4,8,4,32,256]{5,4,3,2,1,0:T(8,128)(2,1)} %bitcast.18, bf16[2,4,256,256]{3,2,1,0:T(8,128)(2,1)} %branch_hbm.3), custom_call_target="tpu_custom_call" | custom-call | flops 1200000000 | bytes 7340032 | tf_op jit(solution)/shard_map/first_step/pallas_call | solution.py:60
  8.9 0.0 collective-permute-done.2.refs_3_
  8.9 0.0 collective-permute-done.1.refs_2_
  9.0 0.0 collective-permute-done.refs_1_
  9.0 0.0 copy-start
  9.0 7.5 %all-to-all-start = ((bf16[32,128,256]{2,1,0:T(8,128)(2,1)}), bf16[32,128,256]{2,1,0:T(8,128)(2,1)S(1)}, u32[]{:S(2)}, u32[]{:S(2)}) async-start(bf16[32,128,256]{2,1,0:T(8,128)(2,1)} %bitcast.21), calls=%async_computation | async-start | bytes 4194304 | tf_op jit(solution)/shard_map/all_to_all | solution.py:282
  16.4 0.0 copy-done
  16.5 2.8 %collective-permute-start.5 = (bf16[4,2,64,512]{3,2,1,0:T(8,128)(2,1)S(1)}, bf16[4,2,64,512]{3,2,1,0:T(8,128)(2,1)S(1)}, u32[]{:S(2)}, u32[]{:S(2)}) collective-permute-start(bf16[4,2,64,512]{3,2,1,0:T(8,128)(2,1)S(1)} %pack.1.refs_0_), channel_id=1, source_target_pairs={{130,0},{97,1},{162,32},{65,33},{194,64},{33,65},{226,96},{1,97},{... | collective-permute-start | bytes 1572872 | tf_op jit(solution)/shard_map/ppermute | solution.py:259
  19.3 0.8 collective-permute-start.4
  20.1 0.6 collective-permute-start.3
  20.7 4.9 %first_step.3 = bf16[8,4,2,4,16,256]{5,4,3,2,1,0:T(8,128)(2,1)} custom-call(bf16[2,4,8,4,32,256]{5,4,3,2,1,0:T(8,128)(2,1)} %bitcast.19, bf16[2,4,256,256]{3,2,1,0:T(8,128)(2,1)} %branch_hbm.3), custom_call_target="tpu_custom_call" | custom-call | flops 1000000 | bytes 7340032 | tf_op jit(solution)/shard_map/first_step/pallas_call | solution.py:60
  25.6 18.4 %all-to-all-done = bf16[32,128,256]{2,1,0:T(8,128)(2,1)S(1)} async-done(((bf16[32,128,256]{2,1,0:T(8,128)(2,1)}), bf16[32,128,256]{2,1,0:T(8,128)(2,1)S(1)}, u32[]{:S(2)}, u32[]{:S(2)}) %all-to-all-start) | async-done | bytes 2097184 | tf_op jit(solution)/shard_map/all_to_all | solution.py:282
  44.0 10.3 %all-to-all-start.1 = ((bf16[32,128,256]{2,1,0:T(8,128)(2,1)}), bf16[32,128,256]{2,1,0:T(8,128)(2,1)}, u32[]{:S(2)}, u32[]{:S(2)}) async-start(bf16[32,128,256]{2,1,0:T(8,128)(2,1)} %bitcast.20), calls=%async_computation.1 | async-start | bytes 4194304 | tf_op jit(solution)/shard_map/all_to_all | solution.py:282
  54.3 0.2 collective-permute-start.6
  54.6 0.0 collective-permute-done.5.refs_3_
  54.6 0.4 collective-permute-start.9
  54.9 0.0 collective-permute-done.4.refs_2_
  55.0 0.1 collective-permute-start.8
  55.1 0.0 collective-permute-done.3.refs_1_
  55.1 0.4 collective-permute-start.7
  55.5 0.1 pad_add_fusion.me_ref
  55.5 0.0 copy-start.1
  55.5 0.9 collective-permute-done.6.refs_4_
  56.5 1.5 %collective-permute-done.9.refs_7_ = bf16[4,2,64,512]{3,2,1,0:T(8,128)(2,1)} collective-permute-done((bf16[4,2,64,512]{3,2,1,0:T(8,128)(2,1)S(1)}, bf16[4,2,64,512]{3,2,1,0:T(8,128)(2,1)}, u32[]{:S(2)}, u32[]{:S(2)}) %collective-permute-start.9) | collective-permute-done | bytes 524320 | tf_op jit(solution)/shard_map/ppermute | solution.py:296
  58.0 0.2 collective-permute-done.8.refs_6_
  58.2 0.8 collective-permute-done.7.refs_5_
  58.9 3.2 %turn_step.1.b_hbm = bf16[2,512,2048]{2,1,0:T(8,128)(2,1)S(1)} custom-call(s32[4]{0:T(128)S(1)} %pad_add_fusion.me_ref, bf16[4,2,64,512]{3,2,1,0:T(8,128)(2,1)S(1)} %pack.1.refs_0_, bf16[4,2,64,512]{3,2,1,0:T(8,128)(2,1)} %collective-permute-done.3.refs_1_, bf16[4,2,64,512]{3,2,1,0:T(8,128)(2,1)} %collective-permute-done.4.refs_2_, ...), custom_call_target="tpu_custom_call" | custom-call | flops 10000000000 | bytes 8388608 | tf_op jit(solution)/shard_map/turn_step/pallas_call | solution.py:95
  62.1 0.0 copy-start.3
  62.1 0.0 copy-done.1
  62.1 4.7 %second_step.2 = (bf16[8,32,128]{2,1,0:T(8,128)(2,1)S(1)}, bf16[8,32,128]{2,1,0:T(8,128)(2,1)S(1)}, bf16[8,32,128]{2,1,0:T(8,128)(2,1)S(1)}, bf16[8,32,128]{2,1,...) custom-call(s32[4]{0:T(128)S(1)} %pad_add_fusion.me_ref, ...), custom_call_target="tpu_custom_call" | custom-call | flops 2150000128 | bytes 7340032 | tf_op jit(solution)/shard_map/second_step/pallas_call | solution.py:152
  66.9 0.0 copy-done.3
  66.9 2.0 %collective-permute-start.10 = (bf16[8,32,128]{2,1,0:T(8,128)(2,1)S(1)}, bf16[8,32,128]{2,1,0:T(8,128)(2,1)S(1)}, u32[]{:S(2)}, u32[]{:S(2)}) collective-permute-start(bf16[8,32,128]{2,1,0:T(8,128)(2,1)S(1)} %get-tuple-element.39), channel_id=1, source_target_pairs={{0,4},{4,0},{8,12},{12,8},{16,20},{20,16},{24,28},{28,24},{1,5},{5... | collective-permute-start | bytes 196616 | tf_op jit(solution)/shard_map/ppermute | solution.py:304
  68.9 3.3 %collective-permute-start.11 = (bf16[8,32,128]{2,1,0:T(8,128)(2,1)S(1)}, bf16[8,32,128]{2,1,0:T(8,128)(2,1)S(1)}, u32[]{:S(2)}, u32[]{:S(2)}) collective-permute-start(bf16[8,32,128]{2,1,0:T(8,128)(2,1)S(1)} %get-tuple-element.40), channel_id=1, source_target_pairs={{0,8},{4,12},{8,0},{12,4},{16,24},{20,28},{24,16},{28,20},{1,9},{5... | collective-permute-start | bytes 196616 | tf_op jit(solution)/shard_map/ppermute | solution.py:304
  72.2 0.0 collective-permute-start.12
  72.2 6.4 %collective-permute-start.13 = (bf16[8,32,128]{2,1,0:T(8,128)(2,1)S(1)}, bf16[8,32,128]{2,1,0:T(8,128)(2,1)S(1)}, u32[]{:S(2)}, u32[]{:S(2)}) collective-permute-start(bf16[8,32,128]{2,1,0:T(8,128)(2,1)S(1)} %get-tuple-element.47), channel_id=1, source_target_pairs={{0,16},{4,20},{8,24},{12,28},{16,0},{20,4},{24,8},{28,12},{1,17},{... | collective-permute-start | bytes 196616 | tf_op jit(solution)/shard_map/ppermute | solution.py:304
  78.5 0.0 collective-permute-start.14
  78.5 0.0 collective-permute-done.10.refs_1_
  78.5 4.6 %collective-permute-start.15 = (bf16[8,32,128]{2,1,0:T(8,128)(2,1)S(1)}, bf16[8,32,128]{2,1,0:T(8,128)(2,1)S(1)}, u32[]{:S(2)}, u32[]{:S(2)}) collective-permute-start(bf16[8,32,128]{2,1,0:T(8,128)(2,1)S(1)} %get-tuple-element.49), channel_id=1, source_target_pairs={{0,24},{4,28},{8,16},{12,20},{16,8},{20,12},{24,0},{28,4},{1,25},{... | collective-permute-start | bytes 196616 | tf_op jit(solution)/shard_map/ppermute | solution.py:304
  83.1 0.0 collective-permute-done.11.refs_2_
  83.1 1.9 %collective-permute-start.16 = (bf16[8,32,128]{2,1,0:T(8,128)(2,1)S(1)}, bf16[8,32,128]{2,1,0:T(8,128)(2,1)S(1)}, u32[]{:S(2)}, u32[]{:S(2)}) collective-permute-start(bf16[8,32,128]{2,1,0:T(8,128)(2,1)S(1)} %get-tuple-element.50), channel_id=1, source_target_pairs={{0,28},{4,24},{8,20},{12,16},{16,12},{20,8},{24,4},{28,0},{1,29},{... | collective-permute-start | bytes 196616 | tf_op jit(solution)/shard_map/ppermute | solution.py:304
  85.0 0.0 collective-permute-done.12.refs_3_
  85.0 0.0 all-to-all-done.1
  85.0 0.0 copy-start.2
  85.0 6.8 %second_step.3 = bf16[8,8,32,128]{3,2,1,0:T(8,128)(2,1)} custom-call(s32[4]{0:T(128)} %copy-done.1, bf16[32,2,64,256]{3,2,1,0:T(8,128)(2,1)} %bitcast.9.x_hbm, bf16[2,512,2048]{2,1,0:T(8,128)(2,1)} %copy-done.3), custom_call_target="tpu_custom_call" | custom-call | flops 2150000128 | bytes 7340032 | tf_op jit(solution)/shard_map/second_step/pallas_call | solution.py:152
  91.8 9.9 %all-to-all-start.2 = ((bf16[64,32,128]{2,1,0:T(8,128)(2,1)}), bf16[64,32,128]{2,1,0:T(8,128)(2,1)S(1)}, u32[]{:S(2)}, u32[]{:S(2)}) async-start(bf16[64,32,128]{2,1,0:T(8,128)(2,1)} %bitcast.22), calls=%async_computation.2 | async-start | bytes 1048576 | tf_op jit(solution)/shard_map/all_to_all | solution.py:282
  101.8 0.0 collective-permute-done.13.refs_4_
  101.8 0.0 collective-permute-done.14.refs_5_
  101.8 0.0 collective-permute-done.15.refs_6_
  101.8 0.0 collective-permute-done.16.refs_7_
  101.8 0.0 copy-done.2
  101.8 0.6 total_step.1
  102.5 0.9 collective-permute-start.17
  103.4 1.1 collective-permute-start.18
  104.5 2.8 %collective-permute-start.19 = (f32[2,32,128]{2,1,0:T(8,128)S(1)}, f32[2,32,128]{2,1,0:T(8,128)S(1)}, u32[]{:S(2)}, u32[]{:S(2)}) collective-permute-start(f32[2,32,128]{2,1,0:T(8,128)S(1)} %get-tuple-element.54), channel_id=1, source_target_pairs={{0,96},{32,64},{64,32},{96,0},{1,97},{33,65},{65,33},{97,1},{2,98}... | collective-permute-start | bytes 98312 | tf_op jit(solution)/shard_map/ppermute | solution.py:313
  107.2 0.0 collective-permute-done.17.refs_1_
  107.2 1.6 %collective-permute-done.18.refs_2_ = f32[2,32,128]{2,1,0:T(8,128)S(1)} collective-permute-done((f32[2,32,128]{2,1,0:T(8,128)S(1)}, f32[2,32,128]{2,1,0:T(8,128)S(1)}, u32[]{:S(2)}, u32[]{:S(2)}) %collective-permute-start.18) | collective-permute-done | bytes 32800 | tf_op jit(solution)/shard_map/ppermute | solution.py:313
  108.8 0.9 collective-permute-done.19.refs_3_
  109.8 2.9 %collective-permute-start.20 = (f32[4,32,128]{2,1,0:T(8,128)S(1)}, f32[4,32,128]{2,1,0:T(8,128)S(1)}, u32[]{:S(2)}, u32[]{:S(2)}) collective-permute-start(f32[4,32,128]{2,1,0:T(8,128)S(1)} %pick_step.1), channel_id=1, source_target_pairs={{0,128},{128,0},{1,129},{129,1},{2,130},{130,2},{3,131},{131,3},{4... | collective-permute-start | bytes 196616 | tf_op jit(solution)/shard_map/ppermute | solution.py:314
  112.7 3.2 %collective-permute-done.20.across_ref = f32[4,32,128]{2,1,0:T(8,128)S(1)} collective-permute-done((f32[4,32,128]{2,1,0:T(8,128)S(1)}, f32[4,32,128]{2,1,0:T(8,128)S(1)}, u32[]{:S(2)}, u32[]{:S(2)}) %collective-permute-start.20) | collective-permute-done | bytes 65568 | tf_op jit(solution)/shard_map/ppermute | solution.py:314
  115.9 4.0 %all-to-all-done.2 = bf16[64,32,128]{2,1,0:T(8,128)(2,1)S(1)} async-done(((bf16[64,32,128]{2,1,0:T(8,128)(2,1)}), bf16[64,32,128]{2,1,0:T(8,128)(2,1)S(1)}, u32[]{:S(2)}, u32[]{:S(2)}) %all-to-all-start.2) | async-done | bytes 524320 | tf_op jit(solution)/shard_map/all_to_all | solution.py:282
  119.9 1.5 %lay_step.1 = f32[2,64,1,512]{3,2,1,0:T(1,128)} custom-call(s32[4]{0:T(128)S(1)} %copy-done.2, bf16[8,8,32,128]{3,2,1,0:T(8,128)(2,1)S(1)} %bitcast.12, f32[4,32,128]{2,1,0:T(8,128)S(1)} %collective-permute-done.20.across_ref, f32[2,32,128]{2,1,0:T(8,128)S(1)} %get-tuple-element.51.refs_0_, f32[2,32,128]{2,1,0:T(8,128)S(1)} %collective-permute-done.17.refs_1_, ...), custom_call_target="tpu_custom_call" | custom-call | flops 1000000 | bytes 1048576 | tf_op jit(solution)/shard_map/lay_step/pallas_call | solution.py:233
  (2 shorter events, 0.0 us)
Async XLA Ops:
  0.0 8.9 %collective-permute-start.2 = (bf16[1,2,64,512]{3,2,1,0:T(8,128)(2,1)}, bf16[1,2,64,512]{3,2,1,0:T(8,128)(2,1)S(1)}, u32[]{:S(2)}, u32[]{:S(2)}) collective-permute-start(bf16[1,2,64,512]{3,2,1,0:T(8,128)(2,1)} %bitcast.14), channel_id=1, source_target_pairs={{96,0},{131,1},{64,32},{163,33},{32,64},{195,65},{0,96},{227,97},{... | collective-permute-start | bytes 393224 | tf_op jit(solution)/shard_map/ppermute | solution.py:259
  2.0 7.0 %collective-permute-start.1 = (bf16[1,2,64,512]{3,2,1,0:T(8,128)(2,1)}, bf16[1,2,64,512]{3,2,1,0:T(8,128)(2,1)S(1)}, u32[]{:S(2)}, u32[]{:S(2)}) collective-permute-start(bf16[1,2,64,512]{3,2,1,0:T(8,128)(2,1)} %bitcast.15), channel_id=1, source_target_pairs={{64,0},{129,1},{96,32},{161,33},{0,64},{193,65},{32,96},{225,97},{... | collective-permute-start | bytes 393224 | tf_op jit(solution)/shard_map/ppermute | solution.py:259
  2.8 6.1 %collective-permute-start = (bf16[1,2,64,512]{3,2,1,0:T(8,128)(2,1)}, bf16[1,2,64,512]{3,2,1,0:T(8,128)(2,1)S(1)}, u32[]{:S(2)}, u32[]{:S(2)}) collective-permute-start(bf16[1,2,64,512]{3,2,1,0:T(8,128)(2,1)} %bitcast.16), channel_id=1, source_target_pairs={{32,0},{3,1},{0,32},{35,33},{96,64},{67,65},{64,96},{99,97},{34,2}... | collective-permute-start | bytes 393224 | tf_op jit(solution)/shard_map/ppermute | solution.py:259
  9.0 7.5 %copy-start = (bf16[2,4,16,512]{3,2,1,0:T(8,128)(2,1)S(1)}, bf16[2,4,16,512]{3,2,1,0:T(8,128)(2,1)}, u32[]{:S(2)}) copy-start(bf16[2,4,16,512]{3,2,1,0:T(8,128)(2,1)} %param.5) | copy-start | bytes 393220
  9.0 35.0 %all-to-all-start = ((bf16[32,128,256]{2,1,0:T(8,128)(2,1)}), bf16[32,128,256]{2,1,0:T(8,128)(2,1)S(1)}, u32[]{:S(2)}, u32[]{:S(2)}) async-start(bf16[32,128,256]{2,1,0:T(8,128)(2,1)} %bitcast.21), calls=%async_computation | async-start | bytes 4194304 | tf_op jit(solution)/shard_map/all_to_all | solution.py:282
  16.5 38.1 %collective-permute-start.5 = (bf16[4,2,64,512]{3,2,1,0:T(8,128)(2,1)S(1)}, bf16[4,2,64,512]{3,2,1,0:T(8,128)(2,1)S(1)}, u32[]{:S(2)}, u32[]{:S(2)}) collective-permute-start(bf16[4,2,64,512]{3,2,1,0:T(8,128)(2,1)S(1)} %pack.1.refs_0_), channel_id=1, source_target_pairs={{130,0},{97,1},{162,32},{65,33},{194,64},{33,65},{226,96},{1,97},{... | collective-permute-start | bytes 1572872 | tf_op jit(solution)/shard_map/ppermute | solution.py:259
  19.3 35.6 %collective-permute-start.4 = (bf16[4,2,64,512]{3,2,1,0:T(8,128)(2,1)S(1)}, bf16[4,2,64,512]{3,2,1,0:T(8,128)(2,1)}, u32[]{:S(2)}, u32[]{:S(2)}) collective-permute-start(bf16[4,2,64,512]{3,2,1,0:T(8,128)(2,1)S(1)} %pack.1.refs_0_), channel_id=1, source_target_pairs={{128,0},{65,1},{160,32},{97,33},{192,64},{1,65},{224,96},{33,97},{... | collective-permute-start | bytes 1572872 | tf_op jit(solution)/shard_map/ppermute | solution.py:259
  20.1 35.0 %collective-permute-start.3 = (bf16[4,2,64,512]{3,2,1,0:T(8,128)(2,1)S(1)}, bf16[4,2,64,512]{3,2,1,0:T(8,128)(2,1)}, u32[]{:S(2)}, u32[]{:S(2)}) collective-permute-start(bf16[4,2,64,512]{3,2,1,0:T(8,128)(2,1)S(1)} %pack.1.refs_0_), channel_id=1, source_target_pairs={{2,0},{33,1},{34,32},{1,33},{66,64},{97,65},{98,96},{65,97},{0,2},... | collective-permute-start | bytes 1572872 | tf_op jit(solution)/shard_map/ppermute | solution.py:259
  44.0 41.0 %all-to-all-start.1 = ((bf16[32,128,256]{2,1,0:T(8,128)(2,1)}), bf16[32,128,256]{2,1,0:T(8,128)(2,1)}, u32[]{:S(2)}, u32[]{:S(2)}) async-start(bf16[32,128,256]{2,1,0:T(8,128)(2,1)} %bitcast.20), calls=%async_computation.1 | async-start | bytes 4194304 | tf_op jit(solution)/shard_map/all_to_all | solution.py:282
  54.3 2.1 %collective-permute-start.6 = (bf16[4,2,64,512]{3,2,1,0:T(8,128)(2,1)S(1)}, bf16[4,2,64,512]{3,2,1,0:T(8,128)(2,1)}, u32[]{:S(2)}, u32[]{:S(2)}) collective-permute-start(bf16[4,2,64,512]{3,2,1,0:T(8,128)(2,1)S(1)} %pack.1.refs_0_), channel_id=1, source_target_pairs={{0,1},{1,0},{2,3},{3,2},{4,5},{5,4},{6,7},{7,6},{8,9},{9,8},{10,11... | collective-permute-start | bytes 1572872 | tf_op jit(solution)/shard_map/ppermute | solution.py:296
  54.6 3.4 %collective-permute-start.9 = (bf16[4,2,64,512]{3,2,1,0:T(8,128)(2,1)S(1)}, bf16[4,2,64,512]{3,2,1,0:T(8,128)(2,1)}, u32[]{:S(2)}, u32[]{:S(2)}) collective-permute-start(bf16[4,2,64,512]{3,2,1,0:T(8,128)(2,1)S(1)} %collective-permute-done.5.refs_3_), channel_id=1, source_target_pairs={{0,1},{1,0},{2,3},{3,2},{4,5},{5,4},{6,7},{7,6},{8,9},{9,8},{10,11... | collective-permute-start | bytes 1572872 | tf_op jit(solution)/shard_map/ppermute | solution.py:296
  55.0 3.2 %collective-permute-start.8 = (bf16[4,2,64,512]{3,2,1,0:T(8,128)(2,1)}, bf16[4,2,64,512]{3,2,1,0:T(8,128)(2,1)}, u32[]{:S(2)}, u32[]{:S(2)}) collective-permute-start(bf16[4,2,64,512]{3,2,1,0:T(8,128)(2,1)} %collective-permute-done.4.refs_2_), channel_id=1, source_target_pairs={{0,1},{1,0},{2,3},{3,2},{4,5},{5,4},{6,7},{7,6},{8,9},{9,8},{10,11... | collective-permute-start | bytes 1572872 | tf_op jit(solution)/shard_map/ppermute | solution.py:296
  55.1 3.8 %collective-permute-start.7 = (bf16[4,2,64,512]{3,2,1,0:T(8,128)(2,1)}, bf16[4,2,64,512]{3,2,1,0:T(8,128)(2,1)}, u32[]{:S(2)}, u32[]{:S(2)}) collective-permute-start(bf16[4,2,64,512]{3,2,1,0:T(8,128)(2,1)} %collective-permute-done.3.refs_1_), channel_id=1, source_target_pairs={{0,1},{1,0},{2,3},{3,2},{4,5},{5,4},{6,7},{7,6},{8,9},{9,8},{10,11... | collective-permute-start | bytes 1572872 | tf_op jit(solution)/shard_map/ppermute | solution.py:296
  55.5 6.6 %copy-start.1 = (s32[4]{0:T(128)}, s32[4]{0:T(128)S(1)}, u32[]{:S(2)}) copy-start(s32[4]{0:T(128)S(1)} %pad_add_fusion.me_ref) | copy-start | bytes 52
  62.1 4.7 %copy-start.3 = (bf16[2,512,2048]{2,1,0:T(8,128)(2,1)}, bf16[2,512,2048]{2,1,0:T(8,128)(2,1)S(1)}, u32[]{:S(2)}) copy-start(bf16[2,512,2048]{2,1,0:T(8,128)(2,1)S(1)} %turn_step.1.b_hbm) | copy-start | bytes 12582916
  66.9 11.7 %collective-permute-start.10 = (bf16[8,32,128]{2,1,0:T(8,128)(2,1)S(1)}, bf16[8,32,128]{2,1,0:T(8,128)(2,1)S(1)}, u32[]{:S(2)}, u32[]{:S(2)}) collective-permute-start(bf16[8,32,128]{2,1,0:T(8,128)(2,1)S(1)} %get-tuple-element.39), channel_id=1, source_target_pairs={{0,4},{4,0},{8,12},{12,8},{16,20},{20,16},{24,28},{28,24},{1,5},{5... | collective-permute-start | bytes 196616 | tf_op jit(solution)/shard_map/ppermute | solution.py:304
  68.9 14.3 %collective-permute-start.11 = (bf16[8,32,128]{2,1,0:T(8,128)(2,1)S(1)}, bf16[8,32,128]{2,1,0:T(8,128)(2,1)S(1)}, u32[]{:S(2)}, u32[]{:S(2)}) collective-permute-start(bf16[8,32,128]{2,1,0:T(8,128)(2,1)S(1)} %get-tuple-element.40), channel_id=1, source_target_pairs={{0,8},{4,12},{8,0},{12,4},{16,24},{20,28},{24,16},{28,20},{1,9},{5... | collective-permute-start | bytes 196616 | tf_op jit(solution)/shard_map/ppermute | solution.py:304
  72.2 12.9 %collective-permute-start.12 = (bf16[8,32,128]{2,1,0:T(8,128)(2,1)S(1)}, bf16[8,32,128]{2,1,0:T(8,128)(2,1)S(1)}, u32[]{:S(2)}, u32[]{:S(2)}) collective-permute-start(bf16[8,32,128]{2,1,0:T(8,128)(2,1)S(1)} %get-tuple-element.41), channel_id=1, source_target_pairs={{0,12},{4,8},{8,4},{12,0},{16,28},{20,24},{24,20},{28,16},{1,13},{... | collective-permute-start | bytes 196616 | tf_op jit(solution)/shard_map/ppermute | solution.py:304
  72.2 29.6 %collective-permute-start.13 = (bf16[8,32,128]{2,1,0:T(8,128)(2,1)S(1)}, bf16[8,32,128]{2,1,0:T(8,128)(2,1)S(1)}, u32[]{:S(2)}, u32[]{:S(2)}) collective-permute-start(bf16[8,32,128]{2,1,0:T(8,128)(2,1)S(1)} %get-tuple-element.47), channel_id=1, source_target_pairs={{0,16},{4,20},{8,24},{12,28},{16,0},{20,4},{24,8},{28,12},{1,17},{... | collective-permute-start | bytes 196616 | tf_op jit(solution)/shard_map/ppermute | solution.py:304
  78.5 23.2 %collective-permute-start.14 = (bf16[8,32,128]{2,1,0:T(8,128)(2,1)S(1)}, bf16[8,32,128]{2,1,0:T(8,128)(2,1)S(1)}, u32[]{:S(2)}, u32[]{:S(2)}) collective-permute-start(bf16[8,32,128]{2,1,0:T(8,128)(2,1)S(1)} %get-tuple-element.48), channel_id=1, source_target_pairs={{0,20},{4,16},{8,28},{12,24},{16,4},{20,0},{24,12},{28,8},{1,21},{... | collective-permute-start | bytes 196616 | tf_op jit(solution)/shard_map/ppermute | solution.py:304
  78.5 23.2 %collective-permute-start.15 = (bf16[8,32,128]{2,1,0:T(8,128)(2,1)S(1)}, bf16[8,32,128]{2,1,0:T(8,128)(2,1)S(1)}, u32[]{:S(2)}, u32[]{:S(2)}) collective-permute-start(bf16[8,32,128]{2,1,0:T(8,128)(2,1)S(1)} %get-tuple-element.49), channel_id=1, source_target_pairs={{0,24},{4,28},{8,16},{12,20},{16,8},{20,12},{24,0},{28,4},{1,25},{... | collective-permute-start | bytes 196616 | tf_op jit(solution)/shard_map/ppermute | solution.py:304
  83.1 18.6 %collective-permute-start.16 = (bf16[8,32,128]{2,1,0:T(8,128)(2,1)S(1)}, bf16[8,32,128]{2,1,0:T(8,128)(2,1)S(1)}, u32[]{:S(2)}, u32[]{:S(2)}) collective-permute-start(bf16[8,32,128]{2,1,0:T(8,128)(2,1)S(1)} %get-tuple-element.50), channel_id=1, source_target_pairs={{0,28},{4,24},{8,20},{12,16},{16,12},{20,8},{24,4},{28,0},{1,29},{... | collective-permute-start | bytes 196616 | tf_op jit(solution)/shard_map/ppermute | solution.py:304
  85.0 16.8 %copy-start.2 = (s32[4]{0:T(128)S(1)}, s32[4]{0:T(128)}, u32[]{:S(2)}) copy-start(s32[4]{0:T(128)} %copy-done.1) | copy-start | bytes 52
  91.8 28.1 %all-to-all-start.2 = ((bf16[64,32,128]{2,1,0:T(8,128)(2,1)}), bf16[64,32,128]{2,1,0:T(8,128)(2,1)S(1)}, u32[]{:S(2)}, u32[]{:S(2)}) async-start(bf16[64,32,128]{2,1,0:T(8,128)(2,1)} %bitcast.22), calls=%async_computation.2 | async-start | bytes 1048576 | tf_op jit(solution)/shard_map/all_to_all | solution.py:282
  102.5 4.8 %collective-permute-start.17 = (f32[2,32,128]{2,1,0:T(8,128)S(1)}, f32[2,32,128]{2,1,0:T(8,128)S(1)}, u32[]{:S(2)}, u32[]{:S(2)}) collective-permute-start(f32[2,32,128]{2,1,0:T(8,128)S(1)} %get-tuple-element.52), channel_id=1, source_target_pairs={{0,32},{32,0},{64,96},{96,64},{1,33},{33,1},{65,97},{97,65},{2,34}... | collective-permute-start | bytes 98312 | tf_op jit(solution)/shard_map/ppermute | solution.py:313
  103.4 5.4 %collective-permute-start.18 = (f32[2,32,128]{2,1,0:T(8,128)S(1)}, f32[2,32,128]{2,1,0:T(8,128)S(1)}, u32[]{:S(2)}, u32[]{:S(2)}) collective-permute-start(f32[2,32,128]{2,1,0:T(8,128)S(1)} %get-tuple-element.53), channel_id=1, source_target_pairs={{0,64},{32,96},{64,0},{96,32},{1,65},{33,97},{65,1},{97,33},{2,66}... | collective-permute-start | bytes 98312 | tf_op jit(solution)/shard_map/ppermute | solution.py:313
  104.5 5.3 %collective-permute-start.19 = (f32[2,32,128]{2,1,0:T(8,128)S(1)}, f32[2,32,128]{2,1,0:T(8,128)S(1)}, u32[]{:S(2)}, u32[]{:S(2)}) collective-permute-start(f32[2,32,128]{2,1,0:T(8,128)S(1)} %get-tuple-element.54), channel_id=1, source_target_pairs={{0,96},{32,64},{64,32},{96,0},{1,97},{33,65},{65,33},{97,1},{2,98}... | collective-permute-start | bytes 98312 | tf_op jit(solution)/shard_map/ppermute | solution.py:313
  109.8 6.1 %collective-permute-start.20 = (f32[4,32,128]{2,1,0:T(8,128)S(1)}, f32[4,32,128]{2,1,0:T(8,128)S(1)}, u32[]{:S(2)}, u32[]{:S(2)}) collective-permute-start(f32[4,32,128]{2,1,0:T(8,128)S(1)} %pick_step.1), channel_id=1, source_target_pairs={{0,128},{128,0},{1,129},{129,1},{2,130},{130,2},{3,131},{131,3},{4... | collective-permute-start | bytes 196616 | tf_op jit(solution)/shard_map/ppermute | solution.py:314

commit v7 on v6

--- a/solution.py
+++ b/solution.py
@@ -22,34 +22,37 @@
 
 
 def first_kernel(lh, stem_hbm, branch_hbm, out_hbm, stem, branch, lhs, out, in_sem, branch_sem, out_sem):
-    slices = stem.shape[1]
+    count = stem.shape[1] // 2
+    parts = [pl.ds(h * count, count) for h in range(2)]
     stem_copies, branch_copies, sends = [], [], []
-    for s in range(slices):
-        branch_copies.append(pltpu.make_async_copy(branch_hbm.at[:, s], branch.at[:, s], branch_sem.at[s]))
-        stem_copies.append(pltpu.make_async_copy(stem_hbm.at[:, s], stem.at[:, s], in_sem.at[s]))
-        branch_copies[s].start()
-        stem_copies[s].start()
+    for h, part in enumerate(parts):
+        branch_copies.append(pltpu.make_async_copy(branch_hbm.at[:, part], branch.at[:, part], branch_sem.at[h]))
+        stem_copies.append(pltpu.make_async_copy(stem_hbm.at[:, part], stem.at[:, part], in_sem.at[h]))
+        branch_copies[h].start()
+        stem_copies[h].start()
     row = lax.broadcasted_iota(jnp.int32, (128, 256), 0)
     col = lax.broadcasted_iota(jnp.int32, (128, 256), 1)
     regroup = (col == (row % 16) * 16 + row // 16 * 2 + lh).astype(jnp.bfloat16)
-    for s in range(slices):
-        branch_copies[s].wait()
-        br = [
-            lax.dot_general(regroup, branch[r, s], NT, preferred_element_type=jnp.float32).astype(jnp.bfloat16)
-            for r in range(2)
-        ]
-        lhs[s, 0:128, 0:256] = br[0]
-        lhs[s, 0:128, 256:512] = -br[1]
-        lhs[s, 128:256, 0:256] = br[1]
-        lhs[s, 128:256, 256:512] = br[0]
-        stem_copies[s].wait()
-        for w in range(4):
-            rhs = jnp.concatenate([stem[r, s, :, w].reshape(256, 256) for r in range(2)], axis=1)
-            res = lax.dot_general(lhs[s], rhs, NT, preferred_element_type=jnp.float32).astype(jnp.bfloat16)
-            for r in range(2):
-                out[:, w, r, s] = res[r * 128 : (r + 1) * 128].reshape(8, 16, 256)
-        sends.append(pltpu.make_async_copy(out.at[:, :, :, s], out_hbm.at[:, :, :, s], out_sem.at[s]))
-        sends[s].start()
+    for h, part in enumerate(parts):
+        branch_copies[h].wait()
+        for s in range(h * count, (h + 1) * count):
+            br = [
+                lax.dot_general(regroup, branch[r, s], NT, preferred_element_type=jnp.float32).astype(jnp.bfloat16)
+                for r in range(2)
+            ]
+            lhs[s, 0:128, 0:256] = br[0]
+            lhs[s, 0:128, 256:512] = -br[1]
+            lhs[s, 128:256, 0:256] = br[1]
+            lhs[s, 128:256, 256:512] = br[0]
+        stem_copies[h].wait()
+        for s in range(h * count, (h + 1) * count):
+            for w in range(4):
+                rhs = jnp.concatenate([stem[r, s, :, w].reshape(256, 256) for r in range(2)], axis=1)
+                res = lax.dot_general(lhs[s], rhs, NT, preferred_element_type=jnp.float32).astype(jnp.bfloat16)
+                for r in range(2):
+                    out[:, w, r, s] = res[r * 128 : (r + 1) * 128].reshape(8, 16, 256)
+        sends.append(pltpu.make_async_copy(out.at[:, :, :, part], out_hbm.at[:, :, :, part], out_sem.at[h]))
+        sends[h].start()
     for send in sends:
         send.wait()
 
@@ -67,9 +70,9 @@
             pltpu.VMEM(branch.shape, jnp.bfloat16),
             pltpu.VMEM((slices, 256, 512), jnp.bfloat16),
             pltpu.VMEM(shape, jnp.bfloat16),
-            pltpu.SemaphoreType.DMA((slices,)),
-            pltpu.SemaphoreType.DMA((slices,)),
-            pltpu.SemaphoreType.DMA((slices,)),
+            pltpu.SemaphoreType.DMA((2,)),
+            pltpu.SemaphoreType.DMA((2,)),
+            pltpu.SemaphoreType.DMA((2,)),
         ],
         compiler_params=pltpu.CompilerParams(vmem_limit_bytes=56 << 20),
         cost_estimate=pl.CostEstimate(flops=flops, bytes_accessed=7 << 20, transcendentals=0),
@@ -104,24 +107,28 @@
 
 
 def second_kernel(split, me_ref, x_hbm, b_hbm, *refs):
-    x, b, out, x_sem, b_sem, out_sem = refs[-6:]
-    out_hbm = refs[:-6]
-    x_copy = pltpu.make_async_copy(x_hbm, x, x_sem)
-    b_copies = [
-        pltpu.make_async_copy(b_hbm.at[:, pl.ds(h * 256, 256)], b.at[:, pl.ds(h * 256, 256)], b_sem.at[h])
-        for h in range(2)
-    ]
-    for copy in (x_copy, *b_copies):
-        copy.start()
+    if split:
+        x, b, (out, out_sem), out_hbm = x_hbm, b_hbm, refs[-2:], refs[:-2]
+    else:
+        x, b, x_sem, b_sem, out, out_sem = refs[-6:]
+        out_hbm = refs[:-6]
+        x_copy = pltpu.make_async_copy(x_hbm, x, x_sem)
+        b_copies = [
+            pltpu.make_async_copy(b_hbm.at[:, pl.ds(h * 256, 256)], b.at[:, pl.ds(h * 256, 256)], b_sem.at[h])
+            for h in range(2)
+        ]
+        for copy in (x_copy, *b_copies):
+            copy.start()
 
     def dot(left, right):
         return lax.dot_general(left, right, NN, preferred_element_type=jnp.float32)
 
-    x_copy.wait()
+    if not split:
+        x_copy.wait()
     xr, xi = (x[:, r].reshape(2048, 256) for r in range(2))
     sends = []
     for t in range(4):
-        if t % 2 == 0:
+        if t % 2 == 0 and not split:
             b_copies[t // 2].wait()
         rows = slice(t * 128, (t + 1) * 128)
         br, bi = b[0, rows], b[1, rows]
@@ -149,19 +156,18 @@
         out_shape = [jax.ShapeDtypeStruct(shape[1:], jnp.bfloat16)] * DEPTH
     else:
         out_shape = [jax.ShapeDtypeStruct(shape, jnp.bfloat16)]
+    held = [] if split else [
+        pltpu.VMEM((32, 2, 64, 256), jnp.bfloat16),
+        pltpu.VMEM((2, 512, 2048), jnp.bfloat16),
+        pltpu.SemaphoreType.DMA,
+        pltpu.SemaphoreType.DMA((2,)),
+    ]
     return pl.pallas_call(
         functools.partial(second_kernel, split),
-        in_specs=[SMEM, ANY, ANY],
+        in_specs=[SMEM] + [VMEM if split else ANY] * 2,
         out_specs=[ANY] * len(out_shape),
         out_shape=out_shape,
-        scratch_shapes=[
-            pltpu.VMEM((32, 2, 64, 256), jnp.bfloat16),
-            pltpu.VMEM((2, 512, 2048), jnp.bfloat16),
-            pltpu.VMEM(shape, jnp.bfloat16),
-            pltpu.SemaphoreType.DMA,
-            pltpu.SemaphoreType.DMA((2,)),
-            pltpu.SemaphoreType.DMA((DEPTH,)),
-        ],
+        scratch_shapes=held + [pltpu.VMEM(shape, jnp.bfloat16), pltpu.SemaphoreType.DMA((DEPTH,))],
         compiler_params=pltpu.CompilerParams(vmem_limit_bytes=(24 if split else 60) << 20),
         cost_estimate=pl.CostEstimate(flops=2150000000, bytes_accessed=7 << 20, transcendentals=0),
         name="second_step",
@@ -210,7 +216,7 @@
 
 
 def lay_kernel(me_ref, later_ref, across_ref, *refs):
-    out_ref, held = refs[-2:]
+    out_hbm, held, out, out_sem = refs[-4:]
     xh = me_ref[0] // 2
     for dy in range(RING):
         held[xh * RING + (me_ref[1] ^ dy)] = refs[dy][0]
@@ -221,21 +227,30 @@
         for z in range(1, DEPTH):
             acc = acc + later_ref[z, i].astype(jnp.float32)
         sums.append((held[i], acc))
+    sends = []
     for r in range(2):
         for jh in range(2):
             at = jh * 64 + r * 32
-            out_ref[r, jh * 32 : (jh + 1) * 32, 0] = jnp.concatenate(
+            out[r, jh * 32 : (jh + 1) * 32, 0] = jnp.concatenate(
                 [half[:, at : at + 32] for pair in sums for half in pair], axis=1
             )
+        sends.append(pltpu.make_async_copy(out.at[r], out_hbm.at[r], out_sem.at[r]))
+        sends[r].start()
+    for send in sends:
+        send.wait()
 
 
 def lay_step(me, later, across, sums):
     return pl.pallas_call(
         lay_kernel,
         in_specs=[SMEM] + [VMEM] * (2 + RING),
-        out_specs=VMEM,
+        out_specs=ANY,
         out_shape=jax.ShapeDtypeStruct((2, 64, 1, 512), jnp.float32),
-        scratch_shapes=[pltpu.VMEM((8, 32, 128), jnp.float32)],
+        scratch_shapes=[
+            pltpu.VMEM((8, 32, 128), jnp.float32),
+            pltpu.VMEM((2, 64, 1, 512), jnp.float32),
+            pltpu.SemaphoreType.DMA((2,)),
+        ],
         compiler_params=pltpu.CompilerParams(vmem_limit_bytes=16 << 20),
         cost_estimate=pl.CostEstimate(flops=1000000, bytes_accessed=1 << 20, transcendentals=0),
         name="lay_step",
@@ -297,7 +312,7 @@
     blocks = (RING, 2, slices * 16, 512)
     own, other = ([block.reshape(blocks) for block in part] for part in (own, other))
     turned = turn_step(me, own, other)
-    arrived, later = lax.optimization_barrier((arrived, later))
+    arrived, later, me = lax.optimization_barrier((arrived, later, me))
     later = exchange(later.reshape(32, 2 * slices * 16, 256), PLANE)
     half = list(second_step(me, arrived.reshape(32, 2, slices * 16, 256), turned, True))
     for d in range(1, DEPTH):

time: 122 us -> 122 us (level)
  Pallas kernels: 26.6 us -> 24.6 us
  transfers between devices with their start and end apart: 24 -> 24, of which waited for: 9 -> 9; matrix products, arithmetic and copies ran while one was open for 0% -> 0% of each run, Pallas kernels for 21% -> 19%
where the time goes in v7:
time: 122 us; the launch traced here: 121 us
  starting transfers between devices  64 us (52%)
  waiting for transfers between devices  32.2 us (26%)
  Pallas kernels  24.6 us (20%)
    all_to_all x3, starting transfers between devices, exchange(): return lax.all_to_all(block, axes, split_axis=0, concat_axis=0, tiled=True)  28.9 us
    all_to_all x3, waiting for transfers between devices, exchange(): return lax.all_to_all(block, axes, split_axis=0, concat_axis=0, tiled=True)  22.7 us
    ppermute x7, starting transfers between devices, shards(): half[d] = lax.ppermute(half[d], 'z', [(z, z ^ d) for z in range(DEPTH)])  18.2 us
    pallas_call x2, Pallas kernels, second_step(): pl.pallas_call(functools.partial(second_kernel, split), in_specs=[SMEM] +...  10.6 us
    pallas_call x2, Pallas kernels, first_step(): pl.pallas_call(functools.partial(first_kernel, lh), in_specs=[ANY] * 2, o...  9.3 us
    ppermute x6, starting transfers between devices, ring_blocks(): blocks.append(lax.ppermute(block, PLANE, pairs))  8.27 us
    ppermute x3, starting transfers between devices, shards(): sums[dy] = lax.ppermute(sums[dy], 'y', [(y, y ^ dy) for y in range(RING)])  4.79 us
    ppermute x4, waiting for transfers between devices, shards(): other = [lax.ppermute(block, 'core', [(0, 1), (1, 0)]) for block in own]  3.34 us
  transfers between devices with their start and end apart: 24, of which 9 were waited for; matrix products, arithmetic and copies ran while one was open for 0% of the time, Pallas kernels for 19%

profile of v7, /device:TPU:24, one launch (start us, length us, event | category | flops | bytes accessed | tf_op | source)
XLA Modules:
  0.0 121.4 jit_solution(4077583156490799178)
XLA Ops:
  0.0 2.0 %collective-permute-start.2 = (bf16[1,2,64,512]{3,2,1,0:T(8,128)(2,1)}, bf16[1,2,64,512]{3,2,1,0:T(8,128)(2,1)S(1)}, u32[]{:S(2)}, u32[]{:S(2)}) collective-permute-start(bf16[1,2,64,512]{3,2,1,0:T(8,128)(2,1)} %bitcast.14), channel_id=1, source_target_pairs={{96,0},{131,1},{64,32},{163,33},{32,64},{195,65},{0,96},{227,97},{... | collective-permute-start | bytes 393224 | tf_op jit(solution)/shard_map/ppermute | solution.py:274
  2.0 0.9 collective-permute-start.1
  2.8 1.3 %collective-permute-start = (bf16[1,2,64,512]{3,2,1,0:T(8,128)(2,1)}, bf16[1,2,64,512]{3,2,1,0:T(8,128)(2,1)S(1)}, u32[]{:S(2)}, u32[]{:S(2)}) collective-permute-start(bf16[1,2,64,512]{3,2,1,0:T(8,128)(2,1)} %bitcast.16), channel_id=1, source_target_pairs={{32,0},{3,1},{0,32},{35,33},{96,64},{67,65},{64,96},{99,97},{34,2}... | collective-permute-start | bytes 393224 | tf_op jit(solution)/shard_map/ppermute | solution.py:274
  4.1 4.6 %first_step.2 = bf16[8,4,2,4,16,256]{5,4,3,2,1,0:T(8,128)(2,1)} custom-call(bf16[2,4,8,4,32,256]{5,4,3,2,1,0:T(8,128)(2,1)} %bitcast.18, bf16[2,4,256,256]{3,2,1,0:T(8,128)(2,1)} %branch_hbm.3), custom_call_target="tpu_custom_call" | custom-call | flops 1200000000 | bytes 7340032 | tf_op jit(solution)/shard_map/first_step/pallas_call | solution.py:63
  8.7 0.0 collective-permute-done.2.refs_3_
  8.7 0.0 collective-permute-done.1.refs_2_
  8.7 0.0 collective-permute-done.refs_1_
  8.7 0.0 copy-start
  8.8 7.5 %all-to-all-start = ((bf16[32,128,256]{2,1,0:T(8,128)(2,1)}), bf16[32,128,256]{2,1,0:T(8,128)(2,1)S(1)}, u32[]{:S(2)}, u32[]{:S(2)}) async-start(bf16[32,128,256]{2,1,0:T(8,128)(2,1)} %bitcast.21), calls=%async_computation | async-start | bytes 4194304 | tf_op jit(solution)/shard_map/all_to_all | solution.py:297
  16.2 0.0 copy-done
  16.3 2.8 %collective-permute-start.5 = (bf16[4,2,64,512]{3,2,1,0:T(8,128)(2,1)S(1)}, bf16[4,2,64,512]{3,2,1,0:T(8,128)(2,1)S(1)}, u32[]{:S(2)}, u32[]{:S(2)}) collective-permute-start(bf16[4,2,64,512]{3,2,1,0:T(8,128)(2,1)S(1)} %pack.1.refs_0_), channel_id=1, source_target_pairs={{130,0},{97,1},{162,32},{65,33},{194,64},{33,65},{226,96},{1,97},{... | collective-permute-start | bytes 1572872 | tf_op jit(solution)/shard_map/ppermute | solution.py:274
  19.1 0.8 collective-permute-start.4
  19.9 0.6 collective-permute-start.3
  20.5 0.1 pad_add_fusion.me_ref
  20.5 0.0 copy-start.1
  20.5 4.7 %first_step.3 = bf16[8,4,2,4,16,256]{5,4,3,2,1,0:T(8,128)(2,1)} custom-call(bf16[2,4,8,4,32,256]{5,4,3,2,1,0:T(8,128)(2,1)} %bitcast.19, bf16[2,4,256,256]{3,2,1,0:T(8,128)(2,1)} %branch_hbm.3), custom_call_target="tpu_custom_call" | custom-call | flops 1000000 | bytes 7340032 | tf_op jit(solution)/shard_map/first_step/pallas_call | solution.py:63
  25.2 18.5 %all-to-all-done = bf16[32,128,256]{2,1,0:T(8,128)(2,1)S(1)} async-done(((bf16[32,128,256]{2,1,0:T(8,128)(2,1)}), bf16[32,128,256]{2,1,0:T(8,128)(2,1)S(1)}, u32[]{:S(2)}, u32[]{:S(2)}) %all-to-all-start) | async-done | bytes 2097184 | tf_op jit(solution)/shard_map/all_to_all | solution.py:297
  43.8 10.3 %all-to-all-start.1 = ((bf16[32,128,256]{2,1,0:T(8,128)(2,1)}), bf16[32,128,256]{2,1,0:T(8,128)(2,1)}, u32[]{:S(2)}, u32[]{:S(2)}) async-start(bf16[32,128,256]{2,1,0:T(8,128)(2,1)} %bitcast.20), calls=%async_computation.1 | async-start | bytes 4194304 | tf_op jit(solution)/shard_map/all_to_all | solution.py:297
  54.1 0.2 collective-permute-start.6
  54.4 0.0 collective-permute-done.5.refs_3_
  54.4 0.4 collective-permute-start.9
  54.7 0.0 collective-permute-done.4.refs_2_
  54.7 0.1 collective-permute-start.8
  54.9 0.0 collective-permute-done.3.refs_1_
  54.9 0.4 collective-permute-start.7
  55.2 0.9 collective-permute-done.6.refs_4_
  56.1 1.5 %collective-permute-done.9.refs_7_ = bf16[4,2,64,512]{3,2,1,0:T(8,128)(2,1)S(1)} collective-permute-done((bf16[4,2,64,512]{3,2,1,0:T(8,128)(2,1)S(1)}, bf16[4,2,64,512]{3,2,1,0:T(8,128)(2,1)S(1)}, u32[]{:S(2)}, u32[]{:S(2)}) %collective-permute-start.9) | collective-permute-done | bytes 524320 | tf_op jit(solution)/shard_map/ppermute | solution.py:311
  57.6 0.2 collective-permute-done.8.refs_6_
  57.8 0.8 collective-permute-done.7.refs_5_
  58.6 2.5 %turn_step.1.b_hbm = bf16[2,512,2048]{2,1,0:T(8,128)(2,1)S(1)} custom-call(s32[4]{0:T(128)S(1)} %pad_add_fusion.me_ref, bf16[4,2,64,512]{3,2,1,0:T(8,128)(2,1)S(1)} %pack.1.refs_0_, bf16[4,2,64,512]{3,2,1,0:T(8,128)(2,1)} %collective-permute-done.3.refs_1_, bf16[4,2,64,512]{3,2,1,0:T(8,128)(2,1)} %collective-permute-done.4.refs_2_, ...), custom_call_target="tpu_custom_call" | custom-call | flops 10000000000 | bytes 8388608 | tf_op jit(solution)/shard_map/turn_step/pallas_call | solution.py:98
  61.1 0.0 copy-start.3
  61.1 0.0 copy-done.1
  61.1 3.8 %second_step.2 = (bf16[8,32,128]{2,1,0:T(8,128)(2,1)S(1)}, bf16[8,32,128]{2,1,0:T(8,128)(2,1)S(1)}, bf16[8,32,128]{2,1,0:T(8,128)(2,1)S(1)}, bf16[8,32,128]{2,1,...) custom-call(s32[4]{0:T(128)S(1)} %pad_add_fusion.me_ref, ...), custom_call_target="tpu_custom_call" | custom-call | flops 2150000128 | bytes 7340032 | tf_op jit(solution)/shard_map/second_step/pallas_call | solution.py:165
  65.0 0.0 copy-done.3
  65.0 2.0 %collective-permute-start.10 = (bf16[8,32,128]{2,1,0:T(8,128)(2,1)S(1)}, bf16[8,32,128]{2,1,0:T(8,128)(2,1)S(1)}, u32[]{:S(2)}, u32[]{:S(2)}) collective-permute-start(bf16[8,32,128]{2,1,0:T(8,128)(2,1)S(1)} %get-tuple-element.41), channel_id=1, source_target_pairs={{0,4},{4,0},{8,12},{12,8},{16,20},{20,16},{24,28},{28,24},{1,5},{5... | collective-permute-start | bytes 196616 | tf_op jit(solution)/shard_map/ppermute | solution.py:319
  67.0 3.3 %collective-permute-start.11 = (bf16[8,32,128]{2,1,0:T(8,128)(2,1)S(1)}, bf16[8,32,128]{2,1,0:T(8,128)(2,1)S(1)}, u32[]{:S(2)}, u32[]{:S(2)}) collective-permute-start(bf16[8,32,128]{2,1,0:T(8,128)(2,1)S(1)} %get-tuple-element.42), channel_id=1, source_target_pairs={{0,8},{4,12},{8,0},{12,4},{16,24},{20,28},{24,16},{28,20},{1,9},{5... | collective-permute-start | bytes 196616 | tf_op jit(solution)/shard_map/ppermute | solution.py:319
  70.2 0.0 collective-permute-start.12
  70.2 6.4 %collective-permute-start.13 = (bf16[8,32,128]{2,1,0:T(8,128)(2,1)S(1)}, bf16[8,32,128]{2,1,0:T(8,128)(2,1)S(1)}, u32[]{:S(2)}, u32[]{:S(2)}) collective-permute-start(bf16[8,32,128]{2,1,0:T(8,128)(2,1)S(1)} %get-tuple-element.49), channel_id=1, source_target_pairs={{0,16},{4,20},{8,24},{12,28},{16,0},{20,4},{24,8},{28,12},{1,17},{... | collective-permute-start | bytes 196616 | tf_op jit(solution)/shard_map/ppermute | solution.py:319
  76.6 0.0 collective-permute-start.14
  76.7 0.0 collective-permute-done.10.refs_1_
  76.7 4.6 %collective-permute-start.15 = (bf16[8,32,128]{2,1,0:T(8,128)(2,1)S(1)}, bf16[8,32,128]{2,1,0:T(8,128)(2,1)S(1)}, u32[]{:S(2)}, u32[]{:S(2)}) collective-permute-start(bf16[8,32,128]{2,1,0:T(8,128)(2,1)S(1)} %get-tuple-element.51), channel_id=1, source_target_pairs={{0,24},{4,28},{8,16},{12,20},{16,8},{20,12},{24,0},{28,4},{1,25},{... | collective-permute-start | bytes 196616 | tf_op jit(solution)/shard_map/ppermute | solution.py:319
  81.2 0.0 collective-permute-done.11.refs_2_
  81.2 1.9 %collective-permute-start.16 = (bf16[8,32,128]{2,1,0:T(8,128)(2,1)S(1)}, bf16[8,32,128]{2,1,0:T(8,128)(2,1)S(1)}, u32[]{:S(2)}, u32[]{:S(2)}) collective-permute-start(bf16[8,32,128]{2,1,0:T(8,128)(2,1)S(1)} %get-tuple-element.52), channel_id=1, source_target_pairs={{0,28},{4,24},{8,20},{12,16},{16,12},{20,8},{24,4},{28,0},{1,29},{... | collective-permute-start | bytes 196616 | tf_op jit(solution)/shard_map/ppermute | solution.py:319
  83.2 0.0 collective-permute-done.12.refs_3_
  83.2 0.0 all-to-all-done.1
  83.2 0.0 copy-start.2
  83.2 6.8 %second_step.3 = bf16[8,8,32,128]{3,2,1,0:T(8,128)(2,1)} custom-call(s32[4]{0:T(128)} %copy-done.1, bf16[32,2,64,256]{3,2,1,0:T(8,128)(2,1)} %bitcast.9.x_hbm, bf16[2,512,2048]{2,1,0:T(8,128)(2,1)} %copy-done.3), custom_call_target="tpu_custom_call" | custom-call | flops 2150000128 | bytes 7340032 | tf_op jit(solution)/shard_map/second_step/pallas_call | solution.py:165
  90.0 11.1 %all-to-all-start.2 = ((bf16[64,32,128]{2,1,0:T(8,128)(2,1)}), bf16[64,32,128]{2,1,0:T(8,128)(2,1)S(1)}, u32[]{:S(2)}, u32[]{:S(2)}) async-start(bf16[64,32,128]{2,1,0:T(8,128)(2,1)} %bitcast.22), calls=%async_computation.2 | async-start | bytes 1048576 | tf_op jit(solution)/shard_map/all_to_all | solution.py:297
  101.0 0.0 collective-permute-done.13.refs_4_
  101.0 0.0 collective-permute-done.14.refs_5_
  101.1 0.0 collective-permute-done.15.refs_6_
  101.1 0.0 collective-permute-done.16.refs_7_
  101.1 0.0 copy-done.2
  101.1 0.6 total_step.1
  101.7 0.9 collective-permute-start.17
  102.7 1.1 collective-permute-start.18
  103.7 2.8 %collective-permute-start.19 = (f32[2,32,128]{2,1,0:T(8,128)S(1)}, f32[2,32,128]{2,1,0:T(8,128)S(1)}, u32[]{:S(2)}, u32[]{:S(2)}) collective-permute-start(f32[2,32,128]{2,1,0:T(8,128)S(1)} %get-tuple-element.56), channel_id=1, source_target_pairs={{0,96},{32,64},{64,32},{96,0},{1,97},{33,65},{65,33},{97,1},{2,98}... | collective-permute-start | bytes 98312 | tf_op jit(solution)/shard_map/ppermute | solution.py:328
  106.5 0.0 collective-permute-done.17.refs_1_
  106.5 2.0 %collective-permute-done.18.refs_2_ = f32[2,32,128]{2,1,0:T(8,128)S(1)} collective-permute-done((f32[2,32,128]{2,1,0:T(8,128)S(1)}, f32[2,32,128]{2,1,0:T(8,128)S(1)}, u32[]{:S(2)}, u32[]{:S(2)}) %collective-permute-start.18) | collective-permute-done | bytes 32800 | tf_op jit(solution)/shard_map/ppermute | solution.py:328
  108.5 0.8 collective-permute-done.19.refs_3_
  109.3 2.9 %collective-permute-start.20 = (f32[4,32,128]{2,1,0:T(8,128)S(1)}, f32[4,32,128]{2,1,0:T(8,128)S(1)}, u32[]{:S(2)}, u32[]{:S(2)}) collective-permute-start(f32[4,32,128]{2,1,0:T(8,128)S(1)} %pick_step.1), channel_id=1, source_target_pairs={{0,128},{128,0},{1,129},{129,1},{2,130},{130,2},{3,131},{131,3},{4... | collective-permute-start | bytes 196616 | tf_op jit(solution)/shard_map/ppermute | solution.py:329
  112.2 3.3 %collective-permute-done.20.across_ref = f32[4,32,128]{2,1,0:T(8,128)S(1)} collective-permute-done((f32[4,32,128]{2,1,0:T(8,128)S(1)}, f32[4,32,128]{2,1,0:T(8,128)S(1)}, u32[]{:S(2)}, u32[]{:S(2)}) %collective-permute-start.20) | collective-permute-done | bytes 65568 | tf_op jit(solution)/shard_map/ppermute | solution.py:329
  115.5 4.2 %all-to-all-done.2 = bf16[64,32,128]{2,1,0:T(8,128)(2,1)S(1)} async-done(((bf16[64,32,128]{2,1,0:T(8,128)(2,1)}), bf16[64,32,128]{2,1,0:T(8,128)(2,1)S(1)}, u32[]{:S(2)}, u32[]{:S(2)}) %all-to-all-start.2) | async-done | bytes 524320 | tf_op jit(solution)/shard_map/all_to_all | solution.py:297
  119.7 1.5 %lay_step.1 = f32[2,64,1,512]{3,2,1,0:T(1,128)} custom-call(s32[4]{0:T(128)S(1)} %copy-done.2, bf16[8,8,32,128]{3,2,1,0:T(8,128)(2,1)S(1)} %bitcast.12, f32[4,32,128]{2,1,0:T(8,128)S(1)} %collective-permute-done.20.across_ref, f32[2,32,128]{2,1,0:T(8,128)S(1)} %get-tuple-element.53.refs_0_, f32[2,32,128]{2,1,0:T(8,128)S(1)} %collective-permute-done.17.refs_1_, ...), custom_call_target="tpu_custom_call" | custom-call | flops 1000000 | bytes 1048576 | tf_op jit(solution)/shard_map/lay_step/pallas_call | solution.py:244
  (2 shorter events, 0.0 us)
Async XLA Ops:
  0.0 8.7 %collective-permute-start.2 = (bf16[1,2,64,512]{3,2,1,0:T(8,128)(2,1)}, bf16[1,2,64,512]{3,2,1,0:T(8,128)(2,1)S(1)}, u32[]{:S(2)}, u32[]{:S(2)}) collective-permute-start(bf16[1,2,64,512]{3,2,1,0:T(8,128)(2,1)} %bitcast.14), channel_id=1, source_target_pairs={{96,0},{131,1},{64,32},{163,33},{32,64},{195,65},{0,96},{227,97},{... | collective-permute-start | bytes 393224 | tf_op jit(solution)/shard_map/ppermute | solution.py:274
  2.0 6.8 %collective-permute-start.1 = (bf16[1,2,64,512]{3,2,1,0:T(8,128)(2,1)}, bf16[1,2,64,512]{3,2,1,0:T(8,128)(2,1)S(1)}, u32[]{:S(2)}, u32[]{:S(2)}) collective-permute-start(bf16[1,2,64,512]{3,2,1,0:T(8,128)(2,1)} %bitcast.15), channel_id=1, source_target_pairs={{64,0},{129,1},{96,32},{161,33},{0,64},{193,65},{32,96},{225,97},{... | collective-permute-start | bytes 393224 | tf_op jit(solution)/shard_map/ppermute | solution.py:274
  2.8 5.9 %collective-permute-start = (bf16[1,2,64,512]{3,2,1,0:T(8,128)(2,1)}, bf16[1,2,64,512]{3,2,1,0:T(8,128)(2,1)S(1)}, u32[]{:S(2)}, u32[]{:S(2)}) collective-permute-start(bf16[1,2,64,512]{3,2,1,0:T(8,128)(2,1)} %bitcast.16), channel_id=1, source_target_pairs={{32,0},{3,1},{0,32},{35,33},{96,64},{67,65},{64,96},{99,97},{34,2}... | collective-permute-start | bytes 393224 | tf_op jit(solution)/shard_map/ppermute | solution.py:274
  8.7 7.5 %copy-start = (bf16[2,4,16,512]{3,2,1,0:T(8,128)(2,1)S(1)}, bf16[2,4,16,512]{3,2,1,0:T(8,128)(2,1)}, u32[]{:S(2)}) copy-start(bf16[2,4,16,512]{3,2,1,0:T(8,128)(2,1)} %param.5) | copy-start | bytes 393220
  8.8 35.0 %all-to-all-start = ((bf16[32,128,256]{2,1,0:T(8,128)(2,1)}), bf16[32,128,256]{2,1,0:T(8,128)(2,1)S(1)}, u32[]{:S(2)}, u32[]{:S(2)}) async-start(bf16[32,128,256]{2,1,0:T(8,128)(2,1)} %bitcast.21), calls=%async_computation | async-start | bytes 4194304 | tf_op jit(solution)/shard_map/all_to_all | solution.py:297
  16.3 38.1 %collective-permute-start.5 = (bf16[4,2,64,512]{3,2,1,0:T(8,128)(2,1)S(1)}, bf16[4,2,64,512]{3,2,1,0:T(8,128)(2,1)S(1)}, u32[]{:S(2)}, u32[]{:S(2)}) collective-permute-start(bf16[4,2,64,512]{3,2,1,0:T(8,128)(2,1)S(1)} %pack.1.refs_0_), channel_id=1, source_target_pairs={{130,0},{97,1},{162,32},{65,33},{194,64},{33,65},{226,96},{1,97},{... | collective-permute-start | bytes 1572872 | tf_op jit(solution)/shard_map/ppermute | solution.py:274
  19.1 35.6 %collective-permute-start.4 = (bf16[4,2,64,512]{3,2,1,0:T(8,128)(2,1)S(1)}, bf16[4,2,64,512]{3,2,1,0:T(8,128)(2,1)}, u32[]{:S(2)}, u32[]{:S(2)}) collective-permute-start(bf16[4,2,64,512]{3,2,1,0:T(8,128)(2,1)S(1)} %pack.1.refs_0_), channel_id=1, source_target_pairs={{128,0},{65,1},{160,32},{97,33},{192,64},{1,65},{224,96},{33,97},{... | collective-permute-start | bytes 1572872 | tf_op jit(solution)/shard_map/ppermute | solution.py:274
  19.9 35.0 %collective-permute-start.3 = (bf16[4,2,64,512]{3,2,1,0:T(8,128)(2,1)S(1)}, bf16[4,2,64,512]{3,2,1,0:T(8,128)(2,1)}, u32[]{:S(2)}, u32[]{:S(2)}) collective-permute-start(bf16[4,2,64,512]{3,2,1,0:T(8,128)(2,1)S(1)} %pack.1.refs_0_), channel_id=1, source_target_pairs={{2,0},{33,1},{34,32},{1,33},{66,64},{97,65},{98,96},{65,97},{0,2},... | collective-permute-start | bytes 1572872 | tf_op jit(solution)/shard_map/ppermute | solution.py:274
  20.5 40.6 %copy-start.1 = (s32[4]{0:T(128)}, s32[4]{0:T(128)S(1)}, u32[]{:S(2)}) copy-start(s32[4]{0:T(128)S(1)} %pad_add_fusion.me_ref) | copy-start | bytes 52
  43.8 39.4 %all-to-all-start.1 = ((bf16[32,128,256]{2,1,0:T(8,128)(2,1)}), bf16[32,128,256]{2,1,0:T(8,128)(2,1)}, u32[]{:S(2)}, u32[]{:S(2)}) async-start(bf16[32,128,256]{2,1,0:T(8,128)(2,1)} %bitcast.20), calls=%async_computation.1 | async-start | bytes 4194304 | tf_op jit(solution)/shard_map/all_to_all | solution.py:297
  54.1 2.0 %collective-permute-start.6 = (bf16[4,2,64,512]{3,2,1,0:T(8,128)(2,1)S(1)}, bf16[4,2,64,512]{3,2,1,0:T(8,128)(2,1)S(1)}, u32[]{:S(2)}, u32[]{:S(2)}) collective-permute-start(bf16[4,2,64,512]{3,2,1,0:T(8,128)(2,1)S(1)} %pack.1.refs_0_), channel_id=1, source_target_pairs={{0,1},{1,0},{2,3},{3,2},{4,5},{5,4},{6,7},{7,6},{8,9},{9,8},{10,11... | collective-permute-start | bytes 1572872 | tf_op jit(solution)/shard_map/ppermute | solution.py:311
  54.4 3.3 %collective-permute-start.9 = (bf16[4,2,64,512]{3,2,1,0:T(8,128)(2,1)S(1)}, bf16[4,2,64,512]{3,2,1,0:T(8,128)(2,1)S(1)}, u32[]{:S(2)}, u32[]{:S(2)}) collective-permute-start(bf16[4,2,64,512]{3,2,1,0:T(8,128)(2,1)S(1)} %collective-permute-done.5.refs_3_), channel_id=1, source_target_pairs={{0,1},{1,0},{2,3},{3,2},{4,5},{5,4},{6,7},{7,6},{8,9},{9,8},{10,11... | collective-permute-start | bytes 1572872 | tf_op jit(solution)/shard_map/ppermute | solution.py:311
  54.7 3.1 %collective-permute-start.8 = (bf16[4,2,64,512]{3,2,1,0:T(8,128)(2,1)}, bf16[4,2,64,512]{3,2,1,0:T(8,128)(2,1)S(1)}, u32[]{:S(2)}, u32[]{:S(2)}) collective-permute-start(bf16[4,2,64,512]{3,2,1,0:T(8,128)(2,1)} %collective-permute-done.4.refs_2_), channel_id=1, source_target_pairs={{0,1},{1,0},{2,3},{3,2},{4,5},{5,4},{6,7},{7,6},{8,9},{9,8},{10,11... | collective-permute-start | bytes 1572872 | tf_op jit(solution)/shard_map/ppermute | solution.py:311
  54.9 3.7 %collective-permute-start.7 = (bf16[4,2,64,512]{3,2,1,0:T(8,128)(2,1)}, bf16[4,2,64,512]{3,2,1,0:T(8,128)(2,1)S(1)}, u32[]{:S(2)}, u32[]{:S(2)}) collective-permute-start(bf16[4,2,64,512]{3,2,1,0:T(8,128)(2,1)} %collective-permute-done.3.refs_1_), channel_id=1, source_target_pairs={{0,1},{1,0},{2,3},{3,2},{4,5},{5,4},{6,7},{7,6},{8,9},{9,8},{10,11... | collective-permute-start | bytes 1572872 | tf_op jit(solution)/shard_map/ppermute | solution.py:311
  61.1 3.8 %copy-start.3 = (bf16[2,512,2048]{2,1,0:T(8,128)(2,1)}, bf16[2,512,2048]{2,1,0:T(8,128)(2,1)S(1)}, u32[]{:S(2)}) copy-start(bf16[2,512,2048]{2,1,0:T(8,128)(2,1)S(1)} %turn_step.1.b_hbm) | copy-start | bytes 12582916
  65.0 11.7 %collective-permute-start.10 = (bf16[8,32,128]{2,1,0:T(8,128)(2,1)S(1)}, bf16[8,32,128]{2,1,0:T(8,128)(2,1)S(1)}, u32[]{:S(2)}, u32[]{:S(2)}) collective-permute-start(bf16[8,32,128]{2,1,0:T(8,128)(2,1)S(1)} %get-tuple-element.41), channel_id=1, source_target_pairs={{0,4},{4,0},{8,12},{12,8},{16,20},{20,16},{24,28},{28,24},{1,5},{5... | collective-permute-start | bytes 196616 | tf_op jit(solution)/shard_map/ppermute | solution.py:319
  67.0 14.3 %collective-permute-start.11 = (bf16[8,32,128]{2,1,0:T(8,128)(2,1)S(1)}, bf16[8,32,128]{2,1,0:T(8,128)(2,1)S(1)}, u32[]{:S(2)}, u32[]{:S(2)}) collective-permute-start(bf16[8,32,128]{2,1,0:T(8,128)(2,1)S(1)} %get-tuple-element.42), channel_id=1, source_target_pairs={{0,8},{4,12},{8,0},{12,4},{16,24},{20,28},{24,16},{28,20},{1,9},{5... | collective-permute-start | bytes 196616 | tf_op jit(solution)/shard_map/ppermute | solution.py:319
  70.2 12.9 %collective-permute-start.12 = (bf16[8,32,128]{2,1,0:T(8,128)(2,1)S(1)}, bf16[8,32,128]{2,1,0:T(8,128)(2,1)S(1)}, u32[]{:S(2)}, u32[]{:S(2)}) collective-permute-start(bf16[8,32,128]{2,1,0:T(8,128)(2,1)S(1)} %get-tuple-element.43), channel_id=1, source_target_pairs={{0,12},{4,8},{8,4},{12,0},{16,28},{20,24},{24,20},{28,16},{1,13},{... | collective-permute-start | bytes 196616 | tf_op jit(solution)/shard_map/ppermute | solution.py:319
  70.2 30.8 %collective-permute-start.13 = (bf16[8,32,128]{2,1,0:T(8,128)(2,1)S(1)}, bf16[8,32,128]{2,1,0:T(8,128)(2,1)S(1)}, u32[]{:S(2)}, u32[]{:S(2)}) collective-permute-start(bf16[8,32,128]{2,1,0:T(8,128)(2,1)S(1)} %get-tuple-element.49), channel_id=1, source_target_pairs={{0,16},{4,20},{8,24},{12,28},{16,0},{20,4},{24,8},{28,12},{1,17},{... | collective-permute-start | bytes 196616 | tf_op jit(solution)/shard_map/ppermute | solution.py:319
  76.6 24.4 %collective-permute-start.14 = (bf16[8,32,128]{2,1,0:T(8,128)(2,1)S(1)}, bf16[8,32,128]{2,1,0:T(8,128)(2,1)S(1)}, u32[]{:S(2)}, u32[]{:S(2)}) collective-permute-start(bf16[8,32,128]{2,1,0:T(8,128)(2,1)S(1)} %get-tuple-element.50), channel_id=1, source_target_pairs={{0,20},{4,16},{8,28},{12,24},{16,4},{20,0},{24,12},{28,8},{1,21},{... | collective-permute-start | bytes 196616 | tf_op jit(solution)/shard_map/ppermute | solution.py:319
  76.7 24.4 %collective-permute-start.15 = (bf16[8,32,128]{2,1,0:T(8,128)(2,1)S(1)}, bf16[8,32,128]{2,1,0:T(8,128)(2,1)S(1)}, u32[]{:S(2)}, u32[]{:S(2)}) collective-permute-start(bf16[8,32,128]{2,1,0:T(8,128)(2,1)S(1)} %get-tuple-element.51), channel_id=1, source_target_pairs={{0,24},{4,28},{8,16},{12,20},{16,8},{20,12},{24,0},{28,4},{1,25},{... | collective-permute-start | bytes 196616 | tf_op jit(solution)/shard_map/ppermute | solution.py:319
  81.2 19.8 %collective-permute-start.16 = (bf16[8,32,128]{2,1,0:T(8,128)(2,1)S(1)}, bf16[8,32,128]{2,1,0:T(8,128)(2,1)S(1)}, u32[]{:S(2)}, u32[]{:S(2)}) collective-permute-start(bf16[8,32,128]{2,1,0:T(8,128)(2,1)S(1)} %get-tuple-element.52), channel_id=1, source_target_pairs={{0,28},{4,24},{8,20},{12,16},{16,12},{20,8},{24,4},{28,0},{1,29},{... | collective-permute-start | bytes 196616 | tf_op jit(solution)/shard_map/ppermute | solution.py:319
  83.2 17.9 %copy-start.2 = (s32[4]{0:T(128)S(1)}, s32[4]{0:T(128)}, u32[]{:S(2)}) copy-start(s32[4]{0:T(128)} %copy-done.1) | copy-start | bytes 52
  90.0 29.7 %all-to-all-start.2 = ((bf16[64,32,128]{2,1,0:T(8,128)(2,1)}), bf16[64,32,128]{2,1,0:T(8,128)(2,1)S(1)}, u32[]{:S(2)}, u32[]{:S(2)}) async-start(bf16[64,32,128]{2,1,0:T(8,128)(2,1)} %bitcast.22), calls=%async_computation.2 | async-start | bytes 1048576 | tf_op jit(solution)/shard_map/all_to_all | solution.py:297
  101.7 4.8 %collective-permute-start.17 = (f32[2,32,128]{2,1,0:T(8,128)S(1)}, f32[2,32,128]{2,1,0:T(8,128)S(1)}, u32[]{:S(2)}, u32[]{:S(2)}) collective-permute-start(f32[2,32,128]{2,1,0:T(8,128)S(1)} %get-tuple-element.54), channel_id=1, source_target_pairs={{0,32},{32,0},{64,96},{96,64},{1,33},{33,1},{65,97},{97,65},{2,34}... | collective-permute-start | bytes 98312 | tf_op jit(solution)/shard_map/ppermute | solution.py:328
  102.7 5.8 %collective-permute-start.18 = (f32[2,32,128]{2,1,0:T(8,128)S(1)}, f32[2,32,128]{2,1,0:T(8,128)S(1)}, u32[]{:S(2)}, u32[]{:S(2)}) collective-permute-start(f32[2,32,128]{2,1,0:T(8,128)S(1)} %get-tuple-element.55), channel_id=1, source_target_pairs={{0,64},{32,96},{64,0},{96,32},{1,65},{33,97},{65,1},{97,33},{2,66}... | collective-permute-start | bytes 98312 | tf_op jit(solution)/shard_map/ppermute | solution.py:328
  103.7 5.6 %collective-permute-start.19 = (f32[2,32,128]{2,1,0:T(8,128)S(1)}, f32[2,32,128]{2,1,0:T(8,128)S(1)}, u32[]{:S(2)}, u32[]{:S(2)}) collective-permute-start(f32[2,32,128]{2,1,0:T(8,128)S(1)} %get-tuple-element.56), channel_id=1, source_target_pairs={{0,96},{32,64},{64,32},{96,0},{1,97},{33,65},{65,33},{97,1},{2,98}... | collective-permute-start | bytes 98312 | tf_op jit(solution)/shard_map/ppermute | solution.py:328
  109.3 6.2 %collective-permute-start.20 = (f32[4,32,128]{2,1,0:T(8,128)S(1)}, f32[4,32,128]{2,1,0:T(8,128)S(1)}, u32[]{:S(2)}, u32[]{:S(2)}) collective-permute-start(f32[4,32,128]{2,1,0:T(8,128)S(1)} %pick_step.1), channel_id=1, source_target_pairs={{0,128},{128,0},{1,129},{129,1},{2,130},{130,2},{3,131},{131,3},{4... | collective-permute-start | bytes 196616 | tf_op jit(solution)/shard_map/ppermute | solution.py:329

commit v8 on v6

--- a/solution.py
+++ b/solution.py
@@ -130,10 +130,11 @@
         for q in range(2):
             parts = [res[r][q * 64 + jh * 32 : q * 64 + (jh + 1) * 32] for jh in range(2) for r in range(2)]
             for za in range(DEPTH):
-                out[za, t * 2 + q] = jnp.concatenate([part[:, za * 32 : (za + 1) * 32] for part in parts], axis=1)
+                at = (za, t * 2 + q) if split else (t * 2 + q, za)
+                out[at] = jnp.concatenate([part[:, za * 32 : (za + 1) * 32] for part in parts], axis=1)
         if t % 2 == 1 and not split:
             part = pl.ds(t * 2 - 2, 4)
-            sends.append(pltpu.make_async_copy(out.at[:, part], out_hbm[0].at[:, part], out_sem.at[t // 2]))
+            sends.append(pltpu.make_async_copy(out.at[part], out_hbm[0].at[part], out_sem.at[t // 2]))
             sends[-1].start()
     if split:
         for d in range(DEPTH):
@@ -217,9 +218,9 @@
         held[(1 - xh) * RING + (me_ref[1] ^ dy)] = across_ref[dy]
     sums = []
     for i in range(8):
-        acc = later_ref[0, i].astype(jnp.float32)
+        acc = later_ref[i, 0].astype(jnp.float32)
         for z in range(1, DEPTH):
-            acc = acc + later_ref[z, i].astype(jnp.float32)
+            acc = acc + later_ref[i, z].astype(jnp.float32)
         sums.append((held[i], acc))
     for r in range(2):
         for jh in range(2):
@@ -307,7 +308,7 @@
     for d, block in zip(early, done):
         half[d] = block
     (rest,) = second_step(me, later.reshape(32, 2, slices * 16, 256), turned, False)
-    rest = exchange(rest.reshape(64, 32, 128), ("z",) + CUTS)
+    rest = exchange(rest.reshape(64, 32, 128), CUTS + ("z",))
     sums = list(total_step(me, half))
     for dy in range(1, RING):
         sums[dy] = lax.ppermute(sums[dy], "y", [(y, y ^ dy) for y in range(RING)])

time: 122 us -> 123 us (level)
  transfers between devices with their start and end apart: 24 -> 24, of which waited for: 9 -> 9; matrix products, arithmetic and copies ran while one was open for 0% -> 0% of each run, Pallas kernels for 21% -> 20%
where the time goes in v8:
time: 123 us; the launch traced here: 122 us
  starting transfers between devices  63.2 us (51%)
  waiting for transfers between devices  32.4 us (26%)
  Pallas kernels  26.6 us (22%)
    all_to_all x3, starting transfers between devices, exchange(): return lax.all_to_all(block, axes, split_axis=0, concat_axis=0, tiled=True)  27.8 us
    all_to_all x3, waiting for transfers between devices, exchange(): return lax.all_to_all(block, axes, split_axis=0, concat_axis=0, tiled=True)  22.7 us
    ppermute x7, starting transfers between devices, shards(): half[d] = lax.ppermute(half[d], 'z', [(z, z ^ d) for z in range(DEPTH)])  18.1 us
    pallas_call x2, Pallas kernels, second_step(): pl.pallas_call(functools.partial(second_kernel, split), in_specs=[SMEM, A...  11.5 us
    pallas_call x2, Pallas kernels, first_step(): pl.pallas_call(functools.partial(first_kernel, lh), in_specs=[ANY] * 2, o...  9.71 us
    ppermute x6, starting transfers between devices, ring_blocks(): blocks.append(lax.ppermute(block, PLANE, pairs))  8.27 us
    ppermute x3, starting transfers between devices, shards(): sums[dy] = lax.ppermute(sums[dy], 'y', [(y, y ^ dy) for y in range(RING)])  4.79 us
    ppermute x1, waiting for transfers between devices, shards(): across = lax.ppermute(pick_step(sums), 'xh', [(0, 1), (1, 0)])  3.69 us
  transfers between devices with their start and end apart: 24, of which 9 were waited for; matrix products, arithmetic and copies ran while one was open for 0% of the time, Pallas kernels for 20%

profile of v8, /device:TPU:24, one launch (start us, length us, event | category | flops | bytes accessed | tf_op | source)
XLA Modules:
  0.0 122.5 jit_solution(2651172035744746925)
XLA Ops:
  0.0 2.0 %collective-permute-start.2 = (bf16[1,2,64,512]{3,2,1,0:T(8,128)(2,1)}, bf16[1,2,64,512]{3,2,1,0:T(8,128)(2,1)S(1)}, u32[]{:S(2)}, u32[]{:S(2)}) collective-permute-start(bf16[1,2,64,512]{3,2,1,0:T(8,128)(2,1)} %bitcast.14), channel_id=1, source_target_pairs={{96,0},{131,1},{64,32},{163,33},{32,64},{195,65},{0,96},{227,97},{... | collective-permute-start | bytes 393224 | tf_op jit(solution)/shard_map/ppermute | solution.py:260
  2.0 0.9 collective-permute-start.1
  2.8 1.3 %collective-permute-start = (bf16[1,2,64,512]{3,2,1,0:T(8,128)(2,1)}, bf16[1,2,64,512]{3,2,1,0:T(8,128)(2,1)S(1)}, u32[]{:S(2)}, u32[]{:S(2)}) collective-permute-start(bf16[1,2,64,512]{3,2,1,0:T(8,128)(2,1)} %bitcast.16), channel_id=1, source_target_pairs={{32,0},{3,1},{0,32},{35,33},{96,64},{67,65},{64,96},{99,97},{34,2}... | collective-permute-start | bytes 393224 | tf_op jit(solution)/shard_map/ppermute | solution.py:260
  4.1 4.8 %first_step.2 = bf16[8,4,2,4,16,256]{5,4,3,2,1,0:T(8,128)(2,1)} custom-call(bf16[2,4,8,4,32,256]{5,4,3,2,1,0:T(8,128)(2,1)} %bitcast.18, bf16[2,4,256,256]{3,2,1,0:T(8,128)(2,1)} %branch_hbm.3), custom_call_target="tpu_custom_call" | custom-call | flops 1200000000 | bytes 7340032 | tf_op jit(solution)/shard_map/first_step/pallas_call | solution.py:60
  8.9 0.0 collective-permute-done.2.refs_3_
  8.9 0.0 collective-permute-done.1.refs_2_
  9.0 0.0 collective-permute-done.refs_1_
  9.0 0.0 copy-start
  9.0 7.5 %all-to-all-start = ((bf16[32,128,256]{2,1,0:T(8,128)(2,1)}), bf16[32,128,256]{2,1,0:T(8,128)(2,1)S(1)}, u32[]{:S(2)}, u32[]{:S(2)}) async-start(bf16[32,128,256]{2,1,0:T(8,128)(2,1)} %bitcast.21), calls=%async_computation | async-start | bytes 4194304 | tf_op jit(solution)/shard_map/all_to_all | solution.py:283
  16.4 0.0 copy-done
  16.5 2.8 %collective-permute-start.5 = (bf16[4,2,64,512]{3,2,1,0:T(8,128)(2,1)S(1)}, bf16[4,2,64,512]{3,2,1,0:T(8,128)(2,1)S(1)}, u32[]{:S(2)}, u32[]{:S(2)}) collective-permute-start(bf16[4,2,64,512]{3,2,1,0:T(8,128)(2,1)S(1)} %pack.1.refs_0_), channel_id=1, source_target_pairs={{130,0},{97,1},{162,32},{65,33},{194,64},{33,65},{226,96},{1,97},{... | collective-permute-start | bytes 1572872 | tf_op jit(solution)/shard_map/ppermute | solution.py:260
  19.3 0.8 collective-permute-start.4
  20.1 0.6 collective-permute-start.3
  20.7 4.9 %first_step.3 = bf16[8,4,2,4,16,256]{5,4,3,2,1,0:T(8,128)(2,1)} custom-call(bf16[2,4,8,4,32,256]{5,4,3,2,1,0:T(8,128)(2,1)} %bitcast.19, bf16[2,4,256,256]{3,2,1,0:T(8,128)(2,1)} %branch_hbm.3), custom_call_target="tpu_custom_call" | custom-call | flops 1000000 | bytes 7340032 | tf_op jit(solution)/shard_map/first_step/pallas_call | solution.py:60
  25.6 18.4 %all-to-all-done = bf16[32,128,256]{2,1,0:T(8,128)(2,1)S(1)} async-done(((bf16[32,128,256]{2,1,0:T(8,128)(2,1)}), bf16[32,128,256]{2,1,0:T(8,128)(2,1)S(1)}, u32[]{:S(2)}, u32[]{:S(2)}) %all-to-all-start) | async-done | bytes 2097184 | tf_op jit(solution)/shard_map/all_to_all | solution.py:283
  44.0 10.3 %all-to-all-start.1 = ((bf16[32,128,256]{2,1,0:T(8,128)(2,1)}), bf16[32,128,256]{2,1,0:T(8,128)(2,1)}, u32[]{:S(2)}, u32[]{:S(2)}) async-start(bf16[32,128,256]{2,1,0:T(8,128)(2,1)} %bitcast.20), calls=%async_computation.1 | async-start | bytes 4194304 | tf_op jit(solution)/shard_map/all_to_all | solution.py:283
  54.3 0.2 collective-permute-start.6
  54.6 0.0 collective-permute-done.5.refs_3_
  54.6 0.4 collective-permute-start.9
  54.9 0.0 collective-permute-done.4.refs_2_
  55.0 0.1 collective-permute-start.8
  55.1 0.0 collective-permute-done.3.refs_1_
  55.1 0.4 collective-permute-start.7
  55.5 0.1 pad_add_fusion.me_ref
  55.5 0.0 copy-start.1
  55.5 0.9 collective-permute-done.6.refs_4_
  56.5 1.5 %collective-permute-done.9.refs_7_ = bf16[4,2,64,512]{3,2,1,0:T(8,128)(2,1)} collective-permute-done((bf16[4,2,64,512]{3,2,1,0:T(8,128)(2,1)S(1)}, bf16[4,2,64,512]{3,2,1,0:T(8,128)(2,1)}, u32[]{:S(2)}, u32[]{:S(2)}) %collective-permute-start.9) | collective-permute-done | bytes 524320 | tf_op jit(solution)/shard_map/ppermute | solution.py:297
  58.0 0.2 collective-permute-done.8.refs_6_
  58.2 0.8 collective-permute-done.7.refs_5_
  58.9 3.2 %turn_step.1.b_hbm = bf16[2,512,2048]{2,1,0:T(8,128)(2,1)S(1)} custom-call(s32[4]{0:T(128)S(1)} %pad_add_fusion.me_ref, bf16[4,2,64,512]{3,2,1,0:T(8,128)(2,1)S(1)} %pack.1.refs_0_, bf16[4,2,64,512]{3,2,1,0:T(8,128)(2,1)} %collective-permute-done.3.refs_1_, bf16[4,2,64,512]{3,2,1,0:T(8,128)(2,1)} %collective-permute-done.4.refs_2_, ...), custom_call_target="tpu_custom_call" | custom-call | flops 10000000000 | bytes 8388608 | tf_op jit(solution)/shard_map/turn_step/pallas_call | solution.py:95
  62.1 0.0 copy-start.3
  62.1 0.0 copy-done.1
  62.1 4.7 %second_step.2 = (bf16[8,32,128]{2,1,0:T(8,128)(2,1)S(1)}, bf16[8,32,128]{2,1,0:T(8,128)(2,1)S(1)}, bf16[8,32,128]{2,1,0:T(8,128)(2,1)S(1)}, bf16[8,32,128]{2,1,...) custom-call(s32[4]{0:T(128)S(1)} %pad_add_fusion.me_ref, ...), custom_call_target="tpu_custom_call" | custom-call | flops 2150000128 | bytes 7340032 | tf_op jit(solution)/shard_map/second_step/pallas_call | solution.py:153
  66.9 0.0 copy-done.3
  66.9 2.0 %collective-permute-start.10 = (bf16[8,32,128]{2,1,0:T(8,128)(2,1)S(1)}, bf16[8,32,128]{2,1,0:T(8,128)(2,1)S(1)}, u32[]{:S(2)}, u32[]{:S(2)}) collective-permute-start(bf16[8,32,128]{2,1,0:T(8,128)(2,1)S(1)} %get-tuple-element.39), channel_id=1, source_target_pairs={{0,4},{4,0},{8,12},{12,8},{16,20},{20,16},{24,28},{28,24},{1,5},{5... | collective-permute-start | bytes 196616 | tf_op jit(solution)/shard_map/ppermute | solution.py:305
  68.9 3.3 %collective-permute-start.11 = (bf16[8,32,128]{2,1,0:T(8,128)(2,1)S(1)}, bf16[8,32,128]{2,1,0:T(8,128)(2,1)S(1)}, u32[]{:S(2)}, u32[]{:S(2)}) collective-permute-start(bf16[8,32,128]{2,1,0:T(8,128)(2,1)S(1)} %get-tuple-element.40), channel_id=1, source_target_pairs={{0,8},{4,12},{8,0},{12,4},{16,24},{20,28},{24,16},{28,20},{1,9},{5... | collective-permute-start | bytes 196616 | tf_op jit(solution)/shard_map/ppermute | solution.py:305
  72.2 0.0 collective-permute-start.12
  72.2 6.4 %collective-permute-start.13 = (bf16[8,32,128]{2,1,0:T(8,128)(2,1)S(1)}, bf16[8,32,128]{2,1,0:T(8,128)(2,1)S(1)}, u32[]{:S(2)}, u32[]{:S(2)}) collective-permute-start(bf16[8,32,128]{2,1,0:T(8,128)(2,1)S(1)} %get-tuple-element.47), channel_id=1, source_target_pairs={{0,16},{4,20},{8,24},{12,28},{16,0},{20,4},{24,8},{28,12},{1,17},{... | collective-permute-start | bytes 196616 | tf_op jit(solution)/shard_map/ppermute | solution.py:305
  78.5 0.0 collective-permute-start.14
  78.5 0.0 collective-permute-done.10.refs_1_
  78.5 4.6 %collective-permute-start.15 = (bf16[8,32,128]{2,1,0:T(8,128)(2,1)S(1)}, bf16[8,32,128]{2,1,0:T(8,128)(2,1)S(1)}, u32[]{:S(2)}, u32[]{:S(2)}) collective-permute-start(bf16[8,32,128]{2,1,0:T(8,128)(2,1)S(1)} %get-tuple-element.49), channel_id=1, source_target_pairs={{0,24},{4,28},{8,16},{12,20},{16,8},{20,12},{24,0},{28,4},{1,25},{... | collective-permute-start | bytes 196616 | tf_op jit(solution)/shard_map/ppermute | solution.py:305
  83.1 0.0 collective-permute-done.11.refs_2_
  83.1 1.9 %collective-permute-start.16 = (bf16[8,32,128]{2,1,0:T(8,128)(2,1)S(1)}, bf16[8,32,128]{2,1,0:T(8,128)(2,1)S(1)}, u32[]{:S(2)}, u32[]{:S(2)}) collective-permute-start(bf16[8,32,128]{2,1,0:T(8,128)(2,1)S(1)} %get-tuple-element.50), channel_id=1, source_target_pairs={{0,28},{4,24},{8,20},{12,16},{16,12},{20,8},{24,4},{28,0},{1,29},{... | collective-permute-start | bytes 196616 | tf_op jit(solution)/shard_map/ppermute | solution.py:305
  85.0 0.0 collective-permute-done.12.refs_3_
  85.0 0.0 all-to-all-done.1
  85.0 0.0 copy-start.2
  85.0 6.8 %second_step.3 = bf16[8,8,32,128]{3,2,1,0:T(8,128)(2,1)} custom-call(s32[4]{0:T(128)} %copy-done.1, bf16[32,2,64,256]{3,2,1,0:T(8,128)(2,1)} %bitcast.9.x_hbm, bf16[2,512,2048]{2,1,0:T(8,128)(2,1)} %copy-done.3), custom_call_target="tpu_custom_call" | custom-call | flops 2150000128 | bytes 7340032 | tf_op jit(solution)/shard_map/second_step/pallas_call | solution.py:153
  91.8 10.0 %all-to-all-start.2 = ((bf16[64,32,128]{2,1,0:T(8,128)(2,1)}), bf16[64,32,128]{2,1,0:T(8,128)(2,1)S(1)}, u32[]{:S(2)}, u32[]{:S(2)}) async-start(bf16[64,32,128]{2,1,0:T(8,128)(2,1)} %bitcast.22), calls=%async_computation.2 | async-start | bytes 1048576 | tf_op jit(solution)/shard_map/all_to_all | solution.py:283
  101.8 0.0 collective-permute-done.13.refs_4_
  101.8 0.0 collective-permute-done.14.refs_5_
  101.8 0.0 collective-permute-done.15.refs_6_
  101.8 0.0 collective-permute-done.16.refs_7_
  101.8 0.0 copy-done.2
  101.8 0.6 total_step.1
  102.5 0.9 collective-permute-start.17
  103.4 1.1 collective-permute-start.18
  104.4 2.8 %collective-permute-start.19 = (f32[2,32,128]{2,1,0:T(8,128)S(1)}, f32[2,32,128]{2,1,0:T(8,128)S(1)}, u32[]{:S(2)}, u32[]{:S(2)}) collective-permute-start(f32[2,32,128]{2,1,0:T(8,128)S(1)} %get-tuple-element.54), channel_id=1, source_target_pairs={{0,96},{32,64},{64,32},{96,0},{1,97},{33,65},{65,33},{97,1},{2,98}... | collective-permute-start | bytes 98312 | tf_op jit(solution)/shard_map/ppermute | solution.py:314
  107.3 0.0 collective-permute-done.17.refs_1_
  107.3 1.9 %collective-permute-done.18.refs_2_ = f32[2,32,128]{2,1,0:T(8,128)S(1)} collective-permute-done((f32[2,32,128]{2,1,0:T(8,128)S(1)}, f32[2,32,128]{2,1,0:T(8,128)S(1)}, u32[]{:S(2)}, u32[]{:S(2)}) %collective-permute-start.18) | collective-permute-done | bytes 32800 | tf_op jit(solution)/shard_map/ppermute | solution.py:314
  109.2 0.6 collective-permute-done.19.refs_3_
  109.8 3.1 %collective-permute-start.20 = (f32[4,32,128]{2,1,0:T(8,128)S(1)}, f32[4,32,128]{2,1,0:T(8,128)S(1)}, u32[]{:S(2)}, u32[]{:S(2)}) collective-permute-start(f32[4,32,128]{2,1,0:T(8,128)S(1)} %pick_step.1), channel_id=1, source_target_pairs={{0,128},{128,0},{1,129},{129,1},{2,130},{130,2},{3,131},{131,3},{4... | collective-permute-start | bytes 196616 | tf_op jit(solution)/shard_map/ppermute | solution.py:315
  112.9 3.7 %collective-permute-done.20.across_ref = f32[4,32,128]{2,1,0:T(8,128)S(1)} collective-permute-done((f32[4,32,128]{2,1,0:T(8,128)S(1)}, f32[4,32,128]{2,1,0:T(8,128)S(1)}, u32[]{:S(2)}, u32[]{:S(2)}) %collective-permute-start.20) | collective-permute-done | bytes 65568 | tf_op jit(solution)/shard_map/ppermute | solution.py:315
  116.6 4.3 %all-to-all-done.2 = bf16[64,32,128]{2,1,0:T(8,128)(2,1)S(1)} async-done(((bf16[64,32,128]{2,1,0:T(8,128)(2,1)}), bf16[64,32,128]{2,1,0:T(8,128)(2,1)S(1)}, u32[]{:S(2)}, u32[]{:S(2)}) %all-to-all-start.2) | async-done | bytes 524320 | tf_op jit(solution)/shard_map/all_to_all | solution.py:283
  120.9 1.5 %lay_step.1 = f32[2,64,1,512]{3,2,1,0:T(1,128)} custom-call(s32[4]{0:T(128)S(1)} %copy-done.2, bf16[8,8,32,128]{3,2,1,0:T(8,128)(2,1)S(1)} %bitcast.12, f32[4,32,128]{2,1,0:T(8,128)S(1)} %collective-permute-done.20.across_ref, f32[2,32,128]{2,1,0:T(8,128)S(1)} %get-tuple-element.51.refs_0_, f32[2,32,128]{2,1,0:T(8,128)S(1)} %collective-permute-done.17.refs_1_, ...), custom_call_target="tpu_custom_call" | custom-call | flops 1000000 | bytes 1048576 | tf_op jit(solution)/shard_map/lay_step/pallas_call | solution.py:234
  (2 shorter events, 0.0 us)
Async XLA Ops:
  0.0 8.9 %collective-permute-start.2 = (bf16[1,2,64,512]{3,2,1,0:T(8,128)(2,1)}, bf16[1,2,64,512]{3,2,1,0:T(8,128)(2,1)S(1)}, u32[]{:S(2)}, u32[]{:S(2)}) collective-permute-start(bf16[1,2,64,512]{3,2,1,0:T(8,128)(2,1)} %bitcast.14), channel_id=1, source_target_pairs={{96,0},{131,1},{64,32},{163,33},{32,64},{195,65},{0,96},{227,97},{... | collective-permute-start | bytes 393224 | tf_op jit(solution)/shard_map/ppermute | solution.py:260
  2.0 7.0 %collective-permute-start.1 = (bf16[1,2,64,512]{3,2,1,0:T(8,128)(2,1)}, bf16[1,2,64,512]{3,2,1,0:T(8,128)(2,1)S(1)}, u32[]{:S(2)}, u32[]{:S(2)}) collective-permute-start(bf16[1,2,64,512]{3,2,1,0:T(8,128)(2,1)} %bitcast.15), channel_id=1, source_target_pairs={{64,0},{129,1},{96,32},{161,33},{0,64},{193,65},{32,96},{225,97},{... | collective-permute-start | bytes 393224 | tf_op jit(solution)/shard_map/ppermute | solution.py:260
  2.8 6.1 %collective-permute-start = (bf16[1,2,64,512]{3,2,1,0:T(8,128)(2,1)}, bf16[1,2,64,512]{3,2,1,0:T(8,128)(2,1)S(1)}, u32[]{:S(2)}, u32[]{:S(2)}) collective-permute-start(bf16[1,2,64,512]{3,2,1,0:T(8,128)(2,1)} %bitcast.16), channel_id=1, source_target_pairs={{32,0},{3,1},{0,32},{35,33},{96,64},{67,65},{64,96},{99,97},{34,2}... | collective-permute-start | bytes 393224 | tf_op jit(solution)/shard_map/ppermute | solution.py:260
  9.0 7.5 %copy-start = (bf16[2,4,16,512]{3,2,1,0:T(8,128)(2,1)S(1)}, bf16[2,4,16,512]{3,2,1,0:T(8,128)(2,1)}, u32[]{:S(2)}) copy-start(bf16[2,4,16,512]{3,2,1,0:T(8,128)(2,1)} %param.5) | copy-start | bytes 393220
  9.0 35.0 %all-to-all-start = ((bf16[32,128,256]{2,1,0:T(8,128)(2,1)}), bf16[32,128,256]{2,1,0:T(8,128)(2,1)S(1)}, u32[]{:S(2)}, u32[]{:S(2)}) async-start(bf16[32,128,256]{2,1,0:T(8,128)(2,1)} %bitcast.21), calls=%async_computation | async-start | bytes 4194304 | tf_op jit(solution)/shard_map/all_to_all | solution.py:283
  16.5 38.1 %collective-permute-start.5 = (bf16[4,2,64,512]{3,2,1,0:T(8,128)(2,1)S(1)}, bf16[4,2,64,512]{3,2,1,0:T(8,128)(2,1)S(1)}, u32[]{:S(2)}, u32[]{:S(2)}) collective-permute-start(bf16[4,2,64,512]{3,2,1,0:T(8,128)(2,1)S(1)} %pack.1.refs_0_), channel_id=1, source_target_pairs={{130,0},{97,1},{162,32},{65,33},{194,64},{33,65},{226,96},{1,97},{... | collective-permute-start | bytes 1572872 | tf_op jit(solution)/shard_map/ppermute | solution.py:260
  19.3 35.6 %collective-permute-start.4 = (bf16[4,2,64,512]{3,2,1,0:T(8,128)(2,1)S(1)}, bf16[4,2,64,512]{3,2,1,0:T(8,128)(2,1)}, u32[]{:S(2)}, u32[]{:S(2)}) collective-permute-start(bf16[4,2,64,512]{3,2,1,0:T(8,128)(2,1)S(1)} %pack.1.refs_0_), channel_id=1, source_target_pairs={{128,0},{65,1},{160,32},{97,33},{192,64},{1,65},{224,96},{33,97},{... | collective-permute-start | bytes 1572872 | tf_op jit(solution)/shard_map/ppermute | solution.py:260
  20.1 35.0 %collective-permute-start.3 = (bf16[4,2,64,512]{3,2,1,0:T(8,128)(2,1)S(1)}, bf16[4,2,64,512]{3,2,1,0:T(8,128)(2,1)}, u32[]{:S(2)}, u32[]{:S(2)}) collective-permute-start(bf16[4,2,64,512]{3,2,1,0:T(8,128)(2,1)S(1)} %pack.1.refs_0_), channel_id=1, source_target_pairs={{2,0},{33,1},{34,32},{1,33},{66,64},{97,65},{98,96},{65,97},{0,2},... | collective-permute-start | bytes 1572872 | tf_op jit(solution)/shard_map/ppermute | solution.py:260
  44.0 41.0 %all-to-all-start.1 = ((bf16[32,128,256]{2,1,0:T(8,128)(2,1)}), bf16[32,128,256]{2,1,0:T(8,128)(2,1)}, u32[]{:S(2)}, u32[]{:S(2)}) async-start(bf16[32,128,256]{2,1,0:T(8,128)(2,1)} %bitcast.20), calls=%async_computation.1 | async-start | bytes 4194304 | tf_op jit(solution)/shard_map/all_to_all | solution.py:283
  54.3 2.1 %collective-permute-start.6 = (bf16[4,2,64,512]{3,2,1,0:T(8,128)(2,1)S(1)}, bf16[4,2,64,512]{3,2,1,0:T(8,128)(2,1)}, u32[]{:S(2)}, u32[]{:S(2)}) collective-permute-start(bf16[4,2,64,512]{3,2,1,0:T(8,128)(2,1)S(1)} %pack.1.refs_0_), channel_id=1, source_target_pairs={{0,1},{1,0},{2,3},{3,2},{4,5},{5,4},{6,7},{7,6},{8,9},{9,8},{10,11... | collective-permute-start | bytes 1572872 | tf_op jit(solution)/shard_map/ppermute | solution.py:297
  54.6 3.4 %collective-permute-start.9 = (bf16[4,2,64,512]{3,2,1,0:T(8,128)(2,1)S(1)}, bf16[4,2,64,512]{3,2,1,0:T(8,128)(2,1)}, u32[]{:S(2)}, u32[]{:S(2)}) collective-permute-start(bf16[4,2,64,512]{3,2,1,0:T(8,128)(2,1)S(1)} %collective-permute-done.5.refs_3_), channel_id=1, source_target_pairs={{0,1},{1,0},{2,3},{3,2},{4,5},{5,4},{6,7},{7,6},{8,9},{9,8},{10,11... | collective-permute-start | bytes 1572872 | tf_op jit(solution)/shard_map/ppermute | solution.py:297
  55.0 3.2 %collective-permute-start.8 = (bf16[4,2,64,512]{3,2,1,0:T(8,128)(2,1)}, bf16[4,2,64,512]{3,2,1,0:T(8,128)(2,1)}, u32[]{:S(2)}, u32[]{:S(2)}) collective-permute-start(bf16[4,2,64,512]{3,2,1,0:T(8,128)(2,1)} %collective-permute-done.4.refs_2_), channel_id=1, source_target_pairs={{0,1},{1,0},{2,3},{3,2},{4,5},{5,4},{6,7},{7,6},{8,9},{9,8},{10,11... | collective-permute-start | bytes 1572872 | tf_op jit(solution)/shard_map/ppermute | solution.py:297
  55.1 3.8 %collective-permute-start.7 = (bf16[4,2,64,512]{3,2,1,0:T(8,128)(2,1)}, bf16[4,2,64,512]{3,2,1,0:T(8,128)(2,1)}, u32[]{:S(2)}, u32[]{:S(2)}) collective-permute-start(bf16[4,2,64,512]{3,2,1,0:T(8,128)(2,1)} %collective-permute-done.3.refs_1_), channel_id=1, source_target_pairs={{0,1},{1,0},{2,3},{3,2},{4,5},{5,4},{6,7},{7,6},{8,9},{9,8},{10,11... | collective-permute-start | bytes 1572872 | tf_op jit(solution)/shard_map/ppermute | solution.py:297
  55.5 6.6 %copy-start.1 = (s32[4]{0:T(128)}, s32[4]{0:T(128)S(1)}, u32[]{:S(2)}) copy-start(s32[4]{0:T(128)S(1)} %pad_add_fusion.me_ref) | copy-start | bytes 52
  62.1 4.7 %copy-start.3 = (bf16[2,512,2048]{2,1,0:T(8,128)(2,1)}, bf16[2,512,2048]{2,1,0:T(8,128)(2,1)S(1)}, u32[]{:S(2)}) copy-start(bf16[2,512,2048]{2,1,0:T(8,128)(2,1)S(1)} %turn_step.1.b_hbm) | copy-start | bytes 12582916
  66.9 11.7 %collective-permute-start.10 = (bf16[8,32,128]{2,1,0:T(8,128)(2,1)S(1)}, bf16[8,32,128]{2,1,0:T(8,128)(2,1)S(1)}, u32[]{:S(2)}, u32[]{:S(2)}) collective-permute-start(bf16[8,32,128]{2,1,0:T(8,128)(2,1)S(1)} %get-tuple-element.39), channel_id=1, source_target_pairs={{0,4},{4,0},{8,12},{12,8},{16,20},{20,16},{24,28},{28,24},{1,5},{5... | collective-permute-start | bytes 196616 | tf_op jit(solution)/shard_map/ppermute | solution.py:305
  68.9 14.3 %collective-permute-start.11 = (bf16[8,32,128]{2,1,0:T(8,128)(2,1)S(1)}, bf16[8,32,128]{2,1,0:T(8,128)(2,1)S(1)}, u32[]{:S(2)}, u32[]{:S(2)}) collective-permute-start(bf16[8,32,128]{2,1,0:T(8,128)(2,1)S(1)} %get-tuple-element.40), channel_id=1, source_target_pairs={{0,8},{4,12},{8,0},{12,4},{16,24},{20,28},{24,16},{28,20},{1,9},{5... | collective-permute-start | bytes 196616 | tf_op jit(solution)/shard_map/ppermute | solution.py:305
  72.2 12.9 %collective-permute-start.12 = (bf16[8,32,128]{2,1,0:T(8,128)(2,1)S(1)}, bf16[8,32,128]{2,1,0:T(8,128)(2,1)S(1)}, u32[]{:S(2)}, u32[]{:S(2)}) collective-permute-start(bf16[8,32,128]{2,1,0:T(8,128)(2,1)S(1)} %get-tuple-element.41), channel_id=1, source_target_pairs={{0,12},{4,8},{8,4},{12,0},{16,28},{20,24},{24,20},{28,16},{1,13},{... | collective-permute-start | bytes 196616 | tf_op jit(solution)/shard_map/ppermute | solution.py:305
  72.2 29.6 %collective-permute-start.13 = (bf16[8,32,128]{2,1,0:T(8,128)(2,1)S(1)}, bf16[8,32,128]{2,1,0:T(8,128)(2,1)S(1)}, u32[]{:S(2)}, u32[]{:S(2)}) collective-permute-start(bf16[8,32,128]{2,1,0:T(8,128)(2,1)S(1)} %get-tuple-element.47), channel_id=1, source_target_pairs={{0,16},{4,20},{8,24},{12,28},{16,0},{20,4},{24,8},{28,12},{1,17},{... | collective-permute-start | bytes 196616 | tf_op jit(solution)/shard_map/ppermute | solution.py:305
  78.5 23.3 %collective-permute-start.14 = (bf16[8,32,128]{2,1,0:T(8,128)(2,1)S(1)}, bf16[8,32,128]{2,1,0:T(8,128)(2,1)S(1)}, u32[]{:S(2)}, u32[]{:S(2)}) collective-permute-start(bf16[8,32,128]{2,1,0:T(8,128)(2,1)S(1)} %get-tuple-element.48), channel_id=1, source_target_pairs={{0,20},{4,16},{8,28},{12,24},{16,4},{20,0},{24,12},{28,8},{1,21},{... | collective-permute-start | bytes 196616 | tf_op jit(solution)/shard_map/ppermute | solution.py:305
  78.5 23.3 %collective-permute-start.15 = (bf16[8,32,128]{2,1,0:T(8,128)(2,1)S(1)}, bf16[8,32,128]{2,1,0:T(8,128)(2,1)S(1)}, u32[]{:S(2)}, u32[]{:S(2)}) collective-permute-start(bf16[8,32,128]{2,1,0:T(8,128)(2,1)S(1)} %get-tuple-element.49), channel_id=1, source_target_pairs={{0,24},{4,28},{8,16},{12,20},{16,8},{20,12},{24,0},{28,4},{1,25},{... | collective-permute-start | bytes 196616 | tf_op jit(solution)/shard_map/ppermute | solution.py:305
  83.1 18.7 %collective-permute-start.16 = (bf16[8,32,128]{2,1,0:T(8,128)(2,1)S(1)}, bf16[8,32,128]{2,1,0:T(8,128)(2,1)S(1)}, u32[]{:S(2)}, u32[]{:S(2)}) collective-permute-start(bf16[8,32,128]{2,1,0:T(8,128)(2,1)S(1)} %get-tuple-element.50), channel_id=1, source_target_pairs={{0,28},{4,24},{8,20},{12,16},{16,12},{20,8},{24,4},{28,0},{1,29},{... | collective-permute-start | bytes 196616 | tf_op jit(solution)/shard_map/ppermute | solution.py:305
  85.0 16.8 %copy-start.2 = (s32[4]{0:T(128)S(1)}, s32[4]{0:T(128)}, u32[]{:S(2)}) copy-start(s32[4]{0:T(128)} %copy-done.1) | copy-start | bytes 52
  91.8 29.1 %all-to-all-start.2 = ((bf16[64,32,128]{2,1,0:T(8,128)(2,1)}), bf16[64,32,128]{2,1,0:T(8,128)(2,1)S(1)}, u32[]{:S(2)}, u32[]{:S(2)}) async-start(bf16[64,32,128]{2,1,0:T(8,128)(2,1)} %bitcast.22), calls=%async_computation.2 | async-start | bytes 1048576 | tf_op jit(solution)/shard_map/all_to_all | solution.py:283
  102.5 4.8 %collective-permute-start.17 = (f32[2,32,128]{2,1,0:T(8,128)S(1)}, f32[2,32,128]{2,1,0:T(8,128)S(1)}, u32[]{:S(2)}, u32[]{:S(2)}) collective-permute-start(f32[2,32,128]{2,1,0:T(8,128)S(1)} %get-tuple-element.52), channel_id=1, source_target_pairs={{0,32},{32,0},{64,96},{96,64},{1,33},{33,1},{65,97},{97,65},{2,34}... | collective-permute-start | bytes 98312 | tf_op jit(solution)/shard_map/ppermute | solution.py:314
  103.4 5.8 %collective-permute-start.18 = (f32[2,32,128]{2,1,0:T(8,128)S(1)}, f32[2,32,128]{2,1,0:T(8,128)S(1)}, u32[]{:S(2)}, u32[]{:S(2)}) collective-permute-start(f32[2,32,128]{2,1,0:T(8,128)S(1)} %get-tuple-element.53), channel_id=1, source_target_pairs={{0,64},{32,96},{64,0},{96,32},{1,65},{33,97},{65,1},{97,33},{2,66}... | collective-permute-start | bytes 98312 | tf_op jit(solution)/shard_map/ppermute | solution.py:314
  104.4 5.4 %collective-permute-start.19 = (f32[2,32,128]{2,1,0:T(8,128)S(1)}, f32[2,32,128]{2,1,0:T(8,128)S(1)}, u32[]{:S(2)}, u32[]{:S(2)}) collective-permute-start(f32[2,32,128]{2,1,0:T(8,128)S(1)} %get-tuple-element.54), channel_id=1, source_target_pairs={{0,96},{32,64},{64,32},{96,0},{1,97},{33,65},{65,33},{97,1},{2,98}... | collective-permute-start | bytes 98312 | tf_op jit(solution)/shard_map/ppermute | solution.py:314
  109.8 6.8 %collective-permute-start.20 = (f32[4,32,128]{2,1,0:T(8,128)S(1)}, f32[4,32,128]{2,1,0:T(8,128)S(1)}, u32[]{:S(2)}, u32[]{:S(2)}) collective-permute-start(f32[4,32,128]{2,1,0:T(8,128)S(1)} %pick_step.1), channel_id=1, source_target_pairs={{0,128},{128,0},{1,129},{129,1},{2,130},{130,2},{3,131},{131,3},{4... | collective-permute-start | bytes 196616 | tf_op jit(solution)/shard_map/ppermute | solution.py:315
